TPU v7x, 32 devices: a whole 2x2x4 slice. The times are simulated.
32 devices in a mesh: groups: 2 (over y), row: 16 (over z, x, core).
Axes of the slice: x: 2, y: 2, z: 4, core: 2. Of those that a mesh axis runs over, the one named last changes fastest.
Arguments:
- object_tiles: bfloat16 [8192, 2, 2048], P(('groups', 'row')), parts along dimension 0, may hold values from -4 to 4
- probe: float32 [4, 256, 2, 256], replicated, may hold values from -3 to 3
- measured: bfloat16 [192, 256, 256], P(('groups', 'row')), parts along dimension 0, may hold values from 0.19921875 to 2.5
- offset_row: int32 [192], P(('groups', 'row')), parts along dimension 0, may hold values from 0 to 255
- offset_col: int32 [192], P(('groups', 'row')), parts along dimension 0, may hold values from 0 to 1791
- subpixel: int32 [192], P(('groups', 'row')), parts along dimension 0, may hold values from 0 to 15
- live_count: int32 [32], P(('groups', 'row')), parts along dimension 0, may hold values from 1 to 6, 48 in all
Outputs:
- object_grad: float32 [8192, 2, 2048], P(('groups', 'row')), parts along dimension 0
- probe_grad: float32 [8, 256, 2, 256], P('groups'), parts along dimension 0
- position_grad: float32 [2, 192], P(None, ('groups', 'row')), parts along dimension 1
There are 2 independent parts, one for each index of `groups`. A program takes and returns all parts, laid end to end along the dimension named above; an argument that names none is the same for every part. Nothing has to cross between parts.
Inputs may be any that keep to these rules, and one draw needn't show every extreme that they name: Device d's live slots are its first live_count[d] slots; live_count sums to 48 and reaches 6 on some device.
All inputs are finite; a program needn't handle non-finite values.
Results may differ from a plain program's by a relative error of at most 0.0099.
Values may be sent and summed in bfloat16 or wider, within the bound.
No kernel may reach another device: no remote copies, remote signals or barrier semaphores. Data moves between devices by JAX's collectives and lax.ppermute only.
A program may use at most 128 MiB of HBM per device.

v0:
```python
import functools
import math

import jax
import jax.numpy as jnp
import ml_dtypes
import numpy as np
from jax import lax
from jax.experimental import pallas as pl
from jax.experimental.pallas import tpu as pltpu
from jax.sharding import PartitionSpec as P

F32 = jnp.float32
BF16 = jnp.bfloat16
LANES = 128
VMEM_BYTES = 56 * 2**20


def dft_tables(size):
    half = size // 2
    index = np.arange(size)
    angle = (index[:, None] * index[None, :] % size) * (2.0 * math.pi / size)
    scale = 1.0 / math.sqrt(size)
    cosine = (np.cos(angle) * scale).astype(ml_dtypes.bfloat16)
    sine = (np.sin(angle) * scale).astype(ml_dtypes.bfloat16)
    tables = []
    for parity in (0, 1):
        c, s = cosine[:half, parity::2], sine[:half, parity::2]
        tables.append(np.block([[c, -s], [s, c]]))
    order = np.zeros((size, size), ml_dtypes.bfloat16)
    order[2 * index[:half], index[:half]] = 1
    order[2 * index[:half] + 1, half + index[:half]] = 1
    even, odd = tables
    return jnp.asarray(np.stack([even, odd, even.T, odd.T, order, order.T]))


def dot(left, right):
    return jnp.dot(left, right, preferred_element_type=F32)


def fractions(code):
    return (code // 4).astype(F32) * 0.25, (code % 4).astype(F32) * 0.25


def project_kernel(size, width, bounds, stage, places, *refs):
    first_stage, last_stage = stage == 0, stage == len(bounds) - 2
    refs = list(refs)
    own, rim = refs[:2]
    rim_before = None if first_stage else refs[2]
    refs = refs[2:] if first_stage else refs[3:]
    probe_in, measured_in, tables_in = refs[:3]
    refs = refs[3:]
    if not first_stage:
        moved_in, sums_in, border_in = refs[:3]
        refs = refs[3:]
    moved, own_part, below = refs[:3]
    refs = refs[3:]
    if last_stage:
        keep, give = refs[:2]
    else:
        sums_out, border_out = refs[:2]
    refs = refs[2:]
    cells, mixed, patch, folded, half_u, half_v, far, error, back, probe, measured, tables, probe_acc = refs[:13]
    held, total, below_wide, sems = refs[13:17]
    if last_stage and not first_stage:
        sums, given = refs[17:]
    elif last_stage:
        given = refs[17]
    even, odd, even_t, odd_t, order, order_t = [tables.at[i] for i in range(6)]
    half = size // 2
    modes = probe.shape[0]
    slots = measured.shape[0]
    rows = own.shape[0]
    low, high = bounds[stage], bounds[stage + 1]
    base = 0 if first_stage else low - size
    extent = high - base
    settled = extent if last_stage else extent - size
    count = places[3, 0]
    copies = []

    def load(source, target):
        copies.append(pltpu.make_async_copy(source, target, sems.at[len(copies)]))

    for part in range(2):
        load(
            own.at[:, pl.ds(part * width + base, extent)],
            cells.at[pl.ds(0, rows), pl.ds(part * extent, extent)],
        )
        load(
            rim.at[:, pl.ds(part * (high - low), high - low)],
            cells.at[pl.ds(rows, size), pl.ds(part * extent + low - base, high - low)],
        )
        if not first_stage:
            before = low - bounds[stage - 1]
            load(
                rim_before.at[:, pl.ds((part + 1) * before - size, size)],
                cells.at[pl.ds(rows, size), pl.ds(part * extent, size)],
            )
    n_cells = len(copies)
    load(tables_in, tables)
    load(probe_in, probe)
    load(measured_in, measured)
    if not first_stage:
        for part in range(2):
            load(
                border_in.at[:, pl.ds(part * size, size)],
                total.at[pl.ds(0, rows + size), pl.ds(part * extent, size)],
            )
    n_later = len(copies)
    if not first_stage:
        load(sums_in, sums if last_stage else probe_acc)
    for copy in copies:
        copy.start()
    if last_stage or first_stage:
        probe_acc[...] = jnp.zeros_like(probe_acc)
    for part in range(2):
        fresh = slice(part * extent + (0 if first_stage else size), (part + 1) * extent)
        total[:, fresh] = jnp.zeros((total.shape[0], fresh.stop - fresh.start), F32)
    cells[rows + size :] = jnp.zeros((cells.shape[0] - rows - size, cells.shape[1]), BF16)
    for slot in range(slots):
        for axis in range(2):
            moved[axis, slot] = 0.0 if first_stage else moved_in[axis, slot]
    for copy in copies[:n_cells]:
        copy.wait()

    def wait_later():
        for copy in copies[n_cells : n_later if last_stage else len(copies)]:
            copy.wait()

    def mine(slot):
        end = places[1, slot] + size + 1
        return jnp.logical_and(slot < count, jnp.logical_and(end > low if not first_stage else True, end <= high))

    first_slot = jnp.int32(slots)
    for slot in reversed(range(slots)):
        first_slot = jnp.where(mine(slot), slot, first_slot)

    block = 16
    blocks = size // block
    lift_rows = half + 8
    lift_from = half + 32

    def one_slot(slot):
        top = places[0, slot]
        left = places[1, slot]
        frac_y, frac_x = fractions(places[2, slot])
        row0 = pl.multiple_of((top // 16) * 16, 16)
        col0 = pl.multiple_of((left // LANES) * LANES - base, LANES)
        down = top - row0
        across = left - base - col0
        source = lax.broadcasted_iota(jnp.int32, (2 * LANES, LANES), 0)
        target = lax.broadcasted_iota(jnp.int32, (2 * LANES, LANES), 1) + across
        here = (source == target).astype(F32)
        after = (source == target + 1).astype(F32)
        blend = jnp.concatenate([(1.0 - frac_x) * here + frac_x * after, after - here], axis=1).astype(BF16)
        source = lax.broadcasted_iota(jnp.int32, (lift_rows, lift_from), 1)
        target = lax.broadcasted_iota(jnp.int32, (lift_rows, lift_from), 0) + down
        lifts = [(source == target + shift).astype(F32).astype(BF16) for shift in (0, 8)]
        for part in range(2):
            start = pl.multiple_of(col0 + part * extent, LANES)
            for piece in range(2):
                taken = pl.ds(pl.multiple_of(row0 + piece * half, 16), lift_from)
                window = dot(lifts[piece], cells[taken, pl.ds(start, size + LANES)]).astype(BF16)
                for h in range(size // LANES):
                    mixed[part, pl.ds(piece * lift_rows, lift_rows), h * size : (h + 1) * size] = dot(
                        window[:, h * LANES : (h + 2) * LANES], blend
                    )
        for part in range(2):
            for h in range(size // LANES):
                cols = slice(h * size, h * size + LANES)
                for b in range(0, size, block):
                    upper = mixed[part, pl.ds(b, block), cols]
                    lower = mixed[part, pl.ds(b + 1, block), cols]
                    to = slice(part * size + h * LANES, part * size + (h + 1) * LANES)
                    patch[pl.ds(b, block), to] = (1.0 - frac_y) * upper + frac_y * lower
        pl.when(slot == first_slot)(wait_later)

        for mode in range(modes):
            for b in range(blocks):
                at = slice(b * block, (b + 1) * block)
                spot = (2 * b if b < blocks // 2 else 2 * b + 1 - blocks) * block
                to = slice(spot, spot + block)
                preal, pimag = probe[mode, at, :size], probe[mode, at, size:]
                oreal, oimag = patch[at, :size], patch[at, size:]
                wreal = preal * oreal - pimag * oimag
                wimag = preal * oimag + pimag * oreal
                for part, wave in enumerate((wreal, wimag)):
                    folded[mode, to, part * half : (part + 1) * half] = (wave[:, :half] + wave[:, half:]).astype(BF16)
                    folded[mode, to, size + part * half : size + (part + 1) * half] = (
                        wave[:, :half] - wave[:, half:]
                    ).astype(BF16)
        for mode in range(modes):
            for k, table in enumerate((even, odd)):
                out = dot(folded[mode, :, k * size : (k + 1) * size], table[...])
                for b in range(blocks // 2):
                    upper = out[2 * b * block : (2 * b + 1) * block]
                    lower = out[(2 * b + 1) * block : (2 * b + 2) * block]
                    plus, minus = (upper + lower).astype(BF16), (upper - lower).astype(BF16)
                    for part in range(2):
                        to = slice(part * half + b * block, part * half + (b + 1) * block)
                        cols = slice(part * half, (part + 1) * half)
                        half_u[mode, to, k * half : (k + 1) * half] = plus[:, cols]
                        half_v[mode, to, k * half : (k + 1) * half] = minus[:, cols]
        for mode in range(modes):
            far[mode, 0] = dot(even_t[...], half_u[mode])
            far[mode, 1] = dot(odd_t[...], half_v[mode])

        amplitude = dot(dot(order_t[...], measured[slot]).astype(BF16), order[...])
        for k in range(2):
            for b in range(0, half, block):
                pieces = [
                    [far[mode, k, part * half + b : part * half + b + block, :] for part in range(2)]
                    for mode in range(modes)
                ]
                power = sum(p * p for pair in pieces for p in pair)
                level = amplitude[k * half + b : k * half + b + block]
                ratio = 1.0 - level / jnp.maximum(jnp.sqrt(power), 0.5)
                for mode in range(modes):
                    for part in range(2):
                        to = slice(part * half + b, part * half + b + block)
                        error[mode, k, to, :] = (pieces[mode][part] * ratio).astype(BF16)

        for mode in range(modes):
            first = dot(even[...], error[mode, 0])
            second = dot(odd[...], error[mode, 1])
            plus, minus = (first + second).astype(BF16), (first - second).astype(BF16)
            for part in range(2):
                for b in range(blocks):
                    pick = part * half + (b % (blocks // 2)) * block
                    piece = (plus if b < blocks // 2 else minus)[pick : pick + block]
                    to = slice((b * modes + mode) * block, (b * modes + mode + 1) * block)
                    for c in range(2):
                        cols = slice(c * size + part * half, c * size + (part + 1) * half)
                        back[to, cols] = piece[:, c * half : (c + 1) * half]

        total_y = jnp.zeros((block, half), F32)
        total_x = jnp.zeros((block, half), F32)
        group = size // (modes * block)
        for g in range(blocks // group):
            span = slice(g * size, (g + 1) * size)
            first = dot(back[span, :size], even_t[...])
            second = dot(back[span, size:], odd_t[...])
            for r in range(group):
                at = slice((g * group + r) * block, (g * group + r + 1) * block)
                below = slice(at.start + 1, at.stop + 1)
                for h in range(2):
                    re = slice(h * half, (h + 1) * half)
                    im = slice(size + h * half, size + (h + 1) * half)
                    oreal, oimag = patch[at, re], patch[at, im]
                    greal = jnp.zeros((block, half), F32)
                    gimag = jnp.zeros((block, half), F32)
                    for mode in range(modes):
                        part = slice((r * modes + mode) * block, (r * modes + mode + 1) * block)
                        piece = first[part] + second[part] if h == 0 else first[part] - second[part]
                        ureal, uimag = piece[:, :half], piece[:, half:]
                        preal, pimag = probe[mode, at, re], probe[mode, at, im]
                        greal += preal * ureal + pimag * uimag
                        gimag += preal * uimag - pimag * ureal
                        probe_acc[mode, at, re] += oreal * ureal + oimag * uimag
                        probe_acc[mode, at, im] += oreal * uimag - oimag * ureal
                    held[at, re] = greal.astype(BF16)
                    held[at, im] = gimag.astype(BF16)
                    for part, grad in enumerate((greal, gimag)):
                        cols = slice(h * size, h * size + LANES)
                        total_y += grad * (mixed[part, below, cols] - mixed[part, at, cols])
                        cols = slice(h * size + LANES, (h + 1) * size)
                        total_x += grad * ((1.0 - frac_y) * mixed[part, at, cols] + frac_y * mixed[part, below, cols])
        moved[0, slot] = jnp.sum(total_y) / size
        moved[1, slot] = jnp.sum(total_x) / size

        source = lax.broadcasted_iota(jnp.int32, (size, size + LANES), 0) + across
        target = lax.broadcasted_iota(jnp.int32, (size, size + LANES), 1)
        along = jnp.where(source == target, 1.0 - frac_x, 0.0) + jnp.where(source + 1 == target, frac_x, 0.0)
        along = along.astype(BF16)
        spread = size + 16
        row8 = pl.multiple_of((top // 8) * 8, 8)
        source = lax.broadcasted_iota(jnp.int32, (spread, size), 1) + (top - row8)
        target = lax.broadcasted_iota(jnp.int32, (spread, size), 0)
        drop = jnp.where(source == target, 1.0 - frac_y, 0.0) + jnp.where(source + 1 == target, frac_y, 0.0)
        drop = drop.astype(BF16)
        for part in range(2):
            wide = dot(held[:, part * size : (part + 1) * size], along).astype(BF16)
            start = pl.multiple_of(col0 + part * extent, LANES)
            total[pl.ds(row8, spread), pl.ds(start, size + LANES)] += dot(drop, wide)

    @pl.loop(0, slots)
    def _(slot):
        pl.when(mine(slot))(functools.partial(one_slot, slot))

    pl.when(first_slot == slots)(wait_later)
    outs = []

    def store(source, target):
        outs.append(pltpu.make_async_copy(source, target, sems.at[len(outs)]))
        outs[-1].start()

    if last_stage:
        core = places[4, 0]
        share = modes // 2
        give_from = (1 - core) * share
        keep_from = core * share
        if first_stage:
            given[...] = probe_acc[pl.ds(give_from, share)].astype(BF16)
        else:
            copies[-1].wait()
            given[...] = (probe_acc[pl.ds(give_from, share)] + sums[pl.ds(give_from, share)]).astype(BF16)
        store(given, give)
        if not first_stage:
            probe_acc[pl.ds(keep_from, share)] += sums[pl.ds(keep_from, share)]
        store(probe_acc.at[pl.ds(keep_from, share)], keep)
    else:
        store(probe_acc, sums_out)
        for part in range(2):
            store(
                total.at[pl.ds(0, rows + size), pl.ds(part * extent + settled, size)],
                border_out.at[:, pl.ds(part * size, size)],
            )
    for part in range(2):
        here = slice(part * extent, part * extent + settled)
        below_wide[:, part * settled : (part + 1) * settled] = total[rows : rows + size, here].astype(BF16)
    store(below_wide, below)
    for part in range(2):
        store(
            total.at[pl.ds(0, rows), pl.ds(part * extent, settled)],
            own_part.at[:, pl.ds(part * settled, settled)],
        )
    for out in outs:
        out.wait()


def project(stage, bounds, places, own, rims, probe, measured, tables, width, carried):
    slots, size, _ = measured.shape
    modes = probe.shape[0]
    rows = own.shape[0]
    smem = pl.BlockSpec(memory_space=pltpu.SMEM)
    hbm = pl.BlockSpec(memory_space=pl.ANY)
    first_stage, last_stage = stage == 0, stage == len(bounds) - 2
    low, high = bounds[stage], bounds[stage + 1]
    extent = high - (0 if first_stage else low - size)
    settled = extent if last_stage else extent - size
    inputs = [places, own, rims[stage]] + ([] if first_stage else [rims[stage - 1]]) + [probe, measured, tables]
    specs = [smem] + [hbm] * (len(inputs) - 1)
    outs = [
        jax.ShapeDtypeStruct((2, slots), F32),
        jax.ShapeDtypeStruct((rows, 2 * settled), F32),
        jax.ShapeDtypeStruct((size, 2 * settled), BF16),
    ]
    share = (modes // 2,) + probe.shape[1:]
    if not first_stage:
        inputs += list(carried)
        specs += [smem, hbm, hbm]
    if last_stage:
        outs += [jax.ShapeDtypeStruct(share, F32), jax.ShapeDtypeStruct(share, BF16)]
    else:
        outs += [jax.ShapeDtypeStruct(probe.shape, F32), jax.ShapeDtypeStruct((rows + size, 2 * size), F32)]
    scratch = [
        pltpu.VMEM((rows + size + 32, 2 * extent), BF16),
        pltpu.VMEM((2, size + 16, 2 * size), F32),
        pltpu.VMEM((size, 2 * size), F32),
        pltpu.VMEM((modes, size, 2 * size), BF16),
        pltpu.VMEM((modes, size, size), BF16),
        pltpu.VMEM((modes, size, size), BF16),
        pltpu.VMEM((modes, 2, size, size), F32),
        pltpu.VMEM((modes, 2, size, size), BF16),
        pltpu.VMEM((modes * size, 2 * size), BF16),
        pltpu.VMEM(probe.shape, F32),
        pltpu.VMEM(measured.shape, BF16),
        pltpu.VMEM(tables.shape, BF16),
        pltpu.VMEM(probe.shape, F32),
        pltpu.VMEM((size, 2 * size), BF16),
        pltpu.VMEM((rows + size + 16, 2 * extent), F32),
        pltpu.VMEM((size, 2 * settled), BF16),
        pltpu.SemaphoreType.DMA((12,)),
    ]
    if last_stage and not first_stage:
        scratch.append(pltpu.VMEM(probe.shape, F32))
    if last_stage:
        scratch.append(pltpu.VMEM(share, BF16))
    return pl.pallas_call(
        functools.partial(project_kernel, size, width, bounds, stage),
        in_specs=specs,
        out_specs=[smem] + [hbm] * (len(outs) - 1),
        out_shape=outs,
        scratch_shapes=scratch,
        compiler_params=pltpu.CompilerParams(vmem_limit_bytes=VMEM_BYTES),
        cost_estimate=pl.CostEstimate(flops=8 * 10**9, bytes_accessed=16 * 2**20, transcendentals=0),
        name=f"project_{stage}",
    )(*inputs)


def finish_kernel(lows, highs, n, *refs):
    owns, aboves = refs[:n], refs[n : 2 * n]
    out, wides, adds, sems = refs[-3 - 2 * n], refs[-2 - 2 * n : -2 - n], refs[-2 - n : -2], refs[-2:]
    outs = []
    loads = []
    for i in range(n):
        loads.append(pltpu.make_async_copy(owns[i], wides[i], sems[0].at[2 * i]))
        loads.append(pltpu.make_async_copy(aboves[i], adds[i], sems[0].at[2 * i + 1]))
    for copy in loads:
        copy.start()
    for i in range(n):
        loads[2 * i].wait()
        loads[2 * i + 1].wait()
        length = highs[i] - lows[i]
        for part in range(2):
            cols = slice(part * length, (part + 1) * length)
            wides[i][:, cols] += adds[i][:, cols].astype(F32)
            copy = pltpu.make_async_copy(
                wides[i].at[:, pl.ds(part * length, length)],
                out.at[:, part, pl.ds(lows[i], length)],
                sems[1].at[2 * i + part],
            )
            copy.start()
            outs.append(copy)
    for copy in outs:
        copy.wait()


def finish(owns, aboves, lows, highs, width):
    n = len(owns)
    hbm = pl.BlockSpec(memory_space=pl.ANY)
    rows = owns[0].shape[0]
    return pl.pallas_call(
        functools.partial(finish_kernel, lows, highs, n),
        in_specs=[hbm] * (2 * n),
        out_specs=hbm,
        out_shape=jax.ShapeDtypeStruct((rows, 2, width), F32),
        scratch_shapes=[pltpu.VMEM(x.shape, F32) for x in owns]
        + [pltpu.VMEM(x.shape, BF16) for x in aboves]
        + [pltpu.SemaphoreType.DMA((2 * n,)), pltpu.SemaphoreType.DMA((2 * n,))],
        compiler_params=pltpu.CompilerParams(vmem_limit_bytes=VMEM_BYTES),
        name="finish",
    )(*owns, *aboves)


def passed_along(x, axis, by):
    length = lax.axis_size(axis)
    pairs = [(i, i + by) for i in range(length) if 0 <= i + by < length]
    return lax.ppermute(x, axis, pairs)


def unpack_kernel(order, *refs):
    pieces, out, wide, sems = refs[:-3], refs[-3], refs[-2], refs[-1]
    rows = pieces[0].shape[0]
    modes, size, _, _ = out.shape
    copies = []
    for i, piece in enumerate(pieces):
        wide[i * rows : (i + 1) * rows] = piece[...].astype(F32)
        mode = order[i] // (size // rows)
        at = pl.multiple_of(order[i] % (size // rows) * rows, 8)
        for part in range(2):
            copy = pltpu.make_async_copy(
                wide.at[pl.ds(i * rows, rows), pl.ds(part * size, size)],
                out.at[mode, pl.ds(at, rows), part, :],
                sems.at[2 * i + part],
            )
            copy.start()
            copies.append(copy)
    for copy in copies:
        copy.wait()


def unpacked(pieces, order, shape):
    vmem = pl.BlockSpec(memory_space=pltpu.VMEM)
    smem = pl.BlockSpec(memory_space=pltpu.SMEM)
    return pl.pallas_call(
        unpack_kernel,
        in_specs=[smem] + [vmem] * len(pieces),
        out_specs=pl.BlockSpec(memory_space=pl.ANY),
        out_shape=jax.ShapeDtypeStruct(shape, F32),
        scratch_shapes=[
            pltpu.VMEM((len(pieces) * pieces[0].shape[0], pieces[0].shape[1]), F32),
            pltpu.SemaphoreType.DMA((2 * len(pieces),)),
        ],
        compiler_params=pltpu.CompilerParams(vmem_limit_bytes=VMEM_BYTES),
        name="unpack",
    )(order, *pieces)


def piece_order(axis):
    length = lax.axis_size(axis)
    near = min(4, length // 2)
    me = lax.axis_index(axis)
    core, spot = me % 2, me // 2 % near
    return jnp.stack(
        [core * near + (spot ^ s) for s in range(near)] + [(1 - core) * near + (spot ^ s) for s in range(near)]
    )


def summed(keep, give, axis, shape, order, late):
    length = lax.axis_size(axis)
    chips = length // 2
    near = min(4, chips)
    far = chips // near
    me = lax.axis_index(axis)
    core, chip = me % 2, me // 2
    across = [(i, i ^ 1) for i in range(length)]

    def hop(shift, stride):
        return [(i, i ^ (2 * stride * shift)) for i in range(length)]

    size, columns = keep.shape[1:]
    mine = keep + lax.ppermute(give, axis, across).astype(F32)
    rows = mine.shape[0] * size // near
    mine = mine.reshape(near, rows, columns)
    parts = mine.astype(BF16)
    spot = chip % near
    got = [
        lax.ppermute(lax.dynamic_index_in_dim(parts, spot ^ s, 0, False), axis, hop(s, 1)) for s in range(1, near)
    ]
    total = lax.dynamic_index_in_dim(mine, spot, 0, False)
    for piece in got:
        total = total + piece.astype(F32)
    sent = total.astype(BF16)
    sent, late = lax.optimization_barrier((sent, late))
    for s in range(1, far):
        total = total + lax.ppermute(sent, axis, hop(s, near)).astype(F32)
    total = total.astype(BF16)
    pieces = [total] + [lax.ppermute(total, axis, hop(s, 1)) for s in range(1, near)]
    others = [lax.ppermute(piece, axis, across) for piece in pieces]
    return unpacked(pieces + others, order, shape), late


def column_bounds(width, shares):
    return tuple([0] + [round(width * share / LANES) * LANES for share in shares] + [width])


def shards(object_tiles, probe, measured, offset_row, offset_col, subpixel, live_count):
    rows, _, width = object_tiles.shape
    modes, size = probe.shape[:2]
    tables = dft_tables(size)
    bounds = column_bounds(width, (0.5625,))
    stages = len(bounds) - 1
    rims = [
        passed_along(object_tiles[:size, :, low:high].reshape(size, 2 * (high - low)), "row", -1)
        for low, high in zip(bounds[:-1], bounds[1:])
    ]
    core = lax.axis_index("row") % 2
    places = jnp.stack(
        [offset_row, offset_col, subpixel] + [jnp.broadcast_to(x, offset_row.shape) for x in (live_count, core)]
    )
    places, order = lax.optimization_barrier((places, piece_order("row")))
    own = object_tiles.reshape(rows, 2 * width)
    flat = probe.reshape(modes, size, 2 * size)
    carried = None
    owns, belows = [], []
    for stage in range(stages):
        moved, own_part, below, *rest = project(
            stage, bounds, places, own, rims, flat, measured, tables, width, carried
        )
        carried = [moved] + rest
        owns.append(own_part)
        belows.append(below)
    _, keep, give = carried
    edges = [0] + [bound - size for bound in bounds[1:-1]] + [width]
    aboves = [passed_along(below, "row", 1) for below in belows[:-1]]
    probe_grad, late = summed(keep, give, "row", probe.shape, order, belows[-1])
    aboves.append(passed_along(late, "row", 1))
    object_grad = finish(owns, aboves, edges[:-1], edges[1:], width)
    return object_grad, probe_grad, moved


def solution(mesh):
    in_specs = (
        P(("groups", "row"), None, None),
        P(),
        P(("groups", "row"), None, None),
        P(("groups", "row")),
        P(("groups", "row")),
        P(("groups", "row")),
        P(("groups", "row")),
    )
    out_specs = (
        P(("groups", "row"), None, None),
        P("groups", None, None, None),
        P(None, ("groups", "row")),
    )
    return jax.shard_map(shards, mesh=mesh, in_specs=in_specs, out_specs=out_specs, check_vma=False)
```

profile of v0, /device:TPU:16, one launch (start us, length us, event | category | flops | bytes accessed | tf_op | source)
XLA Modules:
  0.0 121.4 jit_solution(9584085499680454355)
XLA Ops:
  0.6 1.3 %slice-done = bf16[256,2,1152]{2,1,0:T(2,128)(2,1)S(1)} async-done(((bf16[256,2,2048]{2,1,0:T(2,128)(2,1)}), bf16[256,2,1152]{2,1,0:T(2,128)(2,1)S(1)}, s32[]{:S(2)}) %slice-start) | async-done | bytes 1179672 | tf_op jit(solution)/shard_map/slice | solution.py:535
  2.1 2.9 %collective-permute-start = (bf16[256,2304]{1,0:T(8,128)(2,1)S(1)}, bf16[256,2304]{1,0:T(8,128)(2,1)}, u32[]{:S(2)}, u32[]{:S(2)}) collective-permute-start(bf16[256,2304]{1,0:T(8,128)(2,1)S(1)} %bitcast.44), channel_id=1, source_target_pairs={{1,0},{2,1},{3,2},{4,3},{5,4},{6,5},{7,6},{8,7},{9,8},{10,9},{11,1... | collective-permute-start | bytes 3538952 | tf_op jit(solution)/shard_map/ppermute | solution.py:439
  5.0 1.0 copy.13
  6.0 2.6 %collective-permute-start.1 = (bf16[256,1792]{1,0:T(8,128)(2,1)}, bf16[256,1792]{1,0:T(8,128)(2,1)}, u32[]{:S(2)}, u32[]{:S(2)}) collective-permute-start(bf16[256,1792]{1,0:T(8,128)(2,1)} %bitcast.22), channel_id=1, source_target_pairs={{1,0},{2,1},{3,2},{4,3},{5,4},{6,5},{7,6},{8,7},{9,8},{10,9},{11,1... | collective-permute-start | bytes 2752520 | tf_op jit(solution)/shard_map/ppermute | solution.py:439
  9.3 0.6 stack.42.places
  9.9 0.6 stack.51.order
  10.5 4.0 %reshape.26.refs_2_.refs_3_ = f32[4,256,512]{2,1,0:T(8,128)} reshape(f32[4,256,2,256]{3,2,1,0:T(2,128)} %param.9) | data formatting | bytes 4194304 | tf_op jit(solution)/shard_map/reshape | solution.py:544
  14.6 2.2 %copy.11 = bf16[32,8,2,2048]{3,1,2,0:T(8,128)(2,1)} copy(bf16[32,8,2,2048]{3,2,1,0:T(2,128)(2,1)S(1)} %bitcast.36) | data formatting | bytes 4194304
  16.8 1.8 %collective-permute-done.refs_1_.refs_2_ = bf16[256,2304]{1,0:T(8,128)(2,1)} collective-permute-done((bf16[256,2304]{1,0:T(8,128)(2,1)S(1)}, bf16[256,2304]{1,0:T(8,128)(2,1)}, u32[]{:S(2)}, u32[]{:S(2)}) %collective-permute-start) | collective-permute-done | bytes 1179680 | tf_op jit(solution)/shard_map/ppermute | solution.py:439
  18.6 6.6 %project_0.1 = (f32[2,6]{1,0:T(2,128)}, f32[256,1792]{1,0:T(8,128)}, bf16[256,1792]{1,0:T(8,128)(2,1)}, f32[4,256,512]{2,1,0:T(8,128)}, f32[512,512]{1,0:T(8,128)}) custom-call(s32[5,6]{1,0:T(8,128)} %stack.42.places, bf16[256,4096]{1,0:T(8,128)(2,1)} %bitcast.42, bf16[256,2304]{1,0:T(8,128)(2,1)} %collective-permute-done.refs_1_.refs_2_, ...), custom_call_target="tpu_custom_call" | custom-call | flops 8000000000 | bytes 16777216 | tf_op jit(solution)/shard_map/project_0/pallas_call | solution.py:379
  25.3 3.3 %collective-permute-done.1.refs_1_ = bf16[256,1792]{1,0:T(8,128)(2,1)} collective-permute-done((bf16[256,1792]{1,0:T(8,128)(2,1)}, bf16[256,1792]{1,0:T(8,128)(2,1)}, u32[]{:S(2)}, u32[]{:S(2)}) %collective-permute-start.1) | collective-permute-done | bytes 917536 | tf_op jit(solution)/shard_map/ppermute | solution.py:439
  28.6 14.7 %project_1.1 = (f32[2,6]{1,0:T(2,128)}, f32[256,2304]{1,0:T(8,128)}, bf16[256,2304]{1,0:T(8,128)(2,1)}, f32[2,256,512]{2,1,0:T(8,128)}, bf16[2,256,512]{2,1,0:T(8,128)(2,1)}) custom-call(s32[5,6]{1,0:T(8,128)} %stack.42.places, bf16[256,4096]{1,0:T(8,128)(2,1)} %bitcast.43, bf16[256,1792]{1,0:T(8,128)(2,1)} %collective-permute-done.1.refs_1_, ...), custom_call_target="tpu_custom_call" | custom-call | flops 8000000000 | bytes 16777216 | tf_op jit(solution)/shard_map/project_1/pallas_call | solution.py:379
  43.4 2.1 %collective-permute-done.3 = bf16[2,256,512]{2,1,0:T(8,128)(2,1)S(1)} collective-permute-done((bf16[2,256,512]{2,1,0:T(8,128)(2,1)}, bf16[2,256,512]{2,1,0:T(8,128)(2,1)S(1)}, u32[]{:S(2)}, u32[]{:S(2)}) %collective-permute-start.3) | collective-permute-done | bytes 524320 | tf_op jit(solution)/shard_map/ppermute | solution.py:503
  45.5 1.4 %convert_add_fusion = f32[2,256,512]{2,1,0:T(8,128)S(1)} fusion(f32[2,256,512]{2,1,0:T(8,128)} %get-tuple-element.24, bf16[2,256,512]{2,1,0:T(8,128)(2,1)S(1)} %collective-permute-done.3), kind=kLoop, calls=%fused_computation | loop fusion | flops 524288 | bytes 2621440 | tf_op jit(solution)/shard_map/add | solution.py:503
  47.0 13.8 %collective-permute-start.4 = (bf16[128,512]{1,0:T(8,128)(2,1)S(1)}, bf16[128,512]{1,0:T(8,128)(2,1)S(1)}, u32[]{:S(2)}, u32[]{:S(2)}) collective-permute-start(bf16[128,512]{1,0:T(8,128)(2,1)S(1)} %get-tuple-element.31), channel_id=1, source_target_pairs={{0,2},{1,3},{2,0},{3,1},{4,6},{5,7},{6,4},{7,5},{8,10},{9,11},{10,... | collective-permute-start | bytes 393224 | tf_op jit(solution)/shard_map/ppermute | solution.py:509
  60.8 1.5 %collective-permute-start.5 = (bf16[128,512]{1,0:T(8,128)(2,1)S(1)}, bf16[128,512]{1,0:T(8,128)(2,1)S(1)}, u32[]{:S(2)}, u32[]{:S(2)}) collective-permute-start(bf16[128,512]{1,0:T(8,128)(2,1)S(1)} %get-tuple-element.33), channel_id=1, source_target_pairs={{0,4},{1,5},{2,6},{3,7},{4,0},{5,1},{6,2},{7,3},{8,12},{9,13},{10,... | collective-permute-start | bytes 393224 | tf_op jit(solution)/shard_map/ppermute | solution.py:509
  62.4 4.4 %collective-permute-done.4 = bf16[128,512]{1,0:T(8,128)(2,1)S(1)} collective-permute-done((bf16[128,512]{1,0:T(8,128)(2,1)S(1)}, bf16[128,512]{1,0:T(8,128)(2,1)S(1)}, u32[]{:S(2)}, u32[]{:S(2)}) %collective-permute-start.4) | collective-permute-done | bytes 131104 | tf_op jit(solution)/shard_map/ppermute | solution.py:509
  66.7 1.4 %collective-permute-done.6 = bf16[128,512]{1,0:T(8,128)(2,1)S(1)} collective-permute-done((bf16[128,512]{1,0:T(8,128)(2,1)S(1)}, bf16[128,512]{1,0:T(8,128)(2,1)S(1)}, u32[]{:S(2)}, u32[]{:S(2)}) %collective-permute-start.6) | collective-permute-done | bytes 131104 | tf_op jit(solution)/shard_map/ppermute | solution.py:509
  68.1 0.6 collective-permute-done.5
  68.8 1.9 %collective-permute-start.7 = (bf16[256,2304]{1,0:T(8,128)(2,1)S(1)}, bf16[256,2304]{1,0:T(8,128)(2,1)S(1)}, u32[]{:S(2)}, u32[]{:S(2)}) collective-permute-start(bf16[256,2304]{1,0:T(8,128)(2,1)S(1)} %copy-done.14), channel_id=1, source_target_pairs={{0,1},{1,2},{2,3},{3,4},{4,5},{5,6},{6,7},{7,8},{8,9},{9,10},{10,1... | collective-permute-start | bytes 3538952 | tf_op jit(solution)/shard_map/ppermute | solution.py:439
  70.7 3.7 %collective-permute-start.2 = (bf16[256,1792]{1,0:T(8,128)(2,1)}, bf16[256,1792]{1,0:T(8,128)(2,1)S(1)}, u32[]{:S(2)}, u32[]{:S(2)}) collective-permute-start(bf16[256,1792]{1,0:T(8,128)(2,1)} %get-tuple-element.23), channel_id=1, source_target_pairs={{0,1},{1,2},{2,3},{3,4},{4,5},{5,6},{6,7},{7,8},{8,9},{9,10},{10,1... | collective-permute-start | bytes 2752520 | tf_op jit(solution)/shard_map/ppermute | solution.py:439
  74.4 1.1 collective-permute-start.8
  75.5 5.6 %collective-permute-done.8 = bf16[128,512]{1,0:T(8,128)(2,1)S(1)} collective-permute-done((bf16[128,512]{1,0:T(8,128)(2,1)S(1)}, bf16[128,512]{1,0:T(8,128)(2,1)S(1)}, u32[]{:S(2)}, u32[]{:S(2)}) %collective-permute-start.8) | collective-permute-done | bytes 131104 | tf_op jit(solution)/shard_map/ppermute | solution.py:517
  81.3 23.0 %collective-permute-start.11 = (bf16[128,512]{1,0:T(8,128)(2,1)S(1)}, bf16[128,512]{1,0:T(8,128)(2,1)S(1)}, u32[]{:S(2)}, u32[]{:S(2)}) collective-permute-start(bf16[128,512]{1,0:T(8,128)(2,1)S(1)} %add_convert_fusion.refs_0_), channel_id=1, source_target_pairs={{0,6},{1,7},{2,4},{3,5},{4,2},{5,3},{6,0},{7,1},{8,14},{9,15},{10,... | collective-permute-start | bytes 393224 | tf_op jit(solution)/shard_map/ppermute | solution.py:519
  104.8 3.7 %collective-permute-done.11.refs_3_ = bf16[128,512]{1,0:T(8,128)(2,1)S(1)} collective-permute-done((bf16[128,512]{1,0:T(8,128)(2,1)S(1)}, bf16[128,512]{1,0:T(8,128)(2,1)S(1)}, u32[]{:S(2)}, u32[]{:S(2)}) %collective-permute-start.11) | collective-permute-done | bytes 131104 | tf_op jit(solution)/shard_map/ppermute | solution.py:519
  108.5 1.5 %collective-permute-done.10.refs_2_ = bf16[128,512]{1,0:T(8,128)(2,1)S(1)} collective-permute-done((bf16[128,512]{1,0:T(8,128)(2,1)S(1)}, bf16[128,512]{1,0:T(8,128)(2,1)S(1)}, u32[]{:S(2)}, u32[]{:S(2)}) %collective-permute-start.10) | collective-permute-done | bytes 131104 | tf_op jit(solution)/shard_map/ppermute | solution.py:519
  110.1 0.7 collective-permute-done.9.refs_1_
  111.4 0.7 collective-permute-done.13.refs_5_
  112.2 0.6 copy-done.10
  112.8 2.7 %unpack.1 = f32[4,256,2,256]{3,2,1,0:T(2,128)} custom-call(s32[8]{0:T(128)} %stack.51.order, bf16[128,512]{1,0:T(8,128)(2,1)} %copy-done.3, bf16[128,512]{1,0:T(8,128)(2,1)} %copy-done.7, bf16[128,512]{1,0:T(8,128)(2,1)} %copy-done.6, bf16[128,512]{1,0:T(8,128)(2,1)} %copy-done.5, bf16[128,512]{1,0:T(8,128)(2,1)} %copy-done.4, bf16[128,512]{1,0:T(8,128)(2,1)} %copy-done.10, ...), custom_call_target="tpu_custom_call" | custom-call | tf_op jit(solution)/shard_map/unpack/pallas_call | solution.py:466
  115.6 0.9 copy-done.2
  116.9 4.5 %finish.1 = f32[256,2,2048]{2,1,0:T(2,128)} custom-call(f32[256,1792]{1,0:T(8,128)} %get-tuple-element.18.refs_0_, f32[256,2304]{1,0:T(8,128)} %get-tuple-element.22.refs_1_, bf16[256,1792]{1,0:T(8,128)(2,1)} %copy-done.2, bf16[256,2304]{1,0:T(8,128)(2,1)} %copy-done.1), custom_call_target="tpu_custom_call" | custom-call | tf_op jit(solution)/shard_map/finish/pallas_call | solution.py:423
  (51 shorter events, 2.2 us)
Async XLA Ops:
  0.6 1.3 %slice-start = ((bf16[256,2,2048]{2,1,0:T(2,128)(2,1)}), bf16[256,2,1152]{2,1,0:T(2,128)(2,1)S(1)}, s32[]{:S(2)}) async-start(bf16[256,2,2048]{2,1,0:T(2,128)(2,1)} %param.8), calls=%async_computation | async-start | bytes 2359296 | tf_op jit(solution)/shard_map/slice | solution.py:535
  1.9 3.0 %slice-start.1 = ((bf16[256,2,2048]{2,1,0:T(2,128)(2,1)}), bf16[256,2,896]{2,1,0:T(2,128)(2,1)S(1)}, s32[]{:S(2)}) async-start(bf16[256,2,2048]{2,1,0:T(2,128)(2,1)} %param.8), calls=%async_computation.1 | async-start | bytes 1835008 | tf_op jit(solution)/shard_map/slice | solution.py:535
  2.0 7.2 %copy-start.11 = (s32[6]{0:T(128)S(1)}, s32[6]{0:T(128)}, u32[]{:S(2)}) copy-start(s32[6]{0:T(128)} %param.11) | copy-start | bytes 76
  2.1 7.2 %copy-start.12 = (s32[6]{0:T(128)S(1)}, s32[6]{0:T(128)}, u32[]{:S(2)}) copy-start(s32[6]{0:T(128)} %param.12) | copy-start | bytes 76
  2.1 7.2 %copy-start.13 = (s32[6]{0:T(128)S(1)}, s32[6]{0:T(128)}, u32[]{:S(2)}) copy-start(s32[6]{0:T(128)} %param.13) | copy-start | bytes 76
  2.1 16.6 %collective-permute-start = (bf16[256,2304]{1,0:T(8,128)(2,1)S(1)}, bf16[256,2304]{1,0:T(8,128)(2,1)}, u32[]{:S(2)}, u32[]{:S(2)}) collective-permute-start(bf16[256,2304]{1,0:T(8,128)(2,1)S(1)} %bitcast.44), channel_id=1, source_target_pairs={{1,0},{2,1},{3,2},{4,3},{5,4},{6,5},{7,6},{8,7},{9,8},{10,9},{11,1... | collective-permute-start | bytes 3538952 | tf_op jit(solution)/shard_map/ppermute | solution.py:439
  6.0 22.6 %collective-permute-start.1 = (bf16[256,1792]{1,0:T(8,128)(2,1)}, bf16[256,1792]{1,0:T(8,128)(2,1)}, u32[]{:S(2)}, u32[]{:S(2)}) collective-permute-start(bf16[256,1792]{1,0:T(8,128)(2,1)} %bitcast.22), channel_id=1, source_target_pairs={{1,0},{2,1},{3,2},{4,3},{5,4},{6,5},{7,6},{8,7},{9,8},{10,9},{11,1... | collective-permute-start | bytes 2752520 | tf_op jit(solution)/shard_map/ppermute | solution.py:439
  10.5 4.0 %copy-start = (bf16[256,2,2048]{2,1,0:T(2,128)(2,1)S(1)}, bf16[256,2,2048]{2,1,0:T(2,128)(2,1)}, u32[]{:S(2)}) copy-start(bf16[256,2,2048]{2,1,0:T(2,128)(2,1)} %param.8) | copy-start | bytes 6291460
  43.3 2.2 %collective-permute-start.3 = (bf16[2,256,512]{2,1,0:T(8,128)(2,1)}, bf16[2,256,512]{2,1,0:T(8,128)(2,1)S(1)}, u32[]{:S(2)}, u32[]{:S(2)}) collective-permute-start(bf16[2,256,512]{2,1,0:T(8,128)(2,1)} %get-tuple-element.25), channel_id=1, source_target_pairs={{0,1},{1,0},{2,3},{3,2},{4,5},{5,4},{6,7},{7,6},{8,9},{9,8},{10,11... | collective-permute-start | bytes 1572872 | tf_op jit(solution)/shard_map/ppermute | solution.py:503
  46.9 21.9 %copy-start.14 = (bf16[256,2304]{1,0:T(8,128)(2,1)S(1)}, bf16[256,2304]{1,0:T(8,128)(2,1)}, u32[]{:S(2)}) copy-start(bf16[256,2304]{1,0:T(8,128)(2,1)} %get-tuple-element.27) | copy-start | bytes 3538948
  47.0 19.8 %collective-permute-start.4 = (bf16[128,512]{1,0:T(8,128)(2,1)S(1)}, bf16[128,512]{1,0:T(8,128)(2,1)S(1)}, u32[]{:S(2)}, u32[]{:S(2)}) collective-permute-start(bf16[128,512]{1,0:T(8,128)(2,1)S(1)} %get-tuple-element.31), channel_id=1, source_target_pairs={{0,2},{1,3},{2,0},{3,1},{4,6},{5,7},{6,4},{7,5},{8,10},{9,11},{10,... | collective-permute-start | bytes 393224 | tf_op jit(solution)/shard_map/ppermute | solution.py:509
  60.8 7.3 %collective-permute-start.6 = (bf16[128,512]{1,0:T(8,128)(2,1)S(1)}, bf16[128,512]{1,0:T(8,128)(2,1)S(1)}, u32[]{:S(2)}, u32[]{:S(2)}) collective-permute-start(bf16[128,512]{1,0:T(8,128)(2,1)S(1)} %get-tuple-element.32), channel_id=1, source_target_pairs={{0,6},{1,7},{2,4},{3,5},{4,2},{5,3},{6,0},{7,1},{8,14},{9,15},{10,... | collective-permute-start | bytes 393224 | tf_op jit(solution)/shard_map/ppermute | solution.py:509
  60.8 7.9 %collective-permute-start.5 = (bf16[128,512]{1,0:T(8,128)(2,1)S(1)}, bf16[128,512]{1,0:T(8,128)(2,1)S(1)}, u32[]{:S(2)}, u32[]{:S(2)}) collective-permute-start(bf16[128,512]{1,0:T(8,128)(2,1)S(1)} %get-tuple-element.33), channel_id=1, source_target_pairs={{0,4},{1,5},{2,6},{3,7},{4,0},{5,1},{6,2},{7,3},{8,12},{9,13},{10,... | collective-permute-start | bytes 393224 | tf_op jit(solution)/shard_map/ppermute | solution.py:509
  68.8 46.8 %collective-permute-start.7 = (bf16[256,2304]{1,0:T(8,128)(2,1)S(1)}, bf16[256,2304]{1,0:T(8,128)(2,1)S(1)}, u32[]{:S(2)}, u32[]{:S(2)}) collective-permute-start(bf16[256,2304]{1,0:T(8,128)(2,1)S(1)} %copy-done.14), channel_id=1, source_target_pairs={{0,1},{1,2},{2,3},{3,4},{4,5},{5,6},{6,7},{7,8},{8,9},{9,10},{10,1... | collective-permute-start | bytes 3538952 | tf_op jit(solution)/shard_map/ppermute | solution.py:439
  70.7 44.8 %collective-permute-start.2 = (bf16[256,1792]{1,0:T(8,128)(2,1)}, bf16[256,1792]{1,0:T(8,128)(2,1)S(1)}, u32[]{:S(2)}, u32[]{:S(2)}) collective-permute-start(bf16[256,1792]{1,0:T(8,128)(2,1)} %get-tuple-element.23), channel_id=1, source_target_pairs={{0,1},{1,2},{2,3},{3,4},{4,5},{5,6},{6,7},{7,8},{8,9},{9,10},{10,1... | collective-permute-start | bytes 2752520 | tf_op jit(solution)/shard_map/ppermute | solution.py:439
  74.4 6.7 %collective-permute-start.8 = (bf16[128,512]{1,0:T(8,128)(2,1)S(1)}, bf16[128,512]{1,0:T(8,128)(2,1)S(1)}, u32[]{:S(2)}, u32[]{:S(2)}) collective-permute-start(bf16[128,512]{1,0:T(8,128)(2,1)S(1)} %fusion.2), channel_id=1, source_target_pairs={{0,8},{1,9},{2,10},{3,11},{4,12},{5,13},{6,14},{7,15},{8,0},{9,1},... | collective-permute-start | bytes 393224 | tf_op jit(solution)/shard_map/ppermute | solution.py:517
  81.2 31.0 %copy-start.3 = (bf16[128,512]{1,0:T(8,128)(2,1)}, bf16[128,512]{1,0:T(8,128)(2,1)S(1)}, u32[]{:S(2)}) copy-start(bf16[128,512]{1,0:T(8,128)(2,1)S(1)} %add_convert_fusion.refs_0_) | copy-start | bytes 393220
  81.2 23.1 %collective-permute-start.12 = (bf16[128,512]{1,0:T(8,128)(2,1)S(1)}, bf16[128,512]{1,0:T(8,128)(2,1)S(1)}, u32[]{:S(2)}, u32[]{:S(2)}) collective-permute-start(bf16[128,512]{1,0:T(8,128)(2,1)S(1)} %add_convert_fusion.refs_0_), channel_id=1, source_target_pairs={{0,1},{1,0},{2,3},{3,2},{4,5},{5,4},{6,7},{7,6},{8,9},{9,8},{10,11... | collective-permute-start | bytes 393224 | tf_op jit(solution)/shard_map/ppermute | solution.py:520
  81.3 27.3 %collective-permute-start.11 = (bf16[128,512]{1,0:T(8,128)(2,1)S(1)}, bf16[128,512]{1,0:T(8,128)(2,1)S(1)}, u32[]{:S(2)}, u32[]{:S(2)}) collective-permute-start(bf16[128,512]{1,0:T(8,128)(2,1)S(1)} %add_convert_fusion.refs_0_), channel_id=1, source_target_pairs={{0,6},{1,7},{2,4},{3,5},{4,2},{5,3},{6,0},{7,1},{8,14},{9,15},{10,... | collective-permute-start | bytes 393224 | tf_op jit(solution)/shard_map/ppermute | solution.py:519
  104.2 5.8 %collective-permute-start.10 = (bf16[128,512]{1,0:T(8,128)(2,1)S(1)}, bf16[128,512]{1,0:T(8,128)(2,1)S(1)}, u32[]{:S(2)}, u32[]{:S(2)}) collective-permute-start(bf16[128,512]{1,0:T(8,128)(2,1)S(1)} %add_convert_fusion.refs_0_), channel_id=1, source_target_pairs={{0,4},{1,5},{2,6},{3,7},{4,0},{5,1},{6,2},{7,3},{8,12},{9,13},{10,... | collective-permute-start | bytes 393224 | tf_op jit(solution)/shard_map/ppermute | solution.py:519
  104.2 7.9 %copy-start.4 = (bf16[128,512]{1,0:T(8,128)(2,1)}, bf16[128,512]{1,0:T(8,128)(2,1)S(1)}, u32[]{:S(2)}) copy-start(bf16[128,512]{1,0:T(8,128)(2,1)S(1)} %collective-permute-done.12.refs_4_) | copy-start | bytes 393220
  104.2 6.5 %collective-permute-start.9 = (bf16[128,512]{1,0:T(8,128)(2,1)S(1)}, bf16[128,512]{1,0:T(8,128)(2,1)S(1)}, u32[]{:S(2)}, u32[]{:S(2)}) collective-permute-start(bf16[128,512]{1,0:T(8,128)(2,1)S(1)} %add_convert_fusion.refs_0_), channel_id=1, source_target_pairs={{0,2},{1,3},{2,0},{3,1},{4,6},{5,7},{6,4},{7,5},{8,10},{9,11},{10,... | collective-permute-start | bytes 393224 | tf_op jit(solution)/shard_map/ppermute | solution.py:519
  108.5 3.6 %copy-start.5 = (bf16[128,512]{1,0:T(8,128)(2,1)}, bf16[128,512]{1,0:T(8,128)(2,1)S(1)}, u32[]{:S(2)}) copy-start(bf16[128,512]{1,0:T(8,128)(2,1)S(1)} %collective-permute-done.11.refs_3_) | copy-start | bytes 393220
  108.5 2.3 %collective-permute-start.15 = (bf16[128,512]{1,0:T(8,128)(2,1)S(1)}, bf16[128,512]{1,0:T(8,128)(2,1)S(1)}, u32[]{:S(2)}, u32[]{:S(2)}) collective-permute-start(bf16[128,512]{1,0:T(8,128)(2,1)S(1)} %collective-permute-done.11.refs_3_), channel_id=1, source_target_pairs={{0,1},{1,0},{2,3},{3,2},{4,5},{5,4},{6,7},{7,6},{8,9},{9,8},{10,11... | collective-permute-start | bytes 393224 | tf_op jit(solution)/shard_map/ppermute | solution.py:520
  110.0 2.1 %copy-start.6 = (bf16[128,512]{1,0:T(8,128)(2,1)}, bf16[128,512]{1,0:T(8,128)(2,1)S(1)}, u32[]{:S(2)}) copy-start(bf16[128,512]{1,0:T(8,128)(2,1)S(1)} %collective-permute-done.10.refs_2_) | copy-start | bytes 393220
  110.0 1.3 %collective-permute-start.14 = (bf16[128,512]{1,0:T(8,128)(2,1)S(1)}, bf16[128,512]{1,0:T(8,128)(2,1)S(1)}, u32[]{:S(2)}, u32[]{:S(2)}) collective-permute-start(bf16[128,512]{1,0:T(8,128)(2,1)S(1)} %collective-permute-done.10.refs_2_), channel_id=1, source_target_pairs={{0,1},{1,0},{2,3},{3,2},{4,5},{5,4},{6,7},{7,6},{8,9},{9,8},{10,11... | collective-permute-start | bytes 393224 | tf_op jit(solution)/shard_map/ppermute | solution.py:520
  110.8 1.4 %copy-start.7 = (bf16[128,512]{1,0:T(8,128)(2,1)}, bf16[128,512]{1,0:T(8,128)(2,1)S(1)}, u32[]{:S(2)}) copy-start(bf16[128,512]{1,0:T(8,128)(2,1)S(1)} %collective-permute-done.9.refs_1_) | copy-start | bytes 393220
  110.8 1.3 %collective-permute-start.13 = (bf16[128,512]{1,0:T(8,128)(2,1)S(1)}, bf16[128,512]{1,0:T(8,128)(2,1)S(1)}, u32[]{:S(2)}, u32[]{:S(2)}) collective-permute-start(bf16[128,512]{1,0:T(8,128)(2,1)S(1)} %collective-permute-done.9.refs_1_), channel_id=1, source_target_pairs={{0,1},{1,0},{2,3},{3,2},{4,5},{5,4},{6,7},{7,6},{8,9},{9,8},{10,11... | collective-permute-start | bytes 393224 | tf_op jit(solution)/shard_map/ppermute | solution.py:520
  110.8 1.4 %copy-start.8 = (bf16[128,512]{1,0:T(8,128)(2,1)}, bf16[128,512]{1,0:T(8,128)(2,1)S(1)}, u32[]{:S(2)}) copy-start(bf16[128,512]{1,0:T(8,128)(2,1)S(1)} %collective-permute-done.15.refs_7_) | copy-start | bytes 393220
  111.4 0.8 copy-start.9
  115.6 0.9 copy-start.2
  115.6 1.3 %copy-start.1 = (bf16[256,2304]{1,0:T(8,128)(2,1)}, bf16[256,2304]{1,0:T(8,128)(2,1)S(1)}, u32[]{:S(2)}) copy-start(bf16[256,2304]{1,0:T(8,128)(2,1)S(1)} %collective-permute-done.7.refs_3_) | copy-start | bytes 3538948
  (1 other events, 0.6 us)
where the time goes:
time: 123 us; the launch traced here: 121 us
  starting transfers between devices  51.2 us (42%)
  Pallas kernels  28.5 us (23%)
  waiting for transfers between devices  26.5 us (22%)
  local copies, waits for them, and re-layouts  12 us (10%)
  between operations  1.65 us (1%)
  other arithmetic  1.6 us (1%)
    ppermute x3, starting transfers between devices, summed(): lax.ppermute(total, axis, hop(s, 1))  23.5 us
    pallas_call x2, Pallas kernels, project(): pl.pallas_call(functools.partial(project_kernel, size, width, bounds, sta...  21.3 us
    ppermute x3, starting transfers between devices, summed(): lax.ppermute(lax.dynamic_index_in_dim(parts, spot ^ s, 0, False), axis, h...  15.4 us
    ppermute x4, starting transfers between devices, passed_along(): return lax.ppermute(x, axis, pairs)  11 us
    ppermute x3, waiting for transfers between devices, summed(): lax.ppermute(lax.dynamic_index_in_dim(parts, spot ^ s, 0, False), axis, h...  6.37 us
    ppermute x3, waiting for transfers between devices, summed(): lax.ppermute(total, axis, hop(s, 1))  5.96 us
    ppermute x1, waiting for transfers between devices, summed(): total = total + lax.ppermute(sent, axis, hop(s, near)).astype(F32)  5.56 us
    unnamed x33, local copies, waits for them, and re-layouts  5.38 us
  transfers between devices with their start and end apart: 16, of which 12 were waited for; matrix products, arithmetic and copies ran while one was open for 7% of the time, Pallas kernels for 8%

commit v1 on v0

--- a/solution.py
+++ b/solution.py
@@ -13,7 +13,8 @@
 F32 = jnp.float32
 BF16 = jnp.bfloat16
 LANES = 128
-VMEM_BYTES = 56 * 2**20
+VMEM_BYTES = 36 * 2**20
+VMEM_SMALL = 20 * 2**20
 
 
 def dft_tables(size):
@@ -42,6 +43,14 @@
     return (code // 4).astype(F32) * 0.25, (code % 4).astype(F32) * 0.25
 
 
+def in_stage(places, slot, bounds, stage, size):
+    end = places[1, slot] + size + 1
+    here = end <= bounds[stage + 1]
+    if stage > 0:
+        here = jnp.logical_and(here, end > bounds[stage])
+    return jnp.logical_and(slot < places[3, 0], here)
+
+
 def project_kernel(size, width, bounds, stage, places, *refs):
     first_stage, last_stage = stage == 0, stage == len(bounds) - 2
     refs = list(refs)
@@ -51,21 +60,21 @@
     probe_in, measured_in, tables_in = refs[:3]
     refs = refs[3:]
     if not first_stage:
-        moved_in, sums_in, border_in = refs[:3]
-        refs = refs[3:]
-    moved, own_part, below = refs[:3]
-    refs = refs[3:]
+        moved_in, sums_in = refs[:2]
+        refs = refs[2:]
+    moved, grads = refs[:2]
+    refs = refs[2:]
     if last_stage:
         keep, give = refs[:2]
+        refs = refs[2:]
     else:
-        sums_out, border_out = refs[:2]
-    refs = refs[2:]
-    cells, mixed, patch, folded, half_u, half_v, far, error, back, probe, measured, tables, probe_acc = refs[:13]
-    held, total, below_wide, sems = refs[13:17]
+        sums_out = refs.pop(0)
+    cells, mixed, patch, folded, half_u, half_v, far, error, back, probe, measured, tables, probe_acc, held = refs[:14]
+    sems, slot_sems = refs[14:16]
     if last_stage and not first_stage:
-        sums, given = refs[17:]
+        sums, given = refs[16:]
     elif last_stage:
-        given = refs[17]
+        given = refs[16]
     even, odd, even_t, odd_t, order, order_t = [tables.at[i] for i in range(6)]
     half = size // 2
     modes = probe.shape[0]
@@ -74,7 +83,6 @@
     low, high = bounds[stage], bounds[stage + 1]
     base = 0 if first_stage else low - size
     extent = high - base
-    settled = extent if last_stage else extent - size
     count = places[3, 0]
     copies = []
 
@@ -100,12 +108,6 @@
     load(tables_in, tables)
     load(probe_in, probe)
     load(measured_in, measured)
-    if not first_stage:
-        for part in range(2):
-            load(
-                border_in.at[:, pl.ds(part * size, size)],
-                total.at[pl.ds(0, rows + size), pl.ds(part * extent, size)],
-            )
     n_later = len(copies)
     if not first_stage:
         load(sums_in, sums if last_stage else probe_acc)
@@ -113,9 +115,6 @@
         copy.start()
     if last_stage or first_stage:
         probe_acc[...] = jnp.zeros_like(probe_acc)
-    for part in range(2):
-        fresh = slice(part * extent + (0 if first_stage else size), (part + 1) * extent)
-        total[:, fresh] = jnp.zeros((total.shape[0], fresh.stop - fresh.start), F32)
     cells[rows + size :] = jnp.zeros((cells.shape[0] - rows - size, cells.shape[1]), BF16)
     for slot in range(slots):
         for axis in range(2):
@@ -128,8 +127,10 @@
             copy.wait()
 
     def mine(slot):
-        end = places[1, slot] + size + 1
-        return jnp.logical_and(slot < count, jnp.logical_and(end > low if not first_stage else True, end <= high))
+        return in_stage(places, slot, bounds, stage, size)
+
+    def sent_out(slot):
+        return pltpu.make_async_copy(held.at[slot], grads.at[slot], slot_sems.at[slot])
 
     first_slot = jnp.int32(slots)
     for slot in reversed(range(slots)):
@@ -258,8 +259,8 @@
                         gimag += preal * uimag - pimag * ureal
                         probe_acc[mode, at, re] += oreal * ureal + oimag * uimag
                         probe_acc[mode, at, im] += oreal * uimag - oimag * ureal
-                    held[at, re] = greal.astype(BF16)
-                    held[at, im] = gimag.astype(BF16)
+                    held[slot, at, re] = greal.astype(BF16)
+                    held[slot, at, im] = gimag.astype(BF16)
                     for part, grad in enumerate((greal, gimag)):
                         cols = slice(h * size, h * size + LANES)
                         total_y += grad * (mixed[part, below, cols] - mixed[part, at, cols])
@@ -268,20 +269,7 @@
         moved[0, slot] = jnp.sum(total_y) / size
         moved[1, slot] = jnp.sum(total_x) / size
 
-        source = lax.broadcasted_iota(jnp.int32, (size, size + LANES), 0) + across
-        target = lax.broadcasted_iota(jnp.int32, (size, size + LANES), 1)
-        along = jnp.where(source == target, 1.0 - frac_x, 0.0) + jnp.where(source + 1 == target, frac_x, 0.0)
-        along = along.astype(BF16)
-        spread = size + 16
-        row8 = pl.multiple_of((top // 8) * 8, 8)
-        source = lax.broadcasted_iota(jnp.int32, (spread, size), 1) + (top - row8)
-        target = lax.broadcasted_iota(jnp.int32, (spread, size), 0)
-        drop = jnp.where(source == target, 1.0 - frac_y, 0.0) + jnp.where(source + 1 == target, frac_y, 0.0)
-        drop = drop.astype(BF16)
-        for part in range(2):
-            wide = dot(held[:, part * size : (part + 1) * size], along).astype(BF16)
-            start = pl.multiple_of(col0 + part * extent, LANES)
-            total[pl.ds(row8, spread), pl.ds(start, size + LANES)] += dot(drop, wide)
+        sent_out(slot).start()
 
     @pl.loop(0, slots)
     def _(slot):
@@ -295,35 +283,25 @@
         outs[-1].start()
 
     if last_stage:
-        core = places[4, 0]
-        share = modes // 2
-        give_from = (1 - core) * share
-        keep_from = core * share
         if first_stage:
-            given[...] = probe_acc[pl.ds(give_from, share)].astype(BF16)
+            given[...] = probe_acc[...].astype(BF16)
+            store(given, give)
         else:
             copies[-1].wait()
-            given[...] = (probe_acc[pl.ds(give_from, share)] + sums[pl.ds(give_from, share)]).astype(BF16)
-        store(given, give)
-        if not first_stage:
-            probe_acc[pl.ds(keep_from, share)] += sums[pl.ds(keep_from, share)]
-        store(probe_acc.at[pl.ds(keep_from, share)], keep)
+            for mode in range(modes):
+                probe_acc[mode] += sums[mode]
+                given[mode] = probe_acc[mode].astype(BF16)
+            store(given, give)
+        store(probe_acc, keep)
     else:
         store(probe_acc, sums_out)
-        for part in range(2):
-            store(
-                total.at[pl.ds(0, rows + size), pl.ds(part * extent + settled, size)],
-                border_out.at[:, pl.ds(part * size, size)],
-            )
-    for part in range(2):
-        here = slice(part * extent, part * extent + settled)
-        below_wide[:, part * settled : (part + 1) * settled] = total[rows : rows + size, here].astype(BF16)
-    store(below_wide, below)
-    for part in range(2):
-        store(
-            total.at[pl.ds(0, rows), pl.ds(part * extent, settled)],
-            own_part.at[:, pl.ds(part * settled, settled)],
-        )
+
+    @pl.loop(0, slots)
+    def _(slot):
+        @pl.when(mine(slot))
+        def _():
+            sent_out(slot).wait()
+
     for out in outs:
         out.wait()
 
@@ -337,22 +315,18 @@
     first_stage, last_stage = stage == 0, stage == len(bounds) - 2
     low, high = bounds[stage], bounds[stage + 1]
     extent = high - (0 if first_stage else low - size)
-    settled = extent if last_stage else extent - size
     inputs = [places, own, rims[stage]] + ([] if first_stage else [rims[stage - 1]]) + [probe, measured, tables]
     specs = [smem] + [hbm] * (len(inputs) - 1)
     outs = [
         jax.ShapeDtypeStruct((2, slots), F32),
-        jax.ShapeDtypeStruct((rows, 2 * settled), F32),
-        jax.ShapeDtypeStruct((size, 2 * settled), BF16),
+        jax.ShapeDtypeStruct((slots, size, 2 * size), BF16),
+        jax.ShapeDtypeStruct(probe.shape, F32),
     ]
-    share = (modes // 2,) + probe.shape[1:]
     if not first_stage:
         inputs += list(carried)
-        specs += [smem, hbm, hbm]
+        specs += [smem, hbm]
     if last_stage:
-        outs += [jax.ShapeDtypeStruct(share, F32), jax.ShapeDtypeStruct(share, BF16)]
-    else:
-        outs += [jax.ShapeDtypeStruct(probe.shape, F32), jax.ShapeDtypeStruct((rows + size, 2 * size), F32)]
+        outs += [jax.ShapeDtypeStruct(probe.shape, BF16)]
     scratch = [
         pltpu.VMEM((rows + size + 32, 2 * extent), BF16),
         pltpu.VMEM((2, size + 16, 2 * size), F32),
@@ -367,15 +341,14 @@
         pltpu.VMEM(measured.shape, BF16),
         pltpu.VMEM(tables.shape, BF16),
         pltpu.VMEM(probe.shape, F32),
-        pltpu.VMEM((size, 2 * size), BF16),
-        pltpu.VMEM((rows + size + 16, 2 * extent), F32),
-        pltpu.VMEM((size, 2 * settled), BF16),
+        pltpu.VMEM((slots, size, 2 * size), BF16),
         pltpu.SemaphoreType.DMA((12,)),
+        pltpu.SemaphoreType.DMA((slots,)),
     ]
     if last_stage and not first_stage:
         scratch.append(pltpu.VMEM(probe.shape, F32))
     if last_stage:
-        scratch.append(pltpu.VMEM(share, BF16))
+        scratch.append(pltpu.VMEM(probe.shape, BF16))
     return pl.pallas_call(
         functools.partial(project_kernel, size, width, bounds, stage),
         in_specs=specs,
@@ -388,49 +361,137 @@
     )(*inputs)
 
 
-def finish_kernel(lows, highs, n, *refs):
-    owns, aboves = refs[:n], refs[n : 2 * n]
-    out, wides, adds, sems = refs[-3 - 2 * n], refs[-2 - 2 * n : -2 - n], refs[-2 - n : -2], refs[-2:]
-    outs = []
-    loads = []
+def settle_kernel(size, bounds, low, high, shift, places, *refs):
+    grads = refs[: len(refs) - 5]
+    out, total, held, sems, out_sems = refs[len(refs) - 5 :]
+    slots = held.shape[0]
+    reach = size + LANES
+    base = max(low - size, 0)
+    extent = total.shape[1] // 2
+    length = high - low
+
+    def taken(stage, slot):
+        left = places[1, slot]
+        within = jnp.logical_and(left < high, left + size + 1 > low)
+        return jnp.logical_and(within, in_stage(places, slot, bounds, stage, size))
+
+    def fetch(stage, slot):
+        return pltpu.make_async_copy(grads[stage].at[slot], held.at[slot], sems.at[slot])
+
+    for stage in range(len(grads)):
+
+        @pl.loop(0, slots)
+        def _(slot, stage=stage):
+            @pl.when(taken(stage, slot))
+            def _():
+                fetch(stage, slot).start()
+
+    total[...] = jnp.zeros_like(total)
+
+    def one_slot(stage, slot):
+        left = places[1, slot]
+        frac_y, frac_x = fractions(places[2, slot])
+        col0 = (left // LANES) * LANES
+        ahead = lax.broadcasted_iota(jnp.int32, (size, reach), 1) - lax.broadcasted_iota(jnp.int32, (size, reach), 0)
+        ahead = ahead - (left - col0)
+        along = jnp.where(ahead == 0, 1.0 - frac_x, jnp.where(ahead == 1, frac_x, 0.0)).astype(BF16)
+        ahead = lax.broadcasted_iota(jnp.int32, (size, size), 0) - lax.broadcasted_iota(jnp.int32, (size, size), 1)
+        ahead = ahead - (places[0, slot] - shift)
+        down = jnp.where(ahead == 0, 1.0 - frac_y, jnp.where(ahead == 1, frac_y, 0.0)).astype(BF16)
+        fetch(stage, slot).wait()
+        for part in range(2):
+            wide = dot(held[slot, :, part * size : (part + 1) * size], along).astype(BF16)
+            start = pl.multiple_of(col0 - base + part * extent, LANES)
+            total[:, pl.ds(start, reach)] += dot(down, wide)
+
+    for stage in range(len(grads)):
+
+        @pl.loop(0, slots)
+        def _(slot, stage=stage):
+            pl.when(taken(stage, slot))(functools.partial(one_slot, stage, slot))
+
+    copies = []
+    for part in range(2):
+        here = slice(part * extent + low - base, part * extent + low - base + length)
+        there = slice(part * length, (part + 1) * length)
+        if out.dtype == F32:
+            copies.append(
+                pltpu.make_async_copy(
+                    total.at[:, pl.ds(here.start, length)], out.at[:, pl.ds(there.start, length)], out_sems.at[part]
+                )
+            )
+            copies[-1].start()
+        else:
+            out[:, there] = total[:, here].astype(out.dtype)
+    for copy in copies:
+        copy.wait()
+
+
+def settle(places, grads, bounds, low, high, shift, dtype, width, name):
+    slots, size, _ = grads[0].shape
+    base, end = max(low - size, 0), min(high + size, width)
+    hbm = pl.BlockSpec(memory_space=pl.ANY)
+    return pl.pallas_call(
+        functools.partial(settle_kernel, size, bounds, low, high, shift),
+        in_specs=[pl.BlockSpec(memory_space=pltpu.SMEM)] + [hbm] * len(grads),
+        out_specs=hbm if dtype == F32 else pl.BlockSpec(memory_space=pltpu.VMEM),
+        out_shape=jax.ShapeDtypeStruct((size, 2 * (high - low)), dtype),
+        scratch_shapes=[
+            pltpu.VMEM((size, 2 * (end - base)), F32),
+            pltpu.VMEM(grads[0].shape, BF16),
+            pltpu.SemaphoreType.DMA((slots,)),
+            pltpu.SemaphoreType.DMA((2,)),
+        ],
+        compiler_params=pltpu.CompilerParams(vmem_limit_bytes=VMEM_SMALL),
+        cost_estimate=pl.CostEstimate(flops=10**9, bytes_accessed=8 * 2**20, transcendentals=0),
+        name=name,
+    )(places, *grads)
+
+
+def finish_kernel(edges, n, own, *refs):
+    aboves, out = refs[:n], refs[n]
+    wides, adds, sems = refs[n + 1 : 2 * n + 1], refs[2 * n + 1 : 3 * n + 1], refs[3 * n + 1]
+    width = out.shape[2]
+    loads, outs = [], []
+
+    def copied(source, target, to):
+        to.append(pltpu.make_async_copy(source, target, sems.at[len(loads) + len(outs)]))
+        to[-1].start()
+
     for i in range(n):
-        loads.append(pltpu.make_async_copy(owns[i], wides[i], sems[0].at[2 * i]))
-        loads.append(pltpu.make_async_copy(aboves[i], adds[i], sems[0].at[2 * i + 1]))
-    for copy in loads:
-        copy.start()
+        length = edges[i + 1] - edges[i]
+        for part in range(2):
+            copied(
+                own.at[:, pl.ds(part * width + edges[i], length)], wides[i].at[:, pl.ds(part * length, length)], loads
+            )
+        copied(aboves[i], adds[i], loads)
     for i in range(n):
-        loads[2 * i].wait()
-        loads[2 * i + 1].wait()
-        length = highs[i] - lows[i]
+        for copy in loads[3 * i : 3 * i + 3]:
+            copy.wait()
+        length = edges[i + 1] - edges[i]
         for part in range(2):
             cols = slice(part * length, (part + 1) * length)
             wides[i][:, cols] += adds[i][:, cols].astype(F32)
-            copy = pltpu.make_async_copy(
-                wides[i].at[:, pl.ds(part * length, length)],
-                out.at[:, part, pl.ds(lows[i], length)],
-                sems[1].at[2 * i + part],
-            )
-            copy.start()
-            outs.append(copy)
+            copied(wides[i].at[:, pl.ds(part * length, length)], out.at[:, part, pl.ds(edges[i], length)], outs)
     for copy in outs:
         copy.wait()
 
 
-def finish(owns, aboves, lows, highs, width):
-    n = len(owns)
+def finish(own, aboves, edges, width):
+    n = len(aboves)
     hbm = pl.BlockSpec(memory_space=pl.ANY)
-    rows = owns[0].shape[0]
     return pl.pallas_call(
-        functools.partial(finish_kernel, lows, highs, n),
-        in_specs=[hbm] * (2 * n),
+        functools.partial(finish_kernel, edges, n),
+        in_specs=[hbm] * (n + 1),
         out_specs=hbm,
-        out_shape=jax.ShapeDtypeStruct((rows, 2, width), F32),
-        scratch_shapes=[pltpu.VMEM(x.shape, F32) for x in owns]
+        out_shape=jax.ShapeDtypeStruct((own.shape[0], 2, width), F32),
+        scratch_shapes=[pltpu.VMEM(x.shape, F32) for x in aboves]
         + [pltpu.VMEM(x.shape, BF16) for x in aboves]
-        + [pltpu.SemaphoreType.DMA((2 * n,)), pltpu.SemaphoreType.DMA((2 * n,))],
-        compiler_params=pltpu.CompilerParams(vmem_limit_bytes=VMEM_BYTES),
+        + [pltpu.SemaphoreType.DMA((5 * n,))],
+        compiler_params=pltpu.CompilerParams(vmem_limit_bytes=VMEM_SMALL),
+        cost_estimate=pl.CostEstimate(flops=10**6, bytes_accessed=10 * 2**20, transcendentals=0),
         name="finish",
-    )(*owns, *aboves)
+    )(own, *aboves)
 
 
 def passed_along(x, axis, by):
@@ -440,85 +501,100 @@
 
 
 def unpack_kernel(order, *refs):
-    pieces, out, wide, sems = refs[:-3], refs[-3], refs[-2], refs[-1]
-    rows = pieces[0].shape[0]
-    modes, size, _, _ = out.shape
+    n = (len(refs) - 4) // 2
+    out, wide, narrow, sems = refs[2 * n :]
+    rows = wide.shape[1]
+    size = out.shape[1]
+    span = min(rows, size)
+    for core in range(2):
+
+        @pl.when(order[n] == core)
+        def _():
+            for i in range(n):
+                pltpu.make_async_copy(refs[core * n + i], narrow.at[i], sems.at[0, i]).start()
+
     copies = []
-    for i, piece in enumerate(pieces):
-        wide[i * rows : (i + 1) * rows] = piece[...].astype(F32)
-        mode = order[i] // (size // rows)
-        at = pl.multiple_of(order[i] % (size // rows) * rows, 8)
-        for part in range(2):
-            copy = pltpu.make_async_copy(
-                wide.at[pl.ds(i * rows, rows), pl.ds(part * size, size)],
-                out.at[mode, pl.ds(at, rows), part, :],
-                sems.at[2 * i + part],
-            )
-            copy.start()
-            copies.append(copy)
+    for i in range(n):
+        pltpu.make_async_copy(refs[i], narrow.at[i], sems.at[0, i]).wait()
+        wide[i] = narrow[i].astype(F32)
+        for j in range(rows // span):
+            line = order[i] * rows + j * span
+            mode = line // size
+            at = pl.multiple_of(line % size, 8)
+            for part in range(2):
+                copies.append(
+                    pltpu.make_async_copy(
+                        wide.at[i, pl.ds(j * span, span), pl.ds(part * size, size)],
+                        out.at[mode, pl.ds(at, span), part, :],
+                        sems.at[1, len(copies)],
+                    )
+                )
+                copies[-1].start()
     for copy in copies:
         copy.wait()
 
 
-def unpacked(pieces, order, shape):
-    vmem = pl.BlockSpec(memory_space=pltpu.VMEM)
-    smem = pl.BlockSpec(memory_space=pltpu.SMEM)
+def unpacked(pieces, others, order, shape):
+    n = len(pieces)
+    rows, columns = pieces[0].shape
+    hbm = pl.BlockSpec(memory_space=pl.ANY)
     return pl.pallas_call(
         unpack_kernel,
-        in_specs=[smem] + [vmem] * len(pieces),
-        out_specs=pl.BlockSpec(memory_space=pl.ANY),
+        in_specs=[pl.BlockSpec(memory_space=pltpu.SMEM)] + [hbm] * (2 * n),
+        out_specs=hbm,
         out_shape=jax.ShapeDtypeStruct(shape, F32),
         scratch_shapes=[
-            pltpu.VMEM((len(pieces) * pieces[0].shape[0], pieces[0].shape[1]), F32),
-            pltpu.SemaphoreType.DMA((2 * len(pieces),)),
+            pltpu.VMEM((n, rows, columns), F32),
+            pltpu.VMEM((n, rows, columns), BF16),
+            pltpu.SemaphoreType.DMA((2, 2 * n * max(1, rows // shape[1]))),
         ],
-        compiler_params=pltpu.CompilerParams(vmem_limit_bytes=VMEM_BYTES),
+        compiler_params=pltpu.CompilerParams(vmem_limit_bytes=VMEM_SMALL),
+        cost_estimate=pl.CostEstimate(flops=10**6, bytes_accessed=4 * 2**20, transcendentals=0),
         name="unpack",
-    )(order, *pieces)
+    )(order, *pieces, *others)
+
+
+def near_chips(axis):
+    return min(4, lax.axis_size(axis) // 2)
 
 
 def piece_order(axis):
-    length = lax.axis_size(axis)
-    near = min(4, length // 2)
+    near = near_chips(axis)
     me = lax.axis_index(axis)
     core, spot = me % 2, me // 2 % near
-    return jnp.stack(
-        [core * near + (spot ^ s) for s in range(near)] + [(1 - core) * near + (spot ^ s) for s in range(near)]
-    )
-
-
-def summed(keep, give, axis, shape, order, late):
+    return jnp.stack([spot ^ s for s in range(near)] + [core])
+
+
+def hop(axis, shift, stride):
+    return [(i, i ^ (2 * stride * shift)) for i in range(0, lax.axis_size(axis), 2)]
+
+
+def summed(keep, give, axis, shape, order, first, between, after):
     length = lax.axis_size(axis)
-    chips = length // 2
-    near = min(4, chips)
-    far = chips // near
-    me = lax.axis_index(axis)
-    core, chip = me % 2, me // 2
-    across = [(i, i ^ 1) for i in range(length)]
-
-    def hop(shift, stride):
-        return [(i, i ^ (2 * stride * shift)) for i in range(length)]
-
-    size, columns = keep.shape[1:]
-    mine = keep + lax.ppermute(give, axis, across).astype(F32)
-    rows = mine.shape[0] * size // near
-    mine = mine.reshape(near, rows, columns)
+    near = near_chips(axis)
+    far = length // 2 // near
+    inward = [(i + 1, i) for i in range(0, length, 2)]
+    outward = [(i, i + 1) for i in range(0, length, 2)]
+    modes, size, columns = keep.shape
+    spot = lax.axis_index(axis) // 2 % near
+    mine = keep + lax.ppermute(give, axis, inward).astype(F32)
+    mine = first(mine)
+    mine = mine.reshape(near, modes * size // near, columns)
     parts = mine.astype(BF16)
-    spot = chip % near
     got = [
-        lax.ppermute(lax.dynamic_index_in_dim(parts, spot ^ s, 0, False), axis, hop(s, 1)) for s in range(1, near)
+        lax.ppermute(lax.dynamic_index_in_dim(parts, spot ^ s, 0, False), axis, hop(axis, s, 1)) for s in range(1, near)
     ]
     total = lax.dynamic_index_in_dim(mine, spot, 0, False)
     for piece in got:
         total = total + piece.astype(F32)
+    total = between(total)
     sent = total.astype(BF16)
-    sent, late = lax.optimization_barrier((sent, late))
     for s in range(1, far):
-        total = total + lax.ppermute(sent, axis, hop(s, near)).astype(F32)
-    total = total.astype(BF16)
-    pieces = [total] + [lax.ppermute(total, axis, hop(s, 1)) for s in range(1, near)]
-    others = [lax.ppermute(piece, axis, across) for piece in pieces]
-    return unpacked(pieces + others, order, shape), late
+        total = total + lax.ppermute(sent, axis, hop(axis, s, near)).astype(F32)
+    total = after(total.astype(BF16))
+    pieces = [total] + [lax.ppermute(total, axis, hop(axis, s, 1)) for s in range(1, near)]
+    others = [lax.ppermute(piece, axis, outward) for piece in pieces]
+    return unpacked(pieces, others, order, shape)
 
 
 def column_bounds(width, shares):
@@ -543,20 +619,27 @@
     own = object_tiles.reshape(rows, 2 * width)
     flat = probe.reshape(modes, size, 2 * size)
     carried = None
-    owns, belows = [], []
+    grads, aboves = [], []
+    edges = [0] + [bound - size for bound in bounds[1:-1]] + [width]
     for stage in range(stages):
-        moved, own_part, below, *rest = project(
-            stage, bounds, places, own, rims, flat, measured, tables, width, carried
-        )
+        moved, grad, *rest = project(stage, bounds, places, own, rims, flat, measured, tables, width, carried)
+        grads.append(grad)
         carried = [moved] + rest
-        owns.append(own_part)
-        belows.append(below)
+        below = settle(places, grads, bounds, edges[stage], edges[stage + 1], size, BF16, width, f"below_{stage}")
+        if stage < stages - 1:
+            places, below = lax.optimization_barrier((places, below))
+        aboves.append(passed_along(below, "row", 1))
     _, keep, give = carried
-    edges = [0] + [bound - size for bound in bounds[1:-1]] + [width]
-    aboves = [passed_along(below, "row", 1) for below in belows[:-1]]
-    probe_grad, late = summed(keep, give, "row", probe.shape, order, belows[-1])
-    aboves.append(passed_along(late, "row", 1))
-    object_grad = finish(owns, aboves, edges[:-1], edges[1:], width)
+    give, aboves[0] = lax.optimization_barrier((give, aboves[0]))
+    held = {}
+
+    def between(x):
+        own_rows = settle(places, grads, bounds, 0, width, 0, F32, width, "own_rows")
+        x, held["own"] = lax.optimization_barrier((x, own_rows))
+        return x
+
+    probe_grad = summed(keep, give, "row", probe.shape, order, lambda x: x, between, lambda x: x)
+    object_grad = finish(held["own"], aboves, edges, width)
     return object_grad, probe_grad, moved
 
 

time: 123 us -> 128 us (1.041)
  Pallas kernels: 28.5 us -> 50.4 us
  starting transfers between devices: 51.2 us -> 36.3 us
  waiting for transfers between devices: 26.5 us -> 18.8 us
  other arithmetic: 1.6 us -> 5.2 us
    pallas_call x2 -> x5, Pallas kernels: 7.23 us -> 21.9 us  [the longest x3 16.8 us: settle(): pl.pallas_call(functools.partial(settle_kernel, size, bounds, low, high,...]
    pallas_call x2, Pallas kernels: 21.3 us -> 28.5 us  [project(): pl.pallas_call(functools.partial(project_kernel, size, width, bounds, sta...]
    ppermute x9, starting transfers between devices: 24.8 us -> 17.8 us  [the longest x3 9.21 us: summed(): lax.ppermute(total, axis, hop(axis, s, 1))]
    ppermute x3, waiting for transfers between devices: 6.37 us -> 0.01 us  [summed(): lax.ppermute(lax.dynamic_index_in_dim(parts, spot ^ s, 0, False), axis, h...]
    ppermute x3, starting transfers between devices: 15.4 us -> 9.2 us  [summed(): lax.ppermute(lax.dynamic_index_in_dim(parts, spot ^ s, 0, False), axis, h...]
    ppermute x9, waiting for transfers between devices: 14.9 us -> 11 us  [the longest x1 7.24 us: summed(): total = total + lax.ppermute(sent, axis, hop(axis, s, near)).astype(F32)]
    convert_element_type x1, other arithmetic: 0.07 us -> 3.6 us  [summed(): parts = mine.astype(BF16)]
    ppermute x4, waiting for transfers between devices: 5.15 us -> 7.77 us  [passed_along(): return lax.ppermute(x, axis, pairs)]
  transfers between devices with their start and end apart: 16 -> 16, of which waited for: 12 -> 5; matrix products, arithmetic and copies ran while one was open for 7% -> 7% of each run, Pallas kernels for 8% -> 38%
where the time goes in v1:
time: 128 us; the launch traced here: 126 us
  Pallas kernels  50.4 us (39%)
  starting transfers between devices  36.3 us (28%)
  waiting for transfers between devices  18.8 us (15%)
  local copies, waits for them, and re-layouts  13.2 us (10%)
  other arithmetic  5.2 us (4%)
  between operations  1.89 us (1%)
    pallas_call x2, Pallas kernels, project(): pl.pallas_call(functools.partial(project_kernel, size, width, bounds, sta...  28.5 us
    pallas_call x3, Pallas kernels, settle(): pl.pallas_call(functools.partial(settle_kernel, size, bounds, low, high,...  16.8 us
    ppermute x4, starting transfers between devices, passed_along(): return lax.ppermute(x, axis, pairs)  9.26 us
    ppermute x3, starting transfers between devices, summed(): lax.ppermute(total, axis, hop(axis, s, 1))  9.21 us
    ppermute x3, starting transfers between devices, summed(): lax.ppermute(lax.dynamic_index_in_dim(parts, spot ^ s, 0, False), axis, h...  9.2 us
    ppermute x4, waiting for transfers between devices, passed_along(): return lax.ppermute(x, axis, pairs)  7.77 us
    ppermute x1, waiting for transfers between devices, summed(): total = total + lax.ppermute(sent, axis, hop(axis, s, near)).astype(F32)  7.24 us
    unnamed x25, local copies, waits for them, and re-layouts  7.09 us
  transfers between devices with their start and end apart: 16, of which 5 were waited for; matrix products, arithmetic and copies ran while one was open for 7% of the time, Pallas kernels for 38%

profile of v1, /device:TPU:16, one launch (start us, length us, event | category | flops | bytes accessed | tf_op | source)
XLA Modules:
  0.0 125.7 jit_solution(5704964279390740882)
XLA Ops:
  3.1 2.8 %collective-permute-start = (bf16[256,2304]{1,0:T(8,128)(2,1)}, bf16[256,2304]{1,0:T(8,128)(2,1)S(1)}, u32[]{:S(2)}, u32[]{:S(2)}) collective-permute-start(bf16[256,2304]{1,0:T(8,128)(2,1)} %bitcast.16), channel_id=1, source_target_pairs={{1,0},{2,1},{3,2},{4,3},{5,4},{6,5},{7,6},{8,7},{9,8},{10,9},{11,1... | collective-permute-start | bytes 3538952 | tf_op jit(solution)/shard_map/ppermute | solution.py:500
  7.0 2.6 %collective-permute-start.1 = (bf16[256,1792]{1,0:T(8,128)(2,1)}, bf16[256,1792]{1,0:T(8,128)(2,1)}, u32[]{:S(2)}, u32[]{:S(2)}) collective-permute-start(bf16[256,1792]{1,0:T(8,128)(2,1)} %bitcast.18), channel_id=1, source_target_pairs={{1,0},{2,1},{3,2},{4,3},{5,4},{6,5},{7,6},{8,7},{9,8},{10,9},{11,1... | collective-permute-start | bytes 2752520 | tf_op jit(solution)/shard_map/ppermute | solution.py:500
  10.4 3.9 %reshape.23.refs_2_.refs_3_ = f32[4,256,512]{2,1,0:T(8,128)} reshape(f32[4,256,2,256]{3,2,1,0:T(2,128)} %param.9) | data formatting | bytes 4194304 | tf_op jit(solution)/shard_map/reshape | solution.py:620
  14.3 2.6 %copy.11 = bf16[32,8,2,2048]{3,1,2,0:T(8,128)(2,1)S(1)} copy(bf16[32,8,2,2048]{3,2,1,0:T(2,128)(2,1)} %bitcast.30) | data formatting | bytes 4194304
  16.9 3.0 %collective-permute-done.refs_1_.refs_2_ = bf16[256,2304]{1,0:T(8,128)(2,1)S(1)} collective-permute-done((bf16[256,2304]{1,0:T(8,128)(2,1)}, bf16[256,2304]{1,0:T(8,128)(2,1)S(1)}, u32[]{:S(2)}, u32[]{:S(2)}) %collective-permute-start) | collective-permute-done | bytes 1179680 | tf_op jit(solution)/shard_map/ppermute | solution.py:500
  19.9 20.9 %project_0.1 = (f32[2,6]{1,0:T(2,128)S(1)}, bf16[6,256,512]{2,1,0:T(8,128)(2,1)S(1)}, f32[4,256,512]{2,1,0:T(8,128)S(1)}) custom-call(s32[5,6]{1,0:T(8,128)S(1)} %stack.33.places, bf16[256,4096]{1,0:T(8,128)(2,1)S(1)} %bitcast.28, bf16[256,2304]{1,0:T(8,128)(2,1)S(1)} %collective-permute-done.refs_1_.refs_2_, f32[4,256,512]{2,1,0:T(8,128)S(1)} %copy-done.1, ...), custom_call_target="tpu_custom_call" | custom-call | flops 8000000000 | bytes 16777216 | tf_op jit(solution)/shard_map/project_0/pallas_call | solution.py:352
  40.9 5.5 %below_0.1 = bf16[256,1792]{1,0:T(8,128)(2,1)S(1)} custom-call(s32[5,6]{1,0:T(8,128)S(1)} %stack.33.places, bf16[6,256,512]{2,1,0:T(8,128)(2,1)S(1)} %get-tuple-element.19.refs_0_), custom_call_target="tpu_custom_call" | custom-call | flops 1000000000 | bytes 8388608 | tf_op jit(solution)/shard_map/below_0/pallas_call | solution.py:434
  46.5 1.9 %collective-permute-start.2 = (bf16[256,1792]{1,0:T(8,128)(2,1)S(1)}, bf16[256,1792]{1,0:T(8,128)(2,1)S(1)}, u32[]{:S(2)}, u32[]{:S(2)}) collective-permute-start(bf16[256,1792]{1,0:T(8,128)(2,1)S(1)} %below_0.1), channel_id=1, source_target_pairs={{0,1},{1,2},{2,3},{3,4},{4,5},{5,6},{6,7},{7,8},{8,9},{9,10},{10,1... | collective-permute-start | bytes 2752520 | tf_op jit(solution)/shard_map/ppermute | solution.py:500
  48.4 7.6 %project_1.1 = (f32[2,6]{1,0:T(2,128)}, bf16[6,256,512]{2,1,0:T(8,128)(2,1)S(1)}, f32[4,256,512]{2,1,0:T(8,128)S(1)}, bf16[4,256,512]{2,1,0:T(8,128)(2,1)}) custom-call(s32[5,6]{1,0:T(8,128)S(1)} %stack.33.places, bf16[256,4096]{1,0:T(8,128)(2,1)S(1)} %bitcast.29, bf16[256,1792]{1,0:T(8,128)(2,1)} %collective-permute-done.1.refs_1_, ...), custom_call_target="tpu_custom_call" | custom-call | flops 8000000000 | bytes 16777216 | tf_op jit(solution)/shard_map/project_1/pallas_call | solution.py:352
  56.0 1.3 %copy-done = f32[4,256,512]{2,1,0:T(8,128)} copy-done((f32[4,256,512]{2,1,0:T(8,128)}, f32[4,256,512]{2,1,0:T(8,128)S(1)}, u32[]{:S(2)}) %copy-start) | copy-done | bytes 2097176
  57.3 4.8 %collective-permute-done.2.refs_0_ = bf16[256,1792]{1,0:T(8,128)(2,1)S(1)} collective-permute-done((bf16[256,1792]{1,0:T(8,128)(2,1)S(1)}, bf16[256,1792]{1,0:T(8,128)(2,1)S(1)}, u32[]{:S(2)}, u32[]{:S(2)}) %collective-permute-start.2) | collective-permute-done | bytes 917536 | tf_op jit(solution)/shard_map/ppermute | solution.py:500
  63.0 1.5 %collective-permute-start.3 = (bf16[4,256,512]{2,1,0:T(8,128)(2,1)}, bf16[4,256,512]{2,1,0:T(8,128)(2,1)}, u32[]{:S(2)}, u32[]{:S(2)}) collective-permute-start(bf16[4,256,512]{2,1,0:T(8,128)(2,1)} %get-tuple-element.26), channel_id=1, source_target_pairs={{1,0},{3,2},{5,4},{7,6},{9,8},{11,10},{13,12},{15,14},{17,16},{19,... | collective-permute-start | bytes 3145736 | tf_op jit(solution)/shard_map/ppermute | solution.py:580
  64.5 3.4 %collective-permute-done.3 = bf16[4,256,512]{2,1,0:T(8,128)(2,1)} collective-permute-done((bf16[4,256,512]{2,1,0:T(8,128)(2,1)}, bf16[4,256,512]{2,1,0:T(8,128)(2,1)}, u32[]{:S(2)}, u32[]{:S(2)}) %collective-permute-start.3) | collective-permute-done | bytes 1048608 | tf_op jit(solution)/shard_map/ppermute | solution.py:580
  67.9 3.6 %fusion.2 = (bf16[4,256,512]{2,1,0:T(8,128)(2,1)S(1)}, f32[4,256,512]{2,1,0:T(8,128)}) fusion(f32[4,256,512]{2,1,0:T(8,128)} %copy-done, bf16[4,256,512]{2,1,0:T(8,128)(2,1)} %collective-permute-done.3), kind=kLoop, calls=%fused_computation.8 | loop fusion | flops 1572864 | bytes 6291456 | tf_op jit(solution)/shard_map/convert_element_type | solution.py:583
  72.3 1.9 %collective-permute-start.4 = (bf16[256,512]{1,0:T(8,128)(2,1)}, bf16[256,512]{1,0:T(8,128)(2,1)}, u32[]{:S(2)}, u32[]{:S(2)}) collective-permute-start(bf16[256,512]{1,0:T(8,128)(2,1)} %get-tuple-element.35), channel_id=1, source_target_pairs={{0,2},{2,0},{4,6},{6,4},{8,10},{10,8},{12,14},{14,12},{16,18},{18,... | collective-permute-start | bytes 786440 | tf_op jit(solution)/shard_map/ppermute | solution.py:585
  74.2 1.9 %collective-permute-start.6 = (bf16[256,512]{1,0:T(8,128)(2,1)}, bf16[256,512]{1,0:T(8,128)(2,1)}, u32[]{:S(2)}, u32[]{:S(2)}) collective-permute-start(bf16[256,512]{1,0:T(8,128)(2,1)} %get-tuple-element.36), channel_id=1, source_target_pairs={{0,6},{2,4},{4,2},{6,0},{8,14},{10,12},{12,10},{14,8},{16,22},{18,... | collective-permute-start | bytes 786440 | tf_op jit(solution)/shard_map/ppermute | solution.py:585
  76.1 5.4 %collective-permute-start.5 = (bf16[256,512]{1,0:T(8,128)(2,1)S(1)}, bf16[256,512]{1,0:T(8,128)(2,1)}, u32[]{:S(2)}, u32[]{:S(2)}) collective-permute-start(bf16[256,512]{1,0:T(8,128)(2,1)S(1)} %get-tuple-element.37), channel_id=1, source_target_pairs={{0,4},{2,6},{4,0},{6,2},{8,12},{10,14},{12,8},{14,10},{16,20},{18,... | collective-permute-start | bytes 786440 | tf_op jit(solution)/shard_map/ppermute | solution.py:585
  81.5 4.1 %below_1.1 = bf16[256,2304]{1,0:T(8,128)(2,1)S(1)} custom-call(s32[5,6]{1,0:T(8,128)S(1)} %stack.33.places, bf16[6,256,512]{2,1,0:T(8,128)(2,1)S(1)} %get-tuple-element.19.refs_0_, bf16[6,256,512]{2,1,0:T(8,128)(2,1)S(1)} %get-tuple-element.27.refs_1_), custom_call_target="tpu_custom_call" | custom-call | flops 1000000000 | bytes 8388608 | tf_op jit(solution)/shard_map/below_1/pallas_call | solution.py:434
  85.6 1.9 %collective-permute-start.7 = (bf16[256,2304]{1,0:T(8,128)(2,1)S(1)}, bf16[256,2304]{1,0:T(8,128)(2,1)S(1)}, u32[]{:S(2)}, u32[]{:S(2)}) collective-permute-start(bf16[256,2304]{1,0:T(8,128)(2,1)S(1)} %below_1.1), channel_id=1, source_target_pairs={{0,1},{1,2},{2,3},{3,4},{4,5},{5,6},{6,7},{7,8},{8,9},{9,10},{10,1... | collective-permute-start | bytes 3538952 | tf_op jit(solution)/shard_map/ppermute | solution.py:500
  87.5 7.1 %own_rows.1.own = f32[256,4096]{1,0:T(8,128)S(1)} custom-call(s32[5,6]{1,0:T(8,128)S(1)} %stack.33.places, bf16[6,256,512]{2,1,0:T(8,128)(2,1)S(1)} %get-tuple-element.19.refs_0_, bf16[6,256,512]{2,1,0:T(8,128)(2,1)S(1)} %get-tuple-element.27.refs_1_), custom_call_target="tpu_custom_call" | custom-call | flops 1000000000 | bytes 8388608 | tf_op jit(solution)/shard_map/own_rows/pallas_call | solution.py:434
  94.7 1.5 %fusion.1 = f32[256,512]{1,0:T(8,128)S(1)} fusion(bf16[256,512]{1,0:T(8,128)(2,1)} %collective-permute-done.6, bf16[256,512]{1,0:T(8,128)(2,1)} %collective-permute-done.5, bf16[256,512]{1,0:T(8,128)(2,1)} %collective-permute-done.4, f32[4,256,512]{2,1,0:T(8,128)} %get-tuple-element.34, s32[]{:T(128)S(6)} %select_n.37), kind=kLoop, calls=%fused_computation.3 | loop fusion | flops 786432 | bytes 1835012 | tf_op jit(solution)/shard_map/add | solution.py:589
  96.3 1.9 %collective-permute-start.8 = (bf16[256,512]{1,0:T(8,128)(2,1)S(1)}, bf16[256,512]{1,0:T(8,128)(2,1)S(1)}, u32[]{:S(2)}, u32[]{:S(2)}) collective-permute-start(bf16[256,512]{1,0:T(8,128)(2,1)S(1)} %convert_element_type.29), channel_id=1, source_target_pairs={{0,8},{2,10},{4,12},{6,14},{8,0},{10,2},{12,4},{14,6},{16,24},{18,... | collective-permute-start | bytes 786440 | tf_op jit(solution)/shard_map/ppermute | solution.py:593
  98.2 7.2 %collective-permute-done.8 = bf16[256,512]{1,0:T(8,128)(2,1)S(1)} collective-permute-done((bf16[256,512]{1,0:T(8,128)(2,1)S(1)}, bf16[256,512]{1,0:T(8,128)(2,1)S(1)}, u32[]{:S(2)}, u32[]{:S(2)}) %collective-permute-start.8) | collective-permute-done | bytes 262176 | tf_op jit(solution)/shard_map/ppermute | solution.py:593
  105.5 3.2 %collective-permute-start.11 = (bf16[256,512]{1,0:T(8,128)(2,1)S(1)}, bf16[256,512]{1,0:T(8,128)(2,1)S(1)}, u32[]{:S(2)}, u32[]{:S(2)}) collective-permute-start(bf16[256,512]{1,0:T(8,128)(2,1)S(1)} %add_convert_fusion.refs_0_), channel_id=1, source_target_pairs={{0,6},{2,4},{4,2},{6,0},{8,14},{10,12},{12,10},{14,8},{16,22},{18,... | collective-permute-start | bytes 786440 | tf_op jit(solution)/shard_map/ppermute | solution.py:595
  108.7 1.9 %collective-permute-start.10 = (bf16[256,512]{1,0:T(8,128)(2,1)S(1)}, bf16[256,512]{1,0:T(8,128)(2,1)S(1)}, u32[]{:S(2)}, u32[]{:S(2)}) collective-permute-start(bf16[256,512]{1,0:T(8,128)(2,1)S(1)} %add_convert_fusion.refs_0_), channel_id=1, source_target_pairs={{0,4},{2,6},{4,0},{6,2},{8,12},{10,14},{12,8},{14,10},{16,20},{18,... | collective-permute-start | bytes 786440 | tf_op jit(solution)/shard_map/ppermute | solution.py:595
  110.7 4.1 %collective-permute-start.9 = (bf16[256,512]{1,0:T(8,128)(2,1)S(1)}, bf16[256,512]{1,0:T(8,128)(2,1)S(1)}, u32[]{:S(2)}, u32[]{:S(2)}) collective-permute-start(bf16[256,512]{1,0:T(8,128)(2,1)S(1)} %add_convert_fusion.refs_0_), channel_id=1, source_target_pairs={{0,2},{2,0},{4,6},{6,4},{8,10},{10,8},{12,14},{14,12},{16,18},{18,... | collective-permute-start | bytes 786440 | tf_op jit(solution)/shard_map/ppermute | solution.py:595
  114.8 1.3 %collective-permute-start.12 = (bf16[256,512]{1,0:T(8,128)(2,1)S(1)}, bf16[256,512]{1,0:T(8,128)(2,1)S(1)}, u32[]{:S(2)}, u32[]{:S(2)}) collective-permute-start(bf16[256,512]{1,0:T(8,128)(2,1)S(1)} %add_convert_fusion.refs_0_), channel_id=1, source_target_pairs={{0,1},{2,3},{4,5},{6,7},{8,9},{10,11},{12,13},{14,15},{16,17},{18,... | collective-permute-start | bytes 786440 | tf_op jit(solution)/shard_map/ppermute | solution.py:596
  116.1 1.3 %collective-permute-start.15 = (bf16[256,512]{1,0:T(8,128)(2,1)S(1)}, bf16[256,512]{1,0:T(8,128)(2,1)S(1)}, u32[]{:S(2)}, u32[]{:S(2)}) collective-permute-start(bf16[256,512]{1,0:T(8,128)(2,1)S(1)} %collective-permute-done.11.refs_3_), channel_id=1, source_target_pairs={{0,1},{2,3},{4,5},{6,7},{8,9},{10,11},{12,13},{14,15},{16,17},{18,... | collective-permute-start | bytes 786440 | tf_op jit(solution)/shard_map/ppermute | solution.py:596
  117.4 1.3 %collective-permute-start.14 = (bf16[256,512]{1,0:T(8,128)(2,1)S(1)}, bf16[256,512]{1,0:T(8,128)(2,1)S(1)}, u32[]{:S(2)}, u32[]{:S(2)}) collective-permute-start(bf16[256,512]{1,0:T(8,128)(2,1)S(1)} %collective-permute-done.10.refs_2_), channel_id=1, source_target_pairs={{0,1},{2,3},{4,5},{6,7},{8,9},{10,11},{12,13},{14,15},{16,17},{18,... | collective-permute-start | bytes 786440 | tf_op jit(solution)/shard_map/ppermute | solution.py:596
  119.1 1.3 %collective-permute-start.13 = (bf16[256,512]{1,0:T(8,128)(2,1)S(1)}, bf16[256,512]{1,0:T(8,128)(2,1)S(1)}, u32[]{:S(2)}, u32[]{:S(2)}) collective-permute-start(bf16[256,512]{1,0:T(8,128)(2,1)S(1)} %collective-permute-done.9.refs_1_), channel_id=1, source_target_pairs={{0,1},{2,3},{4,5},{6,7},{8,9},{10,11},{12,13},{14,15},{16,17},{18,... | collective-permute-start | bytes 786440 | tf_op jit(solution)/shard_map/ppermute | solution.py:596
  120.4 3.0 %finish.1 = f32[256,2,2048]{2,1,0:T(2,128)} custom-call(f32[256,4096]{1,0:T(8,128)S(1)} %own_rows.1.own, bf16[256,1792]{1,0:T(8,128)(2,1)S(1)} %copy-done.3, bf16[256,2304]{1,0:T(8,128)(2,1)S(1)} %collective-permute-done.7.refs_1_), custom_call_target="tpu_custom_call" | custom-call | flops 1000000 | bytes 10485760 | tf_op jit(solution)/shard_map/finish/pallas_call | solution.py:483
  123.4 2.1 %unpack.1 = f32[4,256,2,256]{3,2,1,0:T(2,128)} custom-call(s32[5]{0:T(128)S(1)} %stack.39.order, bf16[256,512]{1,0:T(8,128)(2,1)S(1)} %add_convert_fusion.refs_0_, bf16[256,512]{1,0:T(8,128)(2,1)S(1)} %collective-permute-done.9.refs_1_, bf16[256,512]{1,0:T(8,128)(2,1)S(1)} %collective-permute-done.10.refs_2_, ...), custom_call_target="tpu_custom_call" | custom-call | flops 1000000 | bytes 4194304 | tf_op jit(solution)/shard_map/unpack/pallas_call | solution.py:541
  (46 shorter events, 5.9 us)
Async XLA Ops:
  0.6 1.3 %slice-start = ((bf16[256,2,2048]{2,1,0:T(2,128)(2,1)}), bf16[256,2,1152]{2,1,0:T(2,128)(2,1)S(1)}, s32[]{:S(2)}) async-start(bf16[256,2,2048]{2,1,0:T(2,128)(2,1)} %param.8), calls=%async_computation | async-start | bytes 2359296 | tf_op jit(solution)/shard_map/slice | solution.py:611
  1.9 4.0 %slice-start.1 = ((bf16[256,2,2048]{2,1,0:T(2,128)(2,1)}), bf16[256,2,896]{2,1,0:T(2,128)(2,1)S(1)}, s32[]{:S(2)}) async-start(bf16[256,2,2048]{2,1,0:T(2,128)(2,1)} %param.8), calls=%async_computation.1 | async-start | bytes 1835008 | tf_op jit(solution)/shard_map/slice | solution.py:611
  3.0 7.3 %copy-start.8 = (s32[6]{0:T(128)S(1)}, s32[6]{0:T(128)}, u32[]{:S(2)}) copy-start(s32[6]{0:T(128)} %param.11) | copy-start | bytes 76
  3.1 7.3 %copy-start.9 = (s32[6]{0:T(128)S(1)}, s32[6]{0:T(128)}, u32[]{:S(2)}) copy-start(s32[6]{0:T(128)} %param.12) | copy-start | bytes 76
  3.1 7.3 %copy-start.10 = (s32[6]{0:T(128)S(1)}, s32[6]{0:T(128)}, u32[]{:S(2)}) copy-start(s32[6]{0:T(128)} %param.13) | copy-start | bytes 76
  3.1 16.9 %collective-permute-start = (bf16[256,2304]{1,0:T(8,128)(2,1)}, bf16[256,2304]{1,0:T(8,128)(2,1)S(1)}, u32[]{:S(2)}, u32[]{:S(2)}) collective-permute-start(bf16[256,2304]{1,0:T(8,128)(2,1)} %bitcast.16), channel_id=1, source_target_pairs={{1,0},{2,1},{3,2},{4,3},{5,4},{6,5},{7,6},{8,7},{9,8},{10,9},{11,1... | collective-permute-start | bytes 3538952 | tf_op jit(solution)/shard_map/ppermute | solution.py:500
  7.0 41.4 %collective-permute-start.1 = (bf16[256,1792]{1,0:T(8,128)(2,1)}, bf16[256,1792]{1,0:T(8,128)(2,1)}, u32[]{:S(2)}, u32[]{:S(2)}) collective-permute-start(bf16[256,1792]{1,0:T(8,128)(2,1)} %bitcast.18), channel_id=1, source_target_pairs={{1,0},{2,1},{3,2},{4,3},{5,4},{6,5},{7,6},{8,7},{9,8},{10,9},{11,1... | collective-permute-start | bytes 2752520 | tf_op jit(solution)/shard_map/ppermute | solution.py:500
  14.3 5.7 %copy-start.1 = (f32[4,256,512]{2,1,0:T(8,128)S(1)}, f32[4,256,512]{2,1,0:T(8,128)}, u32[]{:S(2)}) copy-start(f32[4,256,512]{2,1,0:T(8,128)} %reshape.23.refs_2_.refs_3_) | copy-start | bytes 6291460
  14.3 5.7 %copy-start.6 = (bf16[6,256,256]{2,1,0:T(8,128)(2,1)S(1)}, bf16[6,256,256]{2,1,0:T(8,128)(2,1)}, u32[]{:S(2)}) copy-start(bf16[6,256,256]{2,1,0:T(8,128)(2,1)} %refs_4_.2) | copy-start | bytes 2359300
  14.3 5.7 %copy-start.7 = (bf16[6,256,256]{2,1,0:T(8,128)(2,1)S(1)}, bf16[6,256,256]{2,1,0:T(8,128)(2,1)}, u32[]{:S(2)}) copy-start(bf16[6,256,256]{2,1,0:T(8,128)(2,1)} %constant.60.clone.refs_4_.refs_5_) | copy-start | bytes 2359300
  19.9 21.0 %copy-start.4 = (bf16[256,2304]{1,0:T(8,128)(2,1)}, bf16[256,2304]{1,0:T(8,128)(2,1)S(1)}, u32[]{:S(2)}) copy-start(bf16[256,2304]{1,0:T(8,128)(2,1)S(1)} %collective-permute-done.refs_1_.refs_2_) | copy-start | bytes 3538948
  40.9 7.5 %copy-start.5 = (bf16[256,2304]{1,0:T(8,128)(2,1)S(1)}, bf16[256,2304]{1,0:T(8,128)(2,1)}, u32[]{:S(2)}) copy-start(bf16[256,2304]{1,0:T(8,128)(2,1)} %copy-done.4) | copy-start | bytes 3538948
  46.5 15.6 %collective-permute-start.2 = (bf16[256,1792]{1,0:T(8,128)(2,1)S(1)}, bf16[256,1792]{1,0:T(8,128)(2,1)S(1)}, u32[]{:S(2)}, u32[]{:S(2)}) collective-permute-start(bf16[256,1792]{1,0:T(8,128)(2,1)S(1)} %below_0.1), channel_id=1, source_target_pairs={{0,1},{1,2},{2,3},{3,4},{4,5},{5,6},{6,7},{7,8},{8,9},{9,10},{10,1... | collective-permute-start | bytes 2752520 | tf_op jit(solution)/shard_map/ppermute | solution.py:500
  56.0 1.3 %copy-start = (f32[4,256,512]{2,1,0:T(8,128)}, f32[4,256,512]{2,1,0:T(8,128)S(1)}, u32[]{:S(2)}) copy-start(f32[4,256,512]{2,1,0:T(8,128)S(1)} %get-tuple-element.23) | copy-start | bytes 6291460
  62.1 0.9 copy-start.2
  63.0 4.9 %collective-permute-start.3 = (bf16[4,256,512]{2,1,0:T(8,128)(2,1)}, bf16[4,256,512]{2,1,0:T(8,128)(2,1)}, u32[]{:S(2)}, u32[]{:S(2)}) collective-permute-start(bf16[4,256,512]{2,1,0:T(8,128)(2,1)} %get-tuple-element.26), channel_id=1, source_target_pairs={{1,0},{3,2},{5,4},{7,6},{9,8},{11,10},{13,12},{15,14},{17,16},{19,... | collective-permute-start | bytes 3145736 | tf_op jit(solution)/shard_map/ppermute | solution.py:580
  72.3 22.4 %collective-permute-start.4 = (bf16[256,512]{1,0:T(8,128)(2,1)}, bf16[256,512]{1,0:T(8,128)(2,1)}, u32[]{:S(2)}, u32[]{:S(2)}) collective-permute-start(bf16[256,512]{1,0:T(8,128)(2,1)} %get-tuple-element.35), channel_id=1, source_target_pairs={{0,2},{2,0},{4,6},{6,4},{8,10},{10,8},{12,14},{14,12},{16,18},{18,... | collective-permute-start | bytes 786440 | tf_op jit(solution)/shard_map/ppermute | solution.py:585
  74.2 20.5 %collective-permute-start.6 = (bf16[256,512]{1,0:T(8,128)(2,1)}, bf16[256,512]{1,0:T(8,128)(2,1)}, u32[]{:S(2)}, u32[]{:S(2)}) collective-permute-start(bf16[256,512]{1,0:T(8,128)(2,1)} %get-tuple-element.36), channel_id=1, source_target_pairs={{0,6},{2,4},{4,2},{6,0},{8,14},{10,12},{12,10},{14,8},{16,22},{18,... | collective-permute-start | bytes 786440 | tf_op jit(solution)/shard_map/ppermute | solution.py:585
  76.1 18.6 %collective-permute-start.5 = (bf16[256,512]{1,0:T(8,128)(2,1)S(1)}, bf16[256,512]{1,0:T(8,128)(2,1)}, u32[]{:S(2)}, u32[]{:S(2)}) collective-permute-start(bf16[256,512]{1,0:T(8,128)(2,1)S(1)} %get-tuple-element.37), channel_id=1, source_target_pairs={{0,4},{2,6},{4,0},{6,2},{8,12},{10,14},{12,8},{14,10},{16,20},{18,... | collective-permute-start | bytes 786440 | tf_op jit(solution)/shard_map/ppermute | solution.py:585
  85.6 34.8 %collective-permute-start.7 = (bf16[256,2304]{1,0:T(8,128)(2,1)S(1)}, bf16[256,2304]{1,0:T(8,128)(2,1)S(1)}, u32[]{:S(2)}, u32[]{:S(2)}) collective-permute-start(bf16[256,2304]{1,0:T(8,128)(2,1)S(1)} %below_1.1), channel_id=1, source_target_pairs={{0,1},{1,2},{2,3},{3,4},{4,5},{5,6},{6,7},{7,8},{8,9},{9,10},{10,1... | collective-permute-start | bytes 3538952 | tf_op jit(solution)/shard_map/ppermute | solution.py:500
  94.7 25.7 %copy-start.3 = (bf16[256,1792]{1,0:T(8,128)(2,1)S(1)}, bf16[256,1792]{1,0:T(8,128)(2,1)}, u32[]{:S(2)}) copy-start(bf16[256,1792]{1,0:T(8,128)(2,1)} %copy-done.2) | copy-start | bytes 2752516
  96.3 9.2 %collective-permute-start.8 = (bf16[256,512]{1,0:T(8,128)(2,1)S(1)}, bf16[256,512]{1,0:T(8,128)(2,1)S(1)}, u32[]{:S(2)}, u32[]{:S(2)}) collective-permute-start(bf16[256,512]{1,0:T(8,128)(2,1)S(1)} %convert_element_type.29), channel_id=1, source_target_pairs={{0,8},{2,10},{4,12},{6,14},{8,0},{10,2},{12,4},{14,6},{16,24},{18,... | collective-permute-start | bytes 786440 | tf_op jit(solution)/shard_map/ppermute | solution.py:593
  105.5 10.6 %collective-permute-start.11 = (bf16[256,512]{1,0:T(8,128)(2,1)S(1)}, bf16[256,512]{1,0:T(8,128)(2,1)S(1)}, u32[]{:S(2)}, u32[]{:S(2)}) collective-permute-start(bf16[256,512]{1,0:T(8,128)(2,1)S(1)} %add_convert_fusion.refs_0_), channel_id=1, source_target_pairs={{0,6},{2,4},{4,2},{6,0},{8,14},{10,12},{12,10},{14,8},{16,22},{18,... | collective-permute-start | bytes 786440 | tf_op jit(solution)/shard_map/ppermute | solution.py:595
  108.7 8.7 %collective-permute-start.10 = (bf16[256,512]{1,0:T(8,128)(2,1)S(1)}, bf16[256,512]{1,0:T(8,128)(2,1)S(1)}, u32[]{:S(2)}, u32[]{:S(2)}) collective-permute-start(bf16[256,512]{1,0:T(8,128)(2,1)S(1)} %add_convert_fusion.refs_0_), channel_id=1, source_target_pairs={{0,4},{2,6},{4,0},{6,2},{8,12},{10,14},{12,8},{14,10},{16,20},{18,... | collective-permute-start | bytes 786440 | tf_op jit(solution)/shard_map/ppermute | solution.py:595
  110.7 8.4 %collective-permute-start.9 = (bf16[256,512]{1,0:T(8,128)(2,1)S(1)}, bf16[256,512]{1,0:T(8,128)(2,1)S(1)}, u32[]{:S(2)}, u32[]{:S(2)}) collective-permute-start(bf16[256,512]{1,0:T(8,128)(2,1)S(1)} %add_convert_fusion.refs_0_), channel_id=1, source_target_pairs={{0,2},{2,0},{4,6},{6,4},{8,10},{10,8},{12,14},{14,12},{16,18},{18,... | collective-permute-start | bytes 786440 | tf_op jit(solution)/shard_map/ppermute | solution.py:595
  114.8 8.6 %collective-permute-start.12 = (bf16[256,512]{1,0:T(8,128)(2,1)S(1)}, bf16[256,512]{1,0:T(8,128)(2,1)S(1)}, u32[]{:S(2)}, u32[]{:S(2)}) collective-permute-start(bf16[256,512]{1,0:T(8,128)(2,1)S(1)} %add_convert_fusion.refs_0_), channel_id=1, source_target_pairs={{0,1},{2,3},{4,5},{6,7},{8,9},{10,11},{12,13},{14,15},{16,17},{18,... | collective-permute-start | bytes 786440 | tf_op jit(solution)/shard_map/ppermute | solution.py:596
  116.1 7.3 %collective-permute-start.15 = (bf16[256,512]{1,0:T(8,128)(2,1)S(1)}, bf16[256,512]{1,0:T(8,128)(2,1)S(1)}, u32[]{:S(2)}, u32[]{:S(2)}) collective-permute-start(bf16[256,512]{1,0:T(8,128)(2,1)S(1)} %collective-permute-done.11.refs_3_), channel_id=1, source_target_pairs={{0,1},{2,3},{4,5},{6,7},{8,9},{10,11},{12,13},{14,15},{16,17},{18,... | collective-permute-start | bytes 786440 | tf_op jit(solution)/shard_map/ppermute | solution.py:596
  117.4 6.0 %collective-permute-start.14 = (bf16[256,512]{1,0:T(8,128)(2,1)S(1)}, bf16[256,512]{1,0:T(8,128)(2,1)S(1)}, u32[]{:S(2)}, u32[]{:S(2)}) collective-permute-start(bf16[256,512]{1,0:T(8,128)(2,1)S(1)} %collective-permute-done.10.refs_2_), channel_id=1, source_target_pairs={{0,1},{2,3},{4,5},{6,7},{8,9},{10,11},{12,13},{14,15},{16,17},{18,... | collective-permute-start | bytes 786440 | tf_op jit(solution)/shard_map/ppermute | solution.py:596
  119.1 4.3 %collective-permute-start.13 = (bf16[256,512]{1,0:T(8,128)(2,1)S(1)}, bf16[256,512]{1,0:T(8,128)(2,1)S(1)}, u32[]{:S(2)}, u32[]{:S(2)}) collective-permute-start(bf16[256,512]{1,0:T(8,128)(2,1)S(1)} %collective-permute-done.9.refs_1_), channel_id=1, source_target_pairs={{0,1},{2,3},{4,5},{6,7},{8,9},{10,11},{12,13},{14,15},{16,17},{18,... | collective-permute-start | bytes 786440 | tf_op jit(solution)/shard_map/ppermute | solution.py:596

commit v2 on v1

--- a/solution.py
+++ b/solution.py
@@ -64,11 +64,7 @@
         refs = refs[2:]
     moved, grads = refs[:2]
     refs = refs[2:]
-    if last_stage:
-        keep, give = refs[:2]
-        refs = refs[2:]
-    else:
-        sums_out = refs.pop(0)
+    sums_out = refs.pop(0)
     cells, mixed, patch, folded, half_u, half_v, far, error, back, probe, measured, tables, probe_acc, held = refs[:14]
     sems, slot_sems = refs[14:16]
     if last_stage and not first_stage:
@@ -285,14 +281,11 @@
     if last_stage:
         if first_stage:
             given[...] = probe_acc[...].astype(BF16)
-            store(given, give)
         else:
             copies[-1].wait()
             for mode in range(modes):
-                probe_acc[mode] += sums[mode]
-                given[mode] = probe_acc[mode].astype(BF16)
-            store(given, give)
-        store(probe_acc, keep)
+                given[mode] = (probe_acc[mode] + sums[mode]).astype(BF16)
+        store(given, sums_out)
     else:
         store(probe_acc, sums_out)
 
@@ -320,13 +313,11 @@
     outs = [
         jax.ShapeDtypeStruct((2, slots), F32),
         jax.ShapeDtypeStruct((slots, size, 2 * size), BF16),
-        jax.ShapeDtypeStruct(probe.shape, F32),
+        jax.ShapeDtypeStruct(probe.shape, BF16 if last_stage else F32),
     ]
     if not first_stage:
         inputs += list(carried)
         specs += [smem, hbm]
-    if last_stage:
-        outs += [jax.ShapeDtypeStruct(probe.shape, BF16)]
     scratch = [
         pltpu.VMEM((rows + size + 32, 2 * extent), BF16),
         pltpu.VMEM((2, size + 16, 2 * size), F32),
@@ -569,29 +560,29 @@
     return [(i, i ^ (2 * stride * shift)) for i in range(0, lax.axis_size(axis), 2)]
 
 
-def summed(keep, give, axis, shape, order, first, between, after):
+def summed(given, axis, shape, order, beside, between):
     length = lax.axis_size(axis)
     near = near_chips(axis)
     far = length // 2 // near
     inward = [(i + 1, i) for i in range(0, length, 2)]
     outward = [(i, i + 1) for i in range(0, length, 2)]
-    modes, size, columns = keep.shape
+    modes, size, columns = given.shape
     spot = lax.axis_index(axis) // 2 % near
-    mine = keep + lax.ppermute(give, axis, inward).astype(F32)
-    mine = first(mine)
-    mine = mine.reshape(near, modes * size // near, columns)
-    parts = mine.astype(BF16)
+    sibling = beside(lax.ppermute(given, axis, inward))
+    parts = (given.astype(F32) + sibling.astype(F32)).astype(BF16).reshape(near, modes * size // near, columns)
     got = [
         lax.ppermute(lax.dynamic_index_in_dim(parts, spot ^ s, 0, False), axis, hop(axis, s, 1)) for s in range(1, near)
     ]
-    total = lax.dynamic_index_in_dim(mine, spot, 0, False)
+    total = lax.dynamic_index_in_dim(parts, spot, 0, False).astype(F32)
     for piece in got:
         total = total + piece.astype(F32)
-    total = between(total)
     sent = total.astype(BF16)
-    for s in range(1, far):
-        total = total + lax.ppermute(sent, axis, hop(axis, s, near)).astype(F32)
-    total = after(total.astype(BF16))
+    others = [lax.ppermute(sent, axis, hop(axis, s, near)) for s in range(1, far)]
+    if others:
+        others[0] = between(others[0])
+    for piece in others:
+        total = total + piece.astype(F32)
+    total = total.astype(BF16)
     pieces = [total] + [lax.ppermute(total, axis, hop(axis, s, 1)) for s in range(1, near)]
     others = [lax.ppermute(piece, axis, outward) for piece in pieces]
     return unpacked(pieces, others, order, shape)
@@ -619,27 +610,27 @@
     own = object_tiles.reshape(rows, 2 * width)
     flat = probe.reshape(modes, size, 2 * size)
     carried = None
-    grads, aboves = [], []
-    edges = [0] + [bound - size for bound in bounds[1:-1]] + [width]
+    grads = []
     for stage in range(stages):
         moved, grad, *rest = project(stage, bounds, places, own, rims, flat, measured, tables, width, carried)
         grads.append(grad)
         carried = [moved] + rest
-        below = settle(places, grads, bounds, edges[stage], edges[stage + 1], size, BF16, width, f"below_{stage}")
-        if stage < stages - 1:
-            places, below = lax.optimization_barrier((places, below))
-        aboves.append(passed_along(below, "row", 1))
-    _, keep, give = carried
-    give, aboves[0] = lax.optimization_barrier((give, aboves[0]))
+    given = carried[1]
+    below = settle(places, grads, bounds, 0, width, size, BF16, width, "below_rows")
     held = {}
+
+    def beside(x):
+        x, held["below"] = lax.optimization_barrier((x, below))
+        return x
 
     def between(x):
         own_rows = settle(places, grads, bounds, 0, width, 0, F32, width, "own_rows")
         x, held["own"] = lax.optimization_barrier((x, own_rows))
         return x
 
-    probe_grad = summed(keep, give, "row", probe.shape, order, lambda x: x, between, lambda x: x)
-    object_grad = finish(held["own"], aboves, edges, width)
+    probe_grad = summed(given, "row", probe.shape, order, beside, between)
+    above = passed_along(held["below"], "row", 1)
+    object_grad = finish(held["own"], [above], (0, width), width)
     return object_grad, probe_grad, moved
 
 

time: 128 us -> 129 us (level)
  the two profiles are of different devices: /device:TPU:16 before, /device:TPU:0 now
where the time goes in v2:
time: 129 us; the launch traced here: 127 us
  starting transfers between devices  59.5 us (46%)
  Pallas kernels  38.4 us (30%)
  local copies, waits for them, and re-layouts  14.2 us (11%)
  waiting for transfers between devices  8.49 us (7%)
  other arithmetic  4.34 us (3%)
  between operations  1.84 us (1%)
    ppermute x3, starting transfers between devices, summed(): lax.ppermute(lax.dynamic_index_in_dim(parts, spot ^ s, 0, False), axis, h...  23.1 us
    pallas_call x2, Pallas kernels, project(): pl.pallas_call(functools.partial(project_kernel, size, width, bounds, sta...  20.2 us
    pallas_call x2, Pallas kernels, settle(): pl.pallas_call(functools.partial(settle_kernel, size, bounds, low, high,...  11.8 us
    ppermute x1, starting transfers between devices, summed(): lax.ppermute(sent, axis, hop(axis, s, near))  10.9 us
    ppermute x3, starting transfers between devices, passed_along(): return lax.ppermute(x, axis, pairs)  9.54 us
    ppermute x3, starting transfers between devices, summed(): lax.ppermute(total, axis, hop(axis, s, 1))  9.21 us
    unnamed x25, local copies, waits for them, and re-layouts  8.05 us
    ppermute x3, waiting for transfers between devices, summed(): lax.ppermute(lax.dynamic_index_in_dim(parts, spot ^ s, 0, False), axis, h...  5.57 us
  transfers between devices with their start and end apart: 15, of which 5 were waited for; matrix products, arithmetic and copies ran while one was open for 10% of the time, Pallas kernels for 19%

profile of v2, /device:TPU:0, one launch (start us, length us, event | category | flops | bytes accessed | tf_op | source)
XLA Modules:
  0.0 126.8 jit_solution(11282776551633167797)
XLA Ops:
  0.6 1.3 slice-done
  1.9 1.1 copy.13
  3.1 1.4 %collective-permute-start.1 = (bf16[256,2304]{1,0:T(8,128)(2,1)}, bf16[256,2304]{1,0:T(8,128)(2,1)S(1)}, u32[]{:S(2)}, u32[]{:S(2)}) collective-permute-start(bf16[256,2304]{1,0:T(8,128)(2,1)} %bitcast.19), channel_id=1, source_target_pairs={{1,0},{2,1},{3,2},{4,3},{5,4},{6,5},{7,6},{8,7},{9,8},{10,9},{11,1... | collective-permute-start | bytes 3538952 | tf_op jit(solution)/shard_map/ppermute | solution.py:491
  5.5 1.3 %collective-permute-start = (bf16[256,1792]{1,0:T(8,128)(2,1)}, bf16[256,1792]{1,0:T(8,128)(2,1)}, u32[]{:S(2)}, u32[]{:S(2)}) collective-permute-start(bf16[256,1792]{1,0:T(8,128)(2,1)} %bitcast.17), channel_id=1, source_target_pairs={{1,0},{2,1},{3,2},{4,3},{5,4},{6,5},{7,6},{8,7},{9,8},{10,9},{11,1... | collective-permute-start | bytes 2752520 | tf_op jit(solution)/shard_map/ppermute | solution.py:491
  7.6 3.9 %reshape.26.refs_2_.refs_3_ = f32[4,256,512]{2,1,0:T(8,128)} reshape(f32[4,256,2,256]{3,2,1,0:T(2,128)} %param.9) | data formatting | bytes 4194304 | tf_op jit(solution)/shard_map/reshape | solution.py:611
  11.5 2.6 %copy.11 = bf16[32,8,2,2048]{3,1,2,0:T(8,128)(2,1)S(1)} copy(bf16[32,8,2,2048]{3,2,1,0:T(2,128)(2,1)} %bitcast.31) | data formatting | bytes 4194304
  14.2 9.8 %project_0.1 = (f32[2,6]{1,0:T(2,128)S(1)}, bf16[6,256,512]{2,1,0:T(8,128)(2,1)S(1)}, f32[4,256,512]{2,1,0:T(8,128)S(1)}) custom-call(s32[5,6]{1,0:T(8,128)S(1)} %stack.33.places, bf16[256,4096]{1,0:T(8,128)(2,1)S(1)} %bitcast.29, bf16[256,2304]{1,0:T(8,128)(2,1)S(1)} %collective-permute-done.1.refs_1_.refs_2_, f32[4,256,512]{2,1,0:T(8,128)S(1)} %copy-done, ...), custom_call_target="tpu_custom_call" | custom-call | flops 8000000000 | bytes 16777216 | tf_op jit(solution)/shard_map/project_0/pallas_call | solution.py:343
  24.0 1.3 copy-done.3
  25.3 10.5 %project_1.1 = (f32[2,6]{1,0:T(2,128)}, bf16[6,256,512]{2,1,0:T(8,128)(2,1)S(1)}, bf16[4,256,512]{2,1,0:T(8,128)(2,1)S(1)}) custom-call(s32[5,6]{1,0:T(8,128)S(1)} %stack.33.places, bf16[256,4096]{1,0:T(8,128)(2,1)S(1)} %bitcast.30, bf16[256,1792]{1,0:T(8,128)(2,1)} %collective-permute-done.refs_1_, bf16[256,2304]{1,0:T(8,128)(2,1)S(1)} %copy-done.3, ...), custom_call_target="tpu_custom_call" | custom-call | flops 8000000000 | bytes 16777216 | tf_op jit(solution)/shard_map/project_1/pallas_call | solution.py:343
  35.8 1.5 %collective-permute-start.2 = (bf16[4,256,512]{2,1,0:T(8,128)(2,1)S(1)}, bf16[4,256,512]{2,1,0:T(8,128)(2,1)S(1)}, u32[]{:S(2)}, u32[]{:S(2)}) collective-permute-start(bf16[4,256,512]{2,1,0:T(8,128)(2,1)S(1)} %get-tuple-element.18), channel_id=1, source_target_pairs={{1,0},{3,2},{5,4},{7,6},{9,8},{11,10},{13,12},{15,14},{17,16},{19,... | collective-permute-start | bytes 3145736 | tf_op jit(solution)/shard_map/ppermute | solution.py:571
  37.2 6.4 %below_rows.1 = bf16[256,4096]{1,0:T(8,128)(2,1)} custom-call(s32[5,6]{1,0:T(8,128)S(1)} %stack.33.places, bf16[6,256,512]{2,1,0:T(8,128)(2,1)S(1)} %get-tuple-element.19.refs_0_, bf16[6,256,512]{2,1,0:T(8,128)(2,1)S(1)} %get-tuple-element.20.refs_1_), custom_call_target="tpu_custom_call" | custom-call | flops 1000000000 | bytes 8388608 | tf_op jit(solution)/shard_map/below_rows/pallas_call | solution.py:425
  44.7 6.9 %collective-permute-start.7 = (bf16[256,4096]{1,0:T(8,128)(2,1)}, bf16[256,4096]{1,0:T(8,128)(2,1)}, u32[]{:S(2)}, u32[]{:S(2)}) collective-permute-start(bf16[256,4096]{1,0:T(8,128)(2,1)} %below_rows.1), channel_id=1, source_target_pairs={{0,1},{1,2},{2,3},{3,4},{4,5},{5,6},{6,7},{7,8},{8,9},{9,10},{10,1... | collective-permute-start | bytes 6291464 | tf_op jit(solution)/shard_map/ppermute | solution.py:491
  51.5 1.8 %add_convert_fusion = bf16[4,256,512]{2,1,0:T(8,128)(2,1)S(1)} fusion(bf16[4,256,512]{2,1,0:T(8,128)(2,1)} %copy-done.7, bf16[4,256,512]{2,1,0:T(8,128)(2,1)} %copy-done.1), kind=kLoop, calls=%fused_computation | loop fusion | flops 2097152 | bytes 3145728 | tf_op jit(solution)/shard_map/convert_element_type | solution.py:572
  55.2 17.8 %collective-permute-start.3 = (bf16[256,512]{1,0:T(8,128)(2,1)}, bf16[256,512]{1,0:T(8,128)(2,1)S(1)}, u32[]{:S(2)}, u32[]{:S(2)}) collective-permute-start(bf16[256,512]{1,0:T(8,128)(2,1)} %get-tuple-element.27), channel_id=1, source_target_pairs={{0,2},{2,0},{4,6},{6,4},{8,10},{10,8},{12,14},{14,12},{16,18},{18,... | collective-permute-start | bytes 786440 | tf_op jit(solution)/shard_map/ppermute | solution.py:574
  73.1 1.9 %collective-permute-start.5 = (bf16[256,512]{1,0:T(8,128)(2,1)}, bf16[256,512]{1,0:T(8,128)(2,1)}, u32[]{:S(2)}, u32[]{:S(2)}) collective-permute-start(bf16[256,512]{1,0:T(8,128)(2,1)} %get-tuple-element.28), channel_id=1, source_target_pairs={{0,6},{2,4},{4,2},{6,0},{8,14},{10,12},{12,10},{14,8},{16,22},{18,... | collective-permute-start | bytes 786440 | tf_op jit(solution)/shard_map/ppermute | solution.py:574
  75.0 3.4 %collective-permute-start.4 = (bf16[256,512]{1,0:T(8,128)(2,1)}, bf16[256,512]{1,0:T(8,128)(2,1)}, u32[]{:S(2)}, u32[]{:S(2)}) collective-permute-start(bf16[256,512]{1,0:T(8,128)(2,1)} %get-tuple-element.29), channel_id=1, source_target_pairs={{0,4},{2,6},{4,0},{6,2},{8,12},{10,14},{12,8},{14,10},{16,20},{18,... | collective-permute-start | bytes 786440 | tf_op jit(solution)/shard_map/ppermute | solution.py:574
  78.4 4.5 %collective-permute-done.3 = bf16[256,512]{1,0:T(8,128)(2,1)S(1)} collective-permute-done((bf16[256,512]{1,0:T(8,128)(2,1)}, bf16[256,512]{1,0:T(8,128)(2,1)S(1)}, u32[]{:S(2)}, u32[]{:S(2)}) %collective-permute-start.3) | collective-permute-done | bytes 262176 | tf_op jit(solution)/shard_map/ppermute | solution.py:574
  84.0 1.2 fusion.2
  85.2 10.9 %collective-permute-start.6 = (bf16[256,512]{1,0:T(8,128)(2,1)S(1)}, bf16[256,512]{1,0:T(8,128)(2,1)S(1)}, u32[]{:S(2)}, u32[]{:S(2)}) collective-permute-start(bf16[256,512]{1,0:T(8,128)(2,1)S(1)} %fusion.2), channel_id=1, source_target_pairs={{0,8},{2,10},{4,12},{6,14},{8,0},{10,2},{12,4},{14,6},{16,24},{18,... | collective-permute-start | bytes 786440 | tf_op jit(solution)/shard_map/ppermute | solution.py:580
  96.1 5.4 %own_rows.1.own = f32[256,4096]{1,0:T(8,128)S(1)} custom-call(s32[5,6]{1,0:T(8,128)S(1)} %stack.33.places, bf16[6,256,512]{2,1,0:T(8,128)(2,1)S(1)} %get-tuple-element.19.refs_0_, bf16[6,256,512]{2,1,0:T(8,128)(2,1)S(1)} %get-tuple-element.20.refs_1_), custom_call_target="tpu_custom_call" | custom-call | flops 1000000000 | bytes 8388608 | tf_op jit(solution)/shard_map/own_rows/pallas_call | solution.py:425
  102.1 1.3 %add_convert_fusion.1.refs_0_ = bf16[256,512]{1,0:T(8,128)(2,1)S(1)} fusion(bf16[256,512]{1,0:T(8,128)(2,1)S(1)} %collective-permute-done.6, bf16[256,512]{1,0:T(8,128)(2,1)} %collective-permute-done.5, bf16[256,512]{1,0:T(8,128)(2,1)} %collective-permute-done.4, bf16[256,512]{1,0:T(8,128)(2,1)S(1)} %collective-permute-done.3, ...), kind=kLoop, calls=%fused_computation.4 | loop fusion | flops 1310720 | bytes 1572868 | tf_op jit(solution)/shard_map/convert_element_type | solution.py:585
  103.4 1.9 %collective-permute-start.10 = (bf16[256,512]{1,0:T(8,128)(2,1)S(1)}, bf16[256,512]{1,0:T(8,128)(2,1)S(1)}, u32[]{:S(2)}, u32[]{:S(2)}) collective-permute-start(bf16[256,512]{1,0:T(8,128)(2,1)S(1)} %add_convert_fusion.1.refs_0_), channel_id=1, source_target_pairs={{0,6},{2,4},{4,2},{6,0},{8,14},{10,12},{12,10},{14,8},{16,22},{18,... | collective-permute-start | bytes 786440 | tf_op jit(solution)/shard_map/ppermute | solution.py:586
  105.3 4.2 %collective-permute-start.9 = (bf16[256,512]{1,0:T(8,128)(2,1)S(1)}, bf16[256,512]{1,0:T(8,128)(2,1)S(1)}, u32[]{:S(2)}, u32[]{:S(2)}) collective-permute-start(bf16[256,512]{1,0:T(8,128)(2,1)S(1)} %add_convert_fusion.1.refs_0_), channel_id=1, source_target_pairs={{0,4},{2,6},{4,0},{6,2},{8,12},{10,14},{12,8},{14,10},{16,20},{18,... | collective-permute-start | bytes 786440 | tf_op jit(solution)/shard_map/ppermute | solution.py:586
  109.5 3.1 %collective-permute-start.8 = (bf16[256,512]{1,0:T(8,128)(2,1)S(1)}, bf16[256,512]{1,0:T(8,128)(2,1)S(1)}, u32[]{:S(2)}, u32[]{:S(2)}) collective-permute-start(bf16[256,512]{1,0:T(8,128)(2,1)S(1)} %add_convert_fusion.1.refs_0_), channel_id=1, source_target_pairs={{0,2},{2,0},{4,6},{6,4},{8,10},{10,8},{12,14},{14,12},{16,18},{18,... | collective-permute-start | bytes 786440 | tf_op jit(solution)/shard_map/ppermute | solution.py:586
  112.6 1.3 %collective-permute-start.11 = (bf16[256,512]{1,0:T(8,128)(2,1)S(1)}, bf16[256,512]{1,0:T(8,128)(2,1)S(1)}, u32[]{:S(2)}, u32[]{:S(2)}) collective-permute-start(bf16[256,512]{1,0:T(8,128)(2,1)S(1)} %add_convert_fusion.1.refs_0_), channel_id=1, source_target_pairs={{0,1},{2,3},{4,5},{6,7},{8,9},{10,11},{12,13},{14,15},{16,17},{18,... | collective-permute-start | bytes 786440 | tf_op jit(solution)/shard_map/ppermute | solution.py:587
  113.9 1.3 %collective-permute-start.14 = (bf16[256,512]{1,0:T(8,128)(2,1)S(1)}, bf16[256,512]{1,0:T(8,128)(2,1)S(1)}, u32[]{:S(2)}, u32[]{:S(2)}) collective-permute-start(bf16[256,512]{1,0:T(8,128)(2,1)S(1)} %collective-permute-done.10.refs_3_), channel_id=1, source_target_pairs={{0,1},{2,3},{4,5},{6,7},{8,9},{10,11},{12,13},{14,15},{16,17},{18,... | collective-permute-start | bytes 786440 | tf_op jit(solution)/shard_map/ppermute | solution.py:587
  115.3 1.3 %collective-permute-start.13 = (bf16[256,512]{1,0:T(8,128)(2,1)S(1)}, bf16[256,512]{1,0:T(8,128)(2,1)S(1)}, u32[]{:S(2)}, u32[]{:S(2)}) collective-permute-start(bf16[256,512]{1,0:T(8,128)(2,1)S(1)} %collective-permute-done.9.refs_2_), channel_id=1, source_target_pairs={{0,1},{2,3},{4,5},{6,7},{8,9},{10,11},{12,13},{14,15},{16,17},{18,... | collective-permute-start | bytes 786440 | tf_op jit(solution)/shard_map/ppermute | solution.py:587
  116.6 1.2 collective-permute-done.8.refs_1_
  117.8 1.3 %collective-permute-start.12 = (bf16[256,512]{1,0:T(8,128)(2,1)S(1)}, bf16[256,512]{1,0:T(8,128)(2,1)S(1)}, u32[]{:S(2)}, u32[]{:S(2)}) collective-permute-start(bf16[256,512]{1,0:T(8,128)(2,1)S(1)} %collective-permute-done.8.refs_1_), channel_id=1, source_target_pairs={{0,1},{2,3},{4,5},{6,7},{8,9},{10,11},{12,13},{14,15},{16,17},{18,... | collective-permute-start | bytes 786440 | tf_op jit(solution)/shard_map/ppermute | solution.py:587
  119.1 1.1 collective-permute-done.12.refs_5_
  120.2 2.1 %unpack.1 = f32[4,256,2,256]{3,2,1,0:T(2,128)} custom-call(s32[5]{0:T(128)S(1)} %stack.39.order, bf16[256,512]{1,0:T(8,128)(2,1)S(1)} %add_convert_fusion.1.refs_0_, bf16[256,512]{1,0:T(8,128)(2,1)S(1)} %collective-permute-done.8.refs_1_, bf16[256,512]{1,0:T(8,128)(2,1)S(1)} %collective-permute-done.9.refs_2_, ...), custom_call_target="tpu_custom_call" | custom-call | flops 1000000 | bytes 4194304 | tf_op jit(solution)/shard_map/unpack/pallas_call | solution.py:532
  122.4 4.3 %finish.1 = f32[256,2,2048]{2,1,0:T(2,128)} custom-call(f32[256,4096]{1,0:T(8,128)S(1)} %own_rows.1.own, bf16[256,4096]{1,0:T(8,128)(2,1)} %collective-permute-done.7.refs_0_), custom_call_target="tpu_custom_call" | custom-call | flops 1000000 | bytes 10485760 | tf_op jit(solution)/shard_map/finish/pallas_call | solution.py:474
  (42 shorter events, 5.7 us)
Async XLA Ops:
  0.6 1.3 %slice-start = ((bf16[256,2,2048]{2,1,0:T(2,128)(2,1)}), bf16[256,2,1152]{2,1,0:T(2,128)(2,1)S(1)}, s32[]{:S(2)}) async-start(bf16[256,2,2048]{2,1,0:T(2,128)(2,1)} %param.8), calls=%async_computation | async-start | bytes 2359296 | tf_op jit(solution)/shard_map/slice | solution.py:602
  1.9 2.6 %slice-start.1 = ((bf16[256,2,2048]{2,1,0:T(2,128)(2,1)}), bf16[256,2,896]{2,1,0:T(2,128)(2,1)S(1)}, s32[]{:S(2)}) async-start(bf16[256,2,2048]{2,1,0:T(2,128)(2,1)} %param.8), calls=%async_computation.1 | async-start | bytes 1835008 | tf_op jit(solution)/shard_map/slice | solution.py:602
  3.0 4.5 %copy-start.8 = (s32[6]{0:T(128)S(1)}, s32[6]{0:T(128)}, u32[]{:S(2)}) copy-start(s32[6]{0:T(128)} %param.11) | copy-start | bytes 76
  3.1 4.5 %copy-start.9 = (s32[6]{0:T(128)S(1)}, s32[6]{0:T(128)}, u32[]{:S(2)}) copy-start(s32[6]{0:T(128)} %param.12) | copy-start | bytes 76
  3.1 4.5 %copy-start.10 = (s32[6]{0:T(128)S(1)}, s32[6]{0:T(128)}, u32[]{:S(2)}) copy-start(s32[6]{0:T(128)} %param.13) | copy-start | bytes 76
  3.1 11.1 %collective-permute-start.1 = (bf16[256,2304]{1,0:T(8,128)(2,1)}, bf16[256,2304]{1,0:T(8,128)(2,1)S(1)}, u32[]{:S(2)}, u32[]{:S(2)}) collective-permute-start(bf16[256,2304]{1,0:T(8,128)(2,1)} %bitcast.19), channel_id=1, source_target_pairs={{1,0},{2,1},{3,2},{4,3},{5,4},{6,5},{7,6},{8,7},{9,8},{10,9},{11,1... | collective-permute-start | bytes 3538952 | tf_op jit(solution)/shard_map/ppermute | solution.py:491
  5.5 18.5 %collective-permute-start = (bf16[256,1792]{1,0:T(8,128)(2,1)}, bf16[256,1792]{1,0:T(8,128)(2,1)}, u32[]{:S(2)}, u32[]{:S(2)}) collective-permute-start(bf16[256,1792]{1,0:T(8,128)(2,1)} %bitcast.17), channel_id=1, source_target_pairs={{1,0},{2,1},{3,2},{4,3},{5,4},{6,5},{7,6},{8,7},{9,8},{10,9},{11,1... | collective-permute-start | bytes 2752520 | tf_op jit(solution)/shard_map/ppermute | solution.py:491
  11.5 2.7 %copy-start = (f32[4,256,512]{2,1,0:T(8,128)S(1)}, f32[4,256,512]{2,1,0:T(8,128)}, u32[]{:S(2)}) copy-start(f32[4,256,512]{2,1,0:T(8,128)} %reshape.26.refs_2_.refs_3_) | copy-start | bytes 6291460
  11.5 2.7 %copy-start.4 = (bf16[6,256,256]{2,1,0:T(8,128)(2,1)S(1)}, bf16[6,256,256]{2,1,0:T(8,128)(2,1)}, u32[]{:S(2)}) copy-start(bf16[6,256,256]{2,1,0:T(8,128)(2,1)} %refs_4_.2) | copy-start | bytes 2359300
  11.5 2.7 %copy-start.5 = (bf16[6,256,256]{2,1,0:T(8,128)(2,1)S(1)}, bf16[6,256,256]{2,1,0:T(8,128)(2,1)}, u32[]{:S(2)}) copy-start(bf16[6,256,256]{2,1,0:T(8,128)(2,1)} %constant.58.clone.refs_4_.refs_5_) | copy-start | bytes 2359300
  14.2 9.8 %copy-start.2 = (bf16[256,2304]{1,0:T(8,128)(2,1)}, bf16[256,2304]{1,0:T(8,128)(2,1)S(1)}, u32[]{:S(2)}) copy-start(bf16[256,2304]{1,0:T(8,128)(2,1)S(1)} %collective-permute-done.1.refs_1_.refs_2_) | copy-start | bytes 3538948
  24.0 1.3 %copy-start.3 = (bf16[256,2304]{1,0:T(8,128)(2,1)S(1)}, bf16[256,2304]{1,0:T(8,128)(2,1)}, u32[]{:S(2)}) copy-start(bf16[256,2304]{1,0:T(8,128)(2,1)} %copy-done.2) | copy-start | bytes 3538948
  35.8 7.9 %copy-start.1 = (bf16[4,256,512]{2,1,0:T(8,128)(2,1)}, bf16[4,256,512]{2,1,0:T(8,128)(2,1)S(1)}, u32[]{:S(2)}) copy-start(bf16[4,256,512]{2,1,0:T(8,128)(2,1)S(1)} %get-tuple-element.18) | copy-start | bytes 3145732
  35.8 7.9 %collective-permute-start.2 = (bf16[4,256,512]{2,1,0:T(8,128)(2,1)S(1)}, bf16[4,256,512]{2,1,0:T(8,128)(2,1)S(1)}, u32[]{:S(2)}, u32[]{:S(2)}) collective-permute-start(bf16[4,256,512]{2,1,0:T(8,128)(2,1)S(1)} %get-tuple-element.18), channel_id=1, source_target_pairs={{1,0},{3,2},{5,4},{7,6},{9,8},{11,10},{13,12},{15,14},{17,16},{19,... | collective-permute-start | bytes 3145736 | tf_op jit(solution)/shard_map/ppermute | solution.py:571
  43.7 1.0 copy-start.7
  44.7 77.7 %collective-permute-start.7 = (bf16[256,4096]{1,0:T(8,128)(2,1)}, bf16[256,4096]{1,0:T(8,128)(2,1)}, u32[]{:S(2)}, u32[]{:S(2)}) collective-permute-start(bf16[256,4096]{1,0:T(8,128)(2,1)} %below_rows.1), channel_id=1, source_target_pairs={{0,1},{1,2},{2,3},{3,4},{4,5},{5,6},{6,7},{7,8},{8,9},{9,10},{10,1... | collective-permute-start | bytes 6291464 | tf_op jit(solution)/shard_map/ppermute | solution.py:491
  53.4 1.0 copy-start.6
  55.2 27.7 %collective-permute-start.3 = (bf16[256,512]{1,0:T(8,128)(2,1)}, bf16[256,512]{1,0:T(8,128)(2,1)S(1)}, u32[]{:S(2)}, u32[]{:S(2)}) collective-permute-start(bf16[256,512]{1,0:T(8,128)(2,1)} %get-tuple-element.27), channel_id=1, source_target_pairs={{0,2},{2,0},{4,6},{6,4},{8,10},{10,8},{12,14},{14,12},{16,18},{18,... | collective-permute-start | bytes 786440 | tf_op jit(solution)/shard_map/ppermute | solution.py:574
  73.1 9.9 %collective-permute-start.5 = (bf16[256,512]{1,0:T(8,128)(2,1)}, bf16[256,512]{1,0:T(8,128)(2,1)}, u32[]{:S(2)}, u32[]{:S(2)}) collective-permute-start(bf16[256,512]{1,0:T(8,128)(2,1)} %get-tuple-element.28), channel_id=1, source_target_pairs={{0,6},{2,4},{4,2},{6,0},{8,14},{10,12},{12,10},{14,8},{16,22},{18,... | collective-permute-start | bytes 786440 | tf_op jit(solution)/shard_map/ppermute | solution.py:574
  75.0 9.0 %collective-permute-start.4 = (bf16[256,512]{1,0:T(8,128)(2,1)}, bf16[256,512]{1,0:T(8,128)(2,1)}, u32[]{:S(2)}, u32[]{:S(2)}) collective-permute-start(bf16[256,512]{1,0:T(8,128)(2,1)} %get-tuple-element.29), channel_id=1, source_target_pairs={{0,4},{2,6},{4,0},{6,2},{8,12},{10,14},{12,8},{14,10},{16,20},{18,... | collective-permute-start | bytes 786440 | tf_op jit(solution)/shard_map/ppermute | solution.py:574
  85.2 16.9 %collective-permute-start.6 = (bf16[256,512]{1,0:T(8,128)(2,1)S(1)}, bf16[256,512]{1,0:T(8,128)(2,1)S(1)}, u32[]{:S(2)}, u32[]{:S(2)}) collective-permute-start(bf16[256,512]{1,0:T(8,128)(2,1)S(1)} %fusion.2), channel_id=1, source_target_pairs={{0,8},{2,10},{4,12},{6,14},{8,0},{10,2},{12,4},{14,6},{16,24},{18,... | collective-permute-start | bytes 786440 | tf_op jit(solution)/shard_map/ppermute | solution.py:580
  103.4 10.6 %collective-permute-start.10 = (bf16[256,512]{1,0:T(8,128)(2,1)S(1)}, bf16[256,512]{1,0:T(8,128)(2,1)S(1)}, u32[]{:S(2)}, u32[]{:S(2)}) collective-permute-start(bf16[256,512]{1,0:T(8,128)(2,1)S(1)} %add_convert_fusion.1.refs_0_), channel_id=1, source_target_pairs={{0,6},{2,4},{4,2},{6,0},{8,14},{10,12},{12,10},{14,8},{16,22},{18,... | collective-permute-start | bytes 786440 | tf_op jit(solution)/shard_map/ppermute | solution.py:586
  105.3 9.9 %collective-permute-start.9 = (bf16[256,512]{1,0:T(8,128)(2,1)S(1)}, bf16[256,512]{1,0:T(8,128)(2,1)S(1)}, u32[]{:S(2)}, u32[]{:S(2)}) collective-permute-start(bf16[256,512]{1,0:T(8,128)(2,1)S(1)} %add_convert_fusion.1.refs_0_), channel_id=1, source_target_pairs={{0,4},{2,6},{4,0},{6,2},{8,12},{10,14},{12,8},{14,10},{16,20},{18,... | collective-permute-start | bytes 786440 | tf_op jit(solution)/shard_map/ppermute | solution.py:586
  109.5 8.3 %collective-permute-start.8 = (bf16[256,512]{1,0:T(8,128)(2,1)S(1)}, bf16[256,512]{1,0:T(8,128)(2,1)S(1)}, u32[]{:S(2)}, u32[]{:S(2)}) collective-permute-start(bf16[256,512]{1,0:T(8,128)(2,1)S(1)} %add_convert_fusion.1.refs_0_), channel_id=1, source_target_pairs={{0,2},{2,0},{4,6},{6,4},{8,10},{10,8},{12,14},{14,12},{16,18},{18,... | collective-permute-start | bytes 786440 | tf_op jit(solution)/shard_map/ppermute | solution.py:586
  112.6 6.5 %collective-permute-start.11 = (bf16[256,512]{1,0:T(8,128)(2,1)S(1)}, bf16[256,512]{1,0:T(8,128)(2,1)S(1)}, u32[]{:S(2)}, u32[]{:S(2)}) collective-permute-start(bf16[256,512]{1,0:T(8,128)(2,1)S(1)} %add_convert_fusion.1.refs_0_), channel_id=1, source_target_pairs={{0,1},{2,3},{4,5},{6,7},{8,9},{10,11},{12,13},{14,15},{16,17},{18,... | collective-permute-start | bytes 786440 | tf_op jit(solution)/shard_map/ppermute | solution.py:587
  113.9 5.2 %collective-permute-start.14 = (bf16[256,512]{1,0:T(8,128)(2,1)S(1)}, bf16[256,512]{1,0:T(8,128)(2,1)S(1)}, u32[]{:S(2)}, u32[]{:S(2)}) collective-permute-start(bf16[256,512]{1,0:T(8,128)(2,1)S(1)} %collective-permute-done.10.refs_3_), channel_id=1, source_target_pairs={{0,1},{2,3},{4,5},{6,7},{8,9},{10,11},{12,13},{14,15},{16,17},{18,... | collective-permute-start | bytes 786440 | tf_op jit(solution)/shard_map/ppermute | solution.py:587
  115.3 3.8 %collective-permute-start.13 = (bf16[256,512]{1,0:T(8,128)(2,1)S(1)}, bf16[256,512]{1,0:T(8,128)(2,1)S(1)}, u32[]{:S(2)}, u32[]{:S(2)}) collective-permute-start(bf16[256,512]{1,0:T(8,128)(2,1)S(1)} %collective-permute-done.9.refs_2_), channel_id=1, source_target_pairs={{0,1},{2,3},{4,5},{6,7},{8,9},{10,11},{12,13},{14,15},{16,17},{18,... | collective-permute-start | bytes 786440 | tf_op jit(solution)/shard_map/ppermute | solution.py:587
  117.8 2.4 %collective-permute-start.12 = (bf16[256,512]{1,0:T(8,128)(2,1)S(1)}, bf16[256,512]{1,0:T(8,128)(2,1)S(1)}, u32[]{:S(2)}, u32[]{:S(2)}) collective-permute-start(bf16[256,512]{1,0:T(8,128)(2,1)S(1)} %collective-permute-done.8.refs_1_), channel_id=1, source_target_pairs={{0,1},{2,3},{4,5},{6,7},{8,9},{10,11},{12,13},{14,15},{16,17},{18,... | collective-permute-start | bytes 786440 | tf_op jit(solution)/shard_map/ppermute | solution.py:587

commit v3 on v2

--- a/solution.py
+++ b/solution.py
@@ -13,8 +13,8 @@
 F32 = jnp.float32
 BF16 = jnp.bfloat16
 LANES = 128
-VMEM_BYTES = 36 * 2**20
-VMEM_SMALL = 20 * 2**20
+VMEM_BYTES = 26 * 2**20
+VMEM_SMALL = 16 * 2**20
 
 
 def dft_tables(size):
@@ -560,20 +560,59 @@
     return [(i, i ^ (2 * stride * shift)) for i in range(0, lax.axis_size(axis), 2)]
 
 
-def summed(given, axis, shape, order, beside, between):
+def paired_kernel(order, given, sibling, *refs):
+    n = len(refs) - 3
+    outs, mine, other, sems = refs[:n], refs[-3], refs[-2], refs[-1]
+    rows = mine.shape[1]
+    copies = []
+    for i in range(n):
+        at = pl.ds(pl.multiple_of(order[i] * rows, 16), rows)
+        copies.append(
+            [
+                pltpu.make_async_copy(given.at[at], mine.at[i], sems.at[0, i]),
+                pltpu.make_async_copy(sibling.at[at], other.at[i], sems.at[1, i]),
+            ]
+        )
+        for copy in copies[-1]:
+            copy.start()
+    for i in range(n):
+        for copy in copies[i]:
+            copy.wait()
+        outs[i][...] = (mine[i].astype(F32) + other[i].astype(F32)).astype(BF16)
+
+
+def paired(given, sibling, order, n):
+    rows, columns = given.shape[0] // n, given.shape[1]
+    hbm = pl.BlockSpec(memory_space=pl.ANY)
+    return pl.pallas_call(
+        paired_kernel,
+        in_specs=[pl.BlockSpec(memory_space=pltpu.SMEM), hbm, hbm],
+        out_specs=[pl.BlockSpec(memory_space=pltpu.VMEM)] * n,
+        out_shape=[jax.ShapeDtypeStruct((rows, columns), BF16)] * n,
+        scratch_shapes=[
+            pltpu.VMEM((n, rows, columns), BF16),
+            pltpu.VMEM((n, rows, columns), BF16),
+            pltpu.SemaphoreType.DMA((2, n)),
+        ],
+        compiler_params=pltpu.CompilerParams(vmem_limit_bytes=VMEM_SMALL),
+        cost_estimate=pl.CostEstimate(flops=10**6, bytes_accessed=3 * 2**20, transcendentals=0),
+        name="paired",
+    )(order, given, sibling)
+
+
+def summed(given, axis, shape, order, beside, during, between):
     length = lax.axis_size(axis)
     near = near_chips(axis)
     far = length // 2 // near
     inward = [(i + 1, i) for i in range(0, length, 2)]
     outward = [(i, i + 1) for i in range(0, length, 2)]
     modes, size, columns = given.shape
-    spot = lax.axis_index(axis) // 2 % near
     sibling = beside(lax.ppermute(given, axis, inward))
-    parts = (given.astype(F32) + sibling.astype(F32)).astype(BF16).reshape(near, modes * size // near, columns)
-    got = [
-        lax.ppermute(lax.dynamic_index_in_dim(parts, spot ^ s, 0, False), axis, hop(axis, s, 1)) for s in range(1, near)
-    ]
-    total = lax.dynamic_index_in_dim(parts, spot, 0, False).astype(F32)
+    flat = (modes * size, columns)
+    parts = paired(given.reshape(flat), sibling.reshape(flat), order, near)
+    got = [lax.ppermute(parts[s], axis, hop(axis, s, 1)) for s in range(1, near)]
+    got[0] = during(got[0])
+    total = parts[0].astype(F32)
     for piece in got:
         total = total + piece.astype(F32)
     sent = total.astype(BF16)
@@ -596,7 +635,7 @@
     rows, _, width = object_tiles.shape
     modes, size = probe.shape[:2]
     tables = dft_tables(size)
-    bounds = column_bounds(width, (0.5625,))
+    bounds = column_bounds(width, (0.3125, 0.625))
     stages = len(bounds) - 1
     rims = [
         passed_along(object_tiles[:size, :, low:high].reshape(size, 2 * (high - low)), "row", -1)
@@ -616,11 +655,19 @@
         grads.append(grad)
         carried = [moved] + rest
     given = carried[1]
-    below = settle(places, grads, bounds, 0, width, size, BF16, width, "below_rows")
+    edges = (0, width // 2 // LANES * LANES, width)
+    belows = [
+        settle(places, grads, bounds, low, high, size, BF16, width, f"below_{low}")
+        for low, high in zip(edges[:-1], edges[1:])
+    ]
     held = {}
 
     def beside(x):
-        x, held["below"] = lax.optimization_barrier((x, below))
+        x, held[0] = lax.optimization_barrier((x, belows[0]))
+        return x
+
+    def during(x):
+        x, held[1] = lax.optimization_barrier((x, belows[1]))
         return x
 
     def between(x):
@@ -628,9 +675,9 @@
         x, held["own"] = lax.optimization_barrier((x, own_rows))
         return x
 
-    probe_grad = summed(given, "row", probe.shape, order, beside, between)
-    above = passed_along(held["below"], "row", 1)
-    object_grad = finish(held["own"], [above], (0, width), width)
+    probe_grad = summed(given, "row", probe.shape, order, beside, during, between)
+    aboves = [passed_along(held[i], "row", 1) for i in range(2)]
+    object_grad = finish(held["own"], aboves, edges, width)
     return object_grad, probe_grad, moved
 
 

time: 129 us -> 130 us (level)
  the two profiles are of different devices: /device:TPU:0 before, /device:TPU:16 now
where the time goes in v3:
time: 130 us; the launch traced here: 129 us
  starting transfers between devices  50.5 us (39%)
  Pallas kernels  41.7 us (32%)
  waiting for transfers between devices  20.4 us (16%)
  local copies, waits for them, and re-layouts  14.5 us (11%)
  between operations  1.89 us (1%)
    pallas_call x3, Pallas kernels, project(): pl.pallas_call(functools.partial(project_kernel, size, width, bounds, sta...  23.3 us
    ppermute x3, starting transfers between devices, summed(): lax.ppermute(parts[s], axis, hop(axis, s, 1))  18.3 us
    ppermute x3, waiting for transfers between devices, summed(): lax.ppermute(total, axis, hop(axis, s, 1))  17.3 us
    ppermute x5, starting transfers between devices, passed_along(): return lax.ppermute(x, axis, pairs)  14.3 us
    pallas_call x3, Pallas kernels, settle(): pl.pallas_call(functools.partial(settle_kernel, size, bounds, low, high,...  12.4 us
    ppermute x3, starting transfers between devices, summed(): lax.ppermute(total, axis, hop(axis, s, 1))  9.21 us
    unnamed x18, local copies, waits for them, and re-layouts  8.03 us
    ppermute x4, starting transfers between devices, summed(): others = [lax.ppermute(piece, axis, outward) for piece in pieces]  5.21 us
  transfers between devices with their start and end apart: 17, of which 4 were waited for; matrix products, arithmetic and copies ran while one was open for 7% of the time, Pallas kernels for 18%

profile of v3, /device:TPU:16, one launch (start us, length us, event | category | flops | bytes accessed | tf_op | source)
XLA Modules:
  0.0 129.2 jit_solution(301022510075922126)
XLA Ops:
  0.6 2.2 %fusion.1 = (bf16[256,2,640]{2,1,0:T(2,128)(2,1)S(1)}, bf16[256,2,640]{2,1,0:T(2,128)(2,1)S(1)}) fusion(bf16[256,2,2048]{2,1,0:T(2,128)(2,1)} %param.8), kind=kLoop, calls=%fused_computation.3 | loop fusion | bytes 2621440 | tf_op jit(solution)/shard_map/slice | solution.py:641
  3.8 2.7 %collective-permute-start.2 = (bf16[256,1280]{1,0:T(8,128)(2,1)}, bf16[256,1280]{1,0:T(8,128)(2,1)}, u32[]{:S(2)}, u32[]{:S(2)}) collective-permute-start(bf16[256,1280]{1,0:T(8,128)(2,1)} %bitcast.18), channel_id=1, source_target_pairs={{1,0},{2,1},{3,2},{4,3},{5,4},{6,5},{7,6},{8,7},{9,8},{10,9},{11,1... | collective-permute-start | bytes 1966088 | tf_op jit(solution)/shard_map/ppermute | solution.py:491
  7.4 2.6 %collective-permute-start.1 = (bf16[256,1280]{1,0:T(8,128)(2,1)}, bf16[256,1280]{1,0:T(8,128)(2,1)S(1)}, u32[]{:S(2)}, u32[]{:S(2)}) collective-permute-start(bf16[256,1280]{1,0:T(8,128)(2,1)} %bitcast.16), channel_id=1, source_target_pairs={{1,0},{2,1},{3,2},{4,3},{5,4},{6,5},{7,6},{8,7},{9,8},{10,9},{11,1... | collective-permute-start | bytes 1966088 | tf_op jit(solution)/shard_map/ppermute | solution.py:491
  11.0 1.9 %collective-permute-start = (bf16[256,1536]{1,0:T(8,128)(2,1)}, bf16[256,1536]{1,0:T(8,128)(2,1)}, u32[]{:S(2)}, u32[]{:S(2)}) collective-permute-start(bf16[256,1536]{1,0:T(8,128)(2,1)} %bitcast.14), channel_id=1, source_target_pairs={{1,0},{2,1},{3,2},{4,3},{5,4},{6,5},{7,6},{8,7},{9,8},{10,9},{11,1... | collective-permute-start | bytes 2359304 | tf_op jit(solution)/shard_map/ppermute | solution.py:491
  13.7 2.5 %copy.11 = bf16[32,8,2,2048]{3,1,2,0:T(8,128)(2,1)S(1)} copy(bf16[32,8,2,2048]{3,2,1,0:T(2,128)(2,1)} %bitcast.25) | data formatting | bytes 4194304
  16.2 4.1 %reshape.33.refs_2_.refs_3_ = f32[4,256,512]{2,1,0:T(8,128)} reshape(f32[4,256,2,256]{3,2,1,0:T(2,128)} %param.9) | data formatting | bytes 4194304 | tf_op jit(solution)/shard_map/reshape | solution.py:650
  20.4 1.6 %copy-done = f32[4,256,512]{2,1,0:T(8,128)S(1)} copy-done((f32[4,256,512]{2,1,0:T(8,128)S(1)}, f32[4,256,512]{2,1,0:T(8,128)}, u32[]{:S(2)}) %copy-start) | copy-done | bytes 2097176
  21.9 1.1 copy-done.2
  23.1 2.7 %project_0.1 = (f32[2,6]{1,0:T(2,128)S(1)}, bf16[6,256,512]{2,1,0:T(8,128)(2,1)S(1)}, f32[4,256,512]{2,1,0:T(8,128)S(1)}) custom-call(s32[5,6]{1,0:T(8,128)S(1)} %stack.33.places, bf16[256,4096]{1,0:T(8,128)(2,1)S(1)} %bitcast.20, bf16[256,1280]{1,0:T(8,128)(2,1)} %collective-permute-done.2.refs_1_.refs_2_, f32[4,256,512]{2,1,0:T(8,128)S(1)} %copy-done, ...), custom_call_target="tpu_custom_call" | custom-call | flops 8000000000 | bytes 16777216 | tf_op jit(solution)/shard_map/project_0/pallas_call | solution.py:343
  25.8 6.5 %project_1.1 = (f32[2,6]{1,0:T(2,128)S(1)}, bf16[6,256,512]{2,1,0:T(8,128)(2,1)S(1)}, f32[4,256,512]{2,1,0:T(8,128)S(1)}) custom-call(s32[5,6]{1,0:T(8,128)S(1)} %stack.33.places, bf16[256,4096]{1,0:T(8,128)(2,1)S(1)} %bitcast.21, bf16[256,1280]{1,0:T(8,128)(2,1)S(1)} %collective-permute-done.1.refs_1_.refs_2_, ...), custom_call_target="tpu_custom_call" | custom-call | flops 8000000000 | bytes 16777216 | tf_op jit(solution)/shard_map/project_1/pallas_call | solution.py:343
  32.3 14.1 %project_2.1 = (f32[2,6]{1,0:T(2,128)}, bf16[6,256,512]{2,1,0:T(8,128)(2,1)S(1)}, bf16[4,256,512]{2,1,0:T(8,128)(2,1)S(1)}) custom-call(s32[5,6]{1,0:T(8,128)S(1)} %stack.33.places, bf16[256,4096]{1,0:T(8,128)(2,1)S(1)} %bitcast.22, bf16[256,1536]{1,0:T(8,128)(2,1)} %collective-permute-done.refs_1_, ...), custom_call_target="tpu_custom_call" | custom-call | flops 8000000000 | bytes 16777216 | tf_op jit(solution)/shard_map/project_2/pallas_call | solution.py:343
  46.4 1.5 %collective-permute-start.3 = (bf16[4,256,512]{2,1,0:T(8,128)(2,1)S(1)}, bf16[4,256,512]{2,1,0:T(8,128)(2,1)S(1)}, u32[]{:S(2)}, u32[]{:S(2)}) collective-permute-start(bf16[4,256,512]{2,1,0:T(8,128)(2,1)S(1)} %get-tuple-element.30), channel_id=1, source_target_pairs={{1,0},{3,2},{5,4},{7,6},{9,8},{11,10},{13,12},{15,14},{17,16},{19,... | collective-permute-start | bytes 3145736 | tf_op jit(solution)/shard_map/ppermute | solution.py:610
  47.9 2.5 %below_0.1 = bf16[256,2048]{1,0:T(8,128)(2,1)S(1)} custom-call(s32[5,6]{1,0:T(8,128)S(1)} %stack.33.places, bf16[6,256,512]{2,1,0:T(8,128)(2,1)S(1)} %get-tuple-element.31.refs_0_, bf16[6,256,512]{2,1,0:T(8,128)(2,1)S(1)} %get-tuple-element.32.refs_1_, bf16[6,256,512]{2,1,0:T(8,128)(2,1)S(1)} %get-tuple-element.33.refs_2_), custom_call_target="tpu_custom_call" | custom-call | flops 1000000000 | bytes 8388608 | tf_op jit(solution)/shard_map/below_0/pallas_call | solution.py:425
  52.0 13.0 %collective-permute-start.4 = (bf16[256,512]{1,0:T(8,128)(2,1)S(1)}, bf16[256,512]{1,0:T(8,128)(2,1)S(1)}, u32[]{:S(2)}, u32[]{:S(2)}) collective-permute-start(bf16[256,512]{1,0:T(8,128)(2,1)S(1)} %get-tuple-element.36), channel_id=1, source_target_pairs={{0,2},{2,0},{4,6},{6,4},{8,10},{10,8},{12,14},{14,12},{16,18},{18,... | collective-permute-start | bytes 786440 | tf_op jit(solution)/shard_map/ppermute | solution.py:613
  65.0 1.9 %collective-permute-start.5 = (bf16[256,512]{1,0:T(8,128)(2,1)S(1)}, bf16[256,512]{1,0:T(8,128)(2,1)S(1)}, u32[]{:S(2)}, u32[]{:S(2)}) collective-permute-start(bf16[256,512]{1,0:T(8,128)(2,1)S(1)} %get-tuple-element.38), channel_id=1, source_target_pairs={{0,4},{2,6},{4,0},{6,2},{8,12},{10,14},{12,8},{14,10},{16,20},{18,... | collective-permute-start | bytes 786440 | tf_op jit(solution)/shard_map/ppermute | solution.py:613
  67.0 3.4 %collective-permute-start.6 = (bf16[256,512]{1,0:T(8,128)(2,1)S(1)}, bf16[256,512]{1,0:T(8,128)(2,1)S(1)}, u32[]{:S(2)}, u32[]{:S(2)}) collective-permute-start(bf16[256,512]{1,0:T(8,128)(2,1)S(1)} %get-tuple-element.39), channel_id=1, source_target_pairs={{0,6},{2,4},{4,2},{6,0},{8,14},{10,12},{12,10},{14,8},{16,22},{18,... | collective-permute-start | bytes 786440 | tf_op jit(solution)/shard_map/ppermute | solution.py:613
  70.3 4.3 %below_1024.1 = bf16[256,2048]{1,0:T(8,128)(2,1)S(1)} custom-call(s32[5,6]{1,0:T(8,128)S(1)} %stack.33.places, bf16[6,256,512]{2,1,0:T(8,128)(2,1)S(1)} %get-tuple-element.31.refs_0_, bf16[6,256,512]{2,1,0:T(8,128)(2,1)S(1)} %get-tuple-element.32.refs_1_, bf16[6,256,512]{2,1,0:T(8,128)(2,1)S(1)} %get-tuple-element.33.refs_2_), custom_call_target="tpu_custom_call" | custom-call | flops 1000000000 | bytes 8388608 | tf_op jit(solution)/shard_map/below_1024/pallas_call | solution.py:425
  74.7 1.5 %collective-permute-done.6 = bf16[256,512]{1,0:T(8,128)(2,1)S(1)} collective-permute-done((bf16[256,512]{1,0:T(8,128)(2,1)S(1)}, bf16[256,512]{1,0:T(8,128)(2,1)S(1)}, u32[]{:S(2)}, u32[]{:S(2)}) %collective-permute-start.6) | collective-permute-done | bytes 262176 | tf_op jit(solution)/shard_map/ppermute | solution.py:613
  76.3 1.9 %collective-permute-start.7 = (bf16[256,512]{1,0:T(8,128)(2,1)S(1)}, bf16[256,512]{1,0:T(8,128)(2,1)S(1)}, u32[]{:S(2)}, u32[]{:S(2)}) collective-permute-start(bf16[256,512]{1,0:T(8,128)(2,1)S(1)} %fusion), channel_id=1, source_target_pairs={{0,8},{2,10},{4,12},{6,14},{8,0},{10,2},{12,4},{14,6},{16,24},{18,... | collective-permute-start | bytes 786440 | tf_op jit(solution)/shard_map/ppermute | solution.py:619
  78.2 5.6 %own_rows.1.own = f32[256,4096]{1,0:T(8,128)S(1)} custom-call(s32[5,6]{1,0:T(8,128)S(1)} %stack.33.places, bf16[6,256,512]{2,1,0:T(8,128)(2,1)S(1)} %get-tuple-element.31.refs_0_, bf16[6,256,512]{2,1,0:T(8,128)(2,1)S(1)} %get-tuple-element.32.refs_1_, bf16[6,256,512]{2,1,0:T(8,128)(2,1)S(1)} %get-tuple-element.33.refs_2_), custom_call_target="tpu_custom_call" | custom-call | flops 1000000000 | bytes 8388608 | tf_op jit(solution)/shard_map/own_rows/pallas_call | solution.py:425
  83.8 1.9 %collective-permute-start.8 = (bf16[256,2048]{1,0:T(8,128)(2,1)S(1)}, bf16[256,2048]{1,0:T(8,128)(2,1)S(1)}, u32[]{:S(2)}, u32[]{:S(2)}) collective-permute-start(bf16[256,2048]{1,0:T(8,128)(2,1)S(1)} %below_0.1), channel_id=1, source_target_pairs={{0,1},{1,2},{2,3},{3,4},{4,5},{5,6},{6,7},{7,8},{8,9},{9,10},{10,1... | collective-permute-start | bytes 3145736 | tf_op jit(solution)/shard_map/ppermute | solution.py:491
  85.8 5.2 %collective-permute-start.9 = (bf16[256,2048]{1,0:T(8,128)(2,1)S(1)}, bf16[256,2048]{1,0:T(8,128)(2,1)S(1)}, u32[]{:S(2)}, u32[]{:S(2)}) collective-permute-start(bf16[256,2048]{1,0:T(8,128)(2,1)S(1)} %below_1024.1), channel_id=1, source_target_pairs={{0,1},{1,2},{2,3},{3,4},{4,5},{5,6},{6,7},{7,8},{8,9},{9,10},{10,1... | collective-permute-start | bytes 3145736 | tf_op jit(solution)/shard_map/ppermute | solution.py:491
  91.2 1.9 %collective-permute-start.10 = (bf16[256,512]{1,0:T(8,128)(2,1)S(1)}, bf16[256,512]{1,0:T(8,128)(2,1)S(1)}, u32[]{:S(2)}, u32[]{:S(2)}) collective-permute-start(bf16[256,512]{1,0:T(8,128)(2,1)S(1)} %add_convert_fusion.refs_0_), channel_id=1, source_target_pairs={{0,2},{2,0},{4,6},{6,4},{8,10},{10,8},{12,14},{14,12},{16,18},{18,... | collective-permute-start | bytes 786440 | tf_op jit(solution)/shard_map/ppermute | solution.py:625
  93.1 1.9 %collective-permute-start.11 = (bf16[256,512]{1,0:T(8,128)(2,1)S(1)}, bf16[256,512]{1,0:T(8,128)(2,1)S(1)}, u32[]{:S(2)}, u32[]{:S(2)}) collective-permute-start(bf16[256,512]{1,0:T(8,128)(2,1)S(1)} %add_convert_fusion.refs_0_), channel_id=1, source_target_pairs={{0,4},{2,6},{4,0},{6,2},{8,12},{10,14},{12,8},{14,10},{16,20},{18,... | collective-permute-start | bytes 786440 | tf_op jit(solution)/shard_map/ppermute | solution.py:625
  95.0 5.4 %collective-permute-start.12 = (bf16[256,512]{1,0:T(8,128)(2,1)S(1)}, bf16[256,512]{1,0:T(8,128)(2,1)S(1)}, u32[]{:S(2)}, u32[]{:S(2)}) collective-permute-start(bf16[256,512]{1,0:T(8,128)(2,1)S(1)} %add_convert_fusion.refs_0_), channel_id=1, source_target_pairs={{0,6},{2,4},{4,2},{6,0},{8,14},{10,12},{12,10},{14,8},{16,22},{18,... | collective-permute-start | bytes 786440 | tf_op jit(solution)/shard_map/ppermute | solution.py:625
  100.4 17.3 %collective-permute-done.10.refs_1_ = bf16[256,512]{1,0:T(8,128)(2,1)S(1)} collective-permute-done((bf16[256,512]{1,0:T(8,128)(2,1)S(1)}, bf16[256,512]{1,0:T(8,128)(2,1)S(1)}, u32[]{:S(2)}, u32[]{:S(2)}) %collective-permute-start.10) | collective-permute-done | bytes 262176 | tf_op jit(solution)/shard_map/ppermute | solution.py:625
  117.7 1.3 %collective-permute-start.13 = (bf16[256,512]{1,0:T(8,128)(2,1)S(1)}, bf16[256,512]{1,0:T(8,128)(2,1)S(1)}, u32[]{:S(2)}, u32[]{:S(2)}) collective-permute-start(bf16[256,512]{1,0:T(8,128)(2,1)S(1)} %add_convert_fusion.refs_0_), channel_id=1, source_target_pairs={{0,1},{2,3},{4,5},{6,7},{8,9},{10,11},{12,13},{14,15},{16,17},{18,... | collective-permute-start | bytes 786440 | tf_op jit(solution)/shard_map/ppermute | solution.py:626
  119.0 1.3 %collective-permute-start.14 = (bf16[256,512]{1,0:T(8,128)(2,1)S(1)}, bf16[256,512]{1,0:T(8,128)(2,1)S(1)}, u32[]{:S(2)}, u32[]{:S(2)}) collective-permute-start(bf16[256,512]{1,0:T(8,128)(2,1)S(1)} %collective-permute-done.10.refs_1_), channel_id=1, source_target_pairs={{0,1},{2,3},{4,5},{6,7},{8,9},{10,11},{12,13},{14,15},{16,17},{18,... | collective-permute-start | bytes 786440 | tf_op jit(solution)/shard_map/ppermute | solution.py:626
  120.3 1.3 %collective-permute-start.15 = (bf16[256,512]{1,0:T(8,128)(2,1)S(1)}, bf16[256,512]{1,0:T(8,128)(2,1)S(1)}, u32[]{:S(2)}, u32[]{:S(2)}) collective-permute-start(bf16[256,512]{1,0:T(8,128)(2,1)S(1)} %collective-permute-done.11.refs_2_), channel_id=1, source_target_pairs={{0,1},{2,3},{4,5},{6,7},{8,9},{10,11},{12,13},{14,15},{16,17},{18,... | collective-permute-start | bytes 786440 | tf_op jit(solution)/shard_map/ppermute | solution.py:626
  121.7 1.3 %collective-permute-start.16 = (bf16[256,512]{1,0:T(8,128)(2,1)S(1)}, bf16[256,512]{1,0:T(8,128)(2,1)S(1)}, u32[]{:S(2)}, u32[]{:S(2)}) collective-permute-start(bf16[256,512]{1,0:T(8,128)(2,1)S(1)} %collective-permute-done.12.refs_3_), channel_id=1, source_target_pairs={{0,1},{2,3},{4,5},{6,7},{8,9},{10,11},{12,13},{14,15},{16,17},{18,... | collective-permute-start | bytes 786440 | tf_op jit(solution)/shard_map/ppermute | solution.py:626
  124.1 2.1 %unpack.1 = f32[4,256,2,256]{3,2,1,0:T(2,128)} custom-call(s32[5]{0:T(128)S(1)} %stack.39.order, bf16[256,512]{1,0:T(8,128)(2,1)S(1)} %add_convert_fusion.refs_0_, bf16[256,512]{1,0:T(8,128)(2,1)S(1)} %collective-permute-done.10.refs_1_, bf16[256,512]{1,0:T(8,128)(2,1)S(1)} %collective-permute-done.11.refs_2_, ...), custom_call_target="tpu_custom_call" | custom-call | flops 1000000 | bytes 4194304 | tf_op jit(solution)/shard_map/unpack/pallas_call | solution.py:532
  126.2 2.8 %finish.1 = f32[256,2,2048]{2,1,0:T(2,128)} custom-call(f32[256,4096]{1,0:T(8,128)S(1)} %own_rows.1.own, bf16[256,2048]{1,0:T(8,128)(2,1)S(1)} %collective-permute-done.8.refs_0_, bf16[256,2048]{1,0:T(8,128)(2,1)S(1)} %collective-permute-done.9.refs_1_), custom_call_target="tpu_custom_call" | custom-call | flops 1000000 | bytes 10485760 | tf_op jit(solution)/shard_map/finish/pallas_call | solution.py:474
  (39 shorter events, 5.9 us)
Async XLA Ops:
  2.8 7.2 %slice-start = ((bf16[256,2,2048]{2,1,0:T(2,128)(2,1)}), bf16[256,2,768]{2,1,0:T(2,128)(2,1)S(1)}, s32[]{:S(2)}) async-start(bf16[256,2,2048]{2,1,0:T(2,128)(2,1)} %param.8), calls=%async_computation | async-start | bytes 1572864 | tf_op jit(solution)/shard_map/slice | solution.py:641
  3.8 16.6 %collective-permute-start.2 = (bf16[256,1280]{1,0:T(8,128)(2,1)}, bf16[256,1280]{1,0:T(8,128)(2,1)}, u32[]{:S(2)}, u32[]{:S(2)}) collective-permute-start(bf16[256,1280]{1,0:T(8,128)(2,1)} %bitcast.18), channel_id=1, source_target_pairs={{1,0},{2,1},{3,2},{4,3},{5,4},{6,5},{7,6},{8,7},{9,8},{10,9},{11,1... | collective-permute-start | bytes 1966088 | tf_op jit(solution)/shard_map/ppermute | solution.py:491
  6.5 7.2 %copy-start.4 = (s32[6]{0:T(128)S(1)}, s32[6]{0:T(128)}, u32[]{:S(2)}) copy-start(s32[6]{0:T(128)} %param.11) | copy-start | bytes 76
  6.5 7.2 %copy-start.5 = (s32[6]{0:T(128)S(1)}, s32[6]{0:T(128)}, u32[]{:S(2)}) copy-start(s32[6]{0:T(128)} %param.12) | copy-start | bytes 76
  6.5 7.2 %copy-start.6 = (s32[6]{0:T(128)S(1)}, s32[6]{0:T(128)}, u32[]{:S(2)}) copy-start(s32[6]{0:T(128)} %param.13) | copy-start | bytes 76
  7.4 18.3 %collective-permute-start.1 = (bf16[256,1280]{1,0:T(8,128)(2,1)}, bf16[256,1280]{1,0:T(8,128)(2,1)S(1)}, u32[]{:S(2)}, u32[]{:S(2)}) collective-permute-start(bf16[256,1280]{1,0:T(8,128)(2,1)} %bitcast.16), channel_id=1, source_target_pairs={{1,0},{2,1},{3,2},{4,3},{5,4},{6,5},{7,6},{8,7},{9,8},{10,9},{11,1... | collective-permute-start | bytes 1966088 | tf_op jit(solution)/shard_map/ppermute | solution.py:491
  11.0 21.3 %collective-permute-start = (bf16[256,1536]{1,0:T(8,128)(2,1)}, bf16[256,1536]{1,0:T(8,128)(2,1)}, u32[]{:S(2)}, u32[]{:S(2)}) collective-permute-start(bf16[256,1536]{1,0:T(8,128)(2,1)} %bitcast.14), channel_id=1, source_target_pairs={{1,0},{2,1},{3,2},{4,3},{5,4},{6,5},{7,6},{8,7},{9,8},{10,9},{11,1... | collective-permute-start | bytes 2359304 | tf_op jit(solution)/shard_map/ppermute | solution.py:491
  16.2 4.1 %copy-start.1 = (bf16[6,256,256]{2,1,0:T(8,128)(2,1)S(1)}, bf16[6,256,256]{2,1,0:T(8,128)(2,1)}, u32[]{:S(2)}) copy-start(bf16[6,256,256]{2,1,0:T(8,128)(2,1)} %refs_4_.4) | copy-start | bytes 2359300
  20.3 1.6 %copy-start = (f32[4,256,512]{2,1,0:T(8,128)S(1)}, f32[4,256,512]{2,1,0:T(8,128)}, u32[]{:S(2)}) copy-start(f32[4,256,512]{2,1,0:T(8,128)} %reshape.33.refs_2_.refs_3_) | copy-start | bytes 6291460
  21.9 1.1 copy-start.2
  23.1 2.7 %copy-start.3 = (bf16[6,256,256]{2,1,0:T(8,128)(2,1)S(1)}, bf16[6,256,256]{2,1,0:T(8,128)(2,1)}, u32[]{:S(2)}) copy-start(bf16[6,256,256]{2,1,0:T(8,128)(2,1)} %constant.44.clone.refs_4_.refs_5_) | copy-start | bytes 2359300
  46.4 4.6 %collective-permute-start.3 = (bf16[4,256,512]{2,1,0:T(8,128)(2,1)S(1)}, bf16[4,256,512]{2,1,0:T(8,128)(2,1)S(1)}, u32[]{:S(2)}, u32[]{:S(2)}) collective-permute-start(bf16[4,256,512]{2,1,0:T(8,128)(2,1)S(1)} %get-tuple-element.30), channel_id=1, source_target_pairs={{1,0},{3,2},{5,4},{7,6},{9,8},{11,10},{13,12},{15,14},{17,16},{19,... | collective-permute-start | bytes 3145736 | tf_op jit(solution)/shard_map/ppermute | solution.py:610
  52.0 22.6 %collective-permute-start.4 = (bf16[256,512]{1,0:T(8,128)(2,1)S(1)}, bf16[256,512]{1,0:T(8,128)(2,1)S(1)}, u32[]{:S(2)}, u32[]{:S(2)}) collective-permute-start(bf16[256,512]{1,0:T(8,128)(2,1)S(1)} %get-tuple-element.36), channel_id=1, source_target_pairs={{0,2},{2,0},{4,6},{6,4},{8,10},{10,8},{12,14},{14,12},{16,18},{18,... | collective-permute-start | bytes 786440 | tf_op jit(solution)/shard_map/ppermute | solution.py:613
  65.0 9.6 %collective-permute-start.5 = (bf16[256,512]{1,0:T(8,128)(2,1)S(1)}, bf16[256,512]{1,0:T(8,128)(2,1)S(1)}, u32[]{:S(2)}, u32[]{:S(2)}) collective-permute-start(bf16[256,512]{1,0:T(8,128)(2,1)S(1)} %get-tuple-element.38), channel_id=1, source_target_pairs={{0,4},{2,6},{4,0},{6,2},{8,12},{10,14},{12,8},{14,10},{16,20},{18,... | collective-permute-start | bytes 786440 | tf_op jit(solution)/shard_map/ppermute | solution.py:613
  67.0 9.2 %collective-permute-start.6 = (bf16[256,512]{1,0:T(8,128)(2,1)S(1)}, bf16[256,512]{1,0:T(8,128)(2,1)S(1)}, u32[]{:S(2)}, u32[]{:S(2)}) collective-permute-start(bf16[256,512]{1,0:T(8,128)(2,1)S(1)} %get-tuple-element.39), channel_id=1, source_target_pairs={{0,6},{2,4},{4,2},{6,0},{8,14},{10,12},{12,10},{14,8},{16,22},{18,... | collective-permute-start | bytes 786440 | tf_op jit(solution)/shard_map/ppermute | solution.py:613
  76.3 14.7 %collective-permute-start.7 = (bf16[256,512]{1,0:T(8,128)(2,1)S(1)}, bf16[256,512]{1,0:T(8,128)(2,1)S(1)}, u32[]{:S(2)}, u32[]{:S(2)}) collective-permute-start(bf16[256,512]{1,0:T(8,128)(2,1)S(1)} %fusion), channel_id=1, source_target_pairs={{0,8},{2,10},{4,12},{6,14},{8,0},{10,2},{12,4},{14,6},{16,24},{18,... | collective-permute-start | bytes 786440 | tf_op jit(solution)/shard_map/ppermute | solution.py:619
  83.8 42.4 %collective-permute-start.8 = (bf16[256,2048]{1,0:T(8,128)(2,1)S(1)}, bf16[256,2048]{1,0:T(8,128)(2,1)S(1)}, u32[]{:S(2)}, u32[]{:S(2)}) collective-permute-start(bf16[256,2048]{1,0:T(8,128)(2,1)S(1)} %below_0.1), channel_id=1, source_target_pairs={{0,1},{1,2},{2,3},{3,4},{4,5},{5,6},{6,7},{7,8},{8,9},{9,10},{10,1... | collective-permute-start | bytes 3145736 | tf_op jit(solution)/shard_map/ppermute | solution.py:491
  85.8 40.5 %collective-permute-start.9 = (bf16[256,2048]{1,0:T(8,128)(2,1)S(1)}, bf16[256,2048]{1,0:T(8,128)(2,1)S(1)}, u32[]{:S(2)}, u32[]{:S(2)}) collective-permute-start(bf16[256,2048]{1,0:T(8,128)(2,1)S(1)} %below_1024.1), channel_id=1, source_target_pairs={{0,1},{1,2},{2,3},{3,4},{4,5},{5,6},{6,7},{7,8},{8,9},{9,10},{10,1... | collective-permute-start | bytes 3145736 | tf_op jit(solution)/shard_map/ppermute | solution.py:491
  91.2 26.5 %collective-permute-start.10 = (bf16[256,512]{1,0:T(8,128)(2,1)S(1)}, bf16[256,512]{1,0:T(8,128)(2,1)S(1)}, u32[]{:S(2)}, u32[]{:S(2)}) collective-permute-start(bf16[256,512]{1,0:T(8,128)(2,1)S(1)} %add_convert_fusion.refs_0_), channel_id=1, source_target_pairs={{0,2},{2,0},{4,6},{6,4},{8,10},{10,8},{12,14},{14,12},{16,18},{18,... | collective-permute-start | bytes 786440 | tf_op jit(solution)/shard_map/ppermute | solution.py:625
  93.1 25.9 %collective-permute-start.11 = (bf16[256,512]{1,0:T(8,128)(2,1)S(1)}, bf16[256,512]{1,0:T(8,128)(2,1)S(1)}, u32[]{:S(2)}, u32[]{:S(2)}) collective-permute-start(bf16[256,512]{1,0:T(8,128)(2,1)S(1)} %add_convert_fusion.refs_0_), channel_id=1, source_target_pairs={{0,4},{2,6},{4,0},{6,2},{8,12},{10,14},{12,8},{14,10},{16,20},{18,... | collective-permute-start | bytes 786440 | tf_op jit(solution)/shard_map/ppermute | solution.py:625
  95.0 25.3 %collective-permute-start.12 = (bf16[256,512]{1,0:T(8,128)(2,1)S(1)}, bf16[256,512]{1,0:T(8,128)(2,1)S(1)}, u32[]{:S(2)}, u32[]{:S(2)}) collective-permute-start(bf16[256,512]{1,0:T(8,128)(2,1)S(1)} %add_convert_fusion.refs_0_), channel_id=1, source_target_pairs={{0,6},{2,4},{4,2},{6,0},{8,14},{10,12},{12,10},{14,8},{16,22},{18,... | collective-permute-start | bytes 786440 | tf_op jit(solution)/shard_map/ppermute | solution.py:625
  117.7 4.0 %collective-permute-start.13 = (bf16[256,512]{1,0:T(8,128)(2,1)S(1)}, bf16[256,512]{1,0:T(8,128)(2,1)S(1)}, u32[]{:S(2)}, u32[]{:S(2)}) collective-permute-start(bf16[256,512]{1,0:T(8,128)(2,1)S(1)} %add_convert_fusion.refs_0_), channel_id=1, source_target_pairs={{0,1},{2,3},{4,5},{6,7},{8,9},{10,11},{12,13},{14,15},{16,17},{18,... | collective-permute-start | bytes 786440 | tf_op jit(solution)/shard_map/ppermute | solution.py:626
  119.0 4.0 %collective-permute-start.14 = (bf16[256,512]{1,0:T(8,128)(2,1)S(1)}, bf16[256,512]{1,0:T(8,128)(2,1)S(1)}, u32[]{:S(2)}, u32[]{:S(2)}) collective-permute-start(bf16[256,512]{1,0:T(8,128)(2,1)S(1)} %collective-permute-done.10.refs_1_), channel_id=1, source_target_pairs={{0,1},{2,3},{4,5},{6,7},{8,9},{10,11},{12,13},{14,15},{16,17},{18,... | collective-permute-start | bytes 786440 | tf_op jit(solution)/shard_map/ppermute | solution.py:626
  120.3 2.7 %collective-permute-start.15 = (bf16[256,512]{1,0:T(8,128)(2,1)S(1)}, bf16[256,512]{1,0:T(8,128)(2,1)S(1)}, u32[]{:S(2)}, u32[]{:S(2)}) collective-permute-start(bf16[256,512]{1,0:T(8,128)(2,1)S(1)} %collective-permute-done.11.refs_2_), channel_id=1, source_target_pairs={{0,1},{2,3},{4,5},{6,7},{8,9},{10,11},{12,13},{14,15},{16,17},{18,... | collective-permute-start | bytes 786440 | tf_op jit(solution)/shard_map/ppermute | solution.py:626
  121.7 2.4 %collective-permute-start.16 = (bf16[256,512]{1,0:T(8,128)(2,1)S(1)}, bf16[256,512]{1,0:T(8,128)(2,1)S(1)}, u32[]{:S(2)}, u32[]{:S(2)}) collective-permute-start(bf16[256,512]{1,0:T(8,128)(2,1)S(1)} %collective-permute-done.12.refs_3_), channel_id=1, source_target_pairs={{0,1},{2,3},{4,5},{6,7},{8,9},{10,11},{12,13},{14,15},{16,17},{18,... | collective-permute-start | bytes 786440 | tf_op jit(solution)/shard_map/ppermute | solution.py:626

commit v4 on v3

--- a/solution.py
+++ b/solution.py
@@ -600,7 +600,7 @@
     )(order, given, sibling)
 
 
-def summed(given, axis, shape, order, beside, during, between):
+def summed(given, axis, shape, order, beside, during, between, last):
     length = lax.axis_size(axis)
     near = near_chips(axis)
     far = length // 2 // near
@@ -611,7 +611,7 @@
     flat = (modes * size, columns)
     parts = paired(given.reshape(flat), sibling.reshape(flat), order, near)
     got = [lax.ppermute(parts[s], axis, hop(axis, s, 1)) for s in range(1, near)]
-    got[0] = during(got[0])
+    got = during(got)
     total = parts[0].astype(F32)
     for piece in got:
         total = total + piece.astype(F32)
@@ -624,7 +624,7 @@
     total = total.astype(BF16)
     pieces = [total] + [lax.ppermute(total, axis, hop(axis, s, 1)) for s in range(1, near)]
     others = [lax.ppermute(piece, axis, outward) for piece in pieces]
-    return unpacked(pieces, others, order, shape)
+    return unpacked(pieces, others, last(order), shape)
 
 
 def column_bounds(width, shares):
@@ -635,7 +635,7 @@
     rows, _, width = object_tiles.shape
     modes, size = probe.shape[:2]
     tables = dft_tables(size)
-    bounds = column_bounds(width, (0.3125, 0.625))
+    bounds = column_bounds(width, (0.4375, 0.75))
     stages = len(bounds) - 1
     rims = [
         passed_along(object_tiles[:size, :, low:high].reshape(size, 2 * (high - low)), "row", -1)
@@ -660,24 +660,29 @@
         settle(places, grads, bounds, low, high, size, BF16, width, f"below_{low}")
         for low, high in zip(edges[:-1], edges[1:])
     ]
+    aboves = [passed_along(belows[0], "row", 1)]
     held = {}
 
     def beside(x):
-        x, held[0] = lax.optimization_barrier((x, belows[0]))
+        return lax.optimization_barrier((x, belows[0]))[0]
+
+    def during(x):
+        x, aboves[0], held["below"] = lax.optimization_barrier((x, aboves[0], belows[1]))
         return x
 
-    def during(x):
-        x, held[1] = lax.optimization_barrier((x, belows[1]))
+    def between(x):
+        aboves.append(passed_along(held["below"], "row", 1))
+        own_rows = settle(places, grads, bounds, 0, width, 0, F32, width, "own_rows")
+        x, aboves[1], held["own"] = lax.optimization_barrier((x, aboves[1], own_rows))
         return x
 
-    def between(x):
-        own_rows = settle(places, grads, bounds, 0, width, 0, F32, width, "own_rows")
-        x, held["own"] = lax.optimization_barrier((x, own_rows))
+    def last(x):
+        object_grad = finish(held["own"], aboves, edges, width)
+        x, held["object_grad"] = lax.optimization_barrier((x, object_grad))
         return x
 
-    probe_grad = summed(given, "row", probe.shape, order, beside, during, between)
-    aboves = [passed_along(held[i], "row", 1) for i in range(2)]
-    object_grad = finish(held["own"], aboves, edges, width)
+    probe_grad = summed(given, "row", probe.shape, order, beside, during, between, last)
+    object_grad = held["object_grad"]
     return object_grad, probe_grad, moved
 
 

time: 130 us -> 124 us (0.954); the launches traced: 129 us -> 125 us
  Pallas kernels: 41.7 us -> 52.3 us
  starting transfers between devices: 50.5 us -> 40.1 us
  waiting for transfers between devices: 20.4 us -> 15.7 us
    ppermute x3, waiting for transfers between devices: 17.3 us -> 1.26 us  [summed(): lax.ppermute(total, axis, hop(axis, s, 1))]
    ppermute x5, waiting for transfers between devices: 0.01 us -> 11.2 us  [passed_along(): return lax.ppermute(x, axis, pairs)]
    ppermute x3, starting transfers between devices: 18.3 us -> 9.21 us  [summed(): lax.ppermute(parts[s], axis, hop(axis, s, 1))]
    pallas_call x3, Pallas kernels: 23.3 us -> 30.4 us  [project(): pl.pallas_call(functools.partial(project_kernel, size, width, bounds, sta...]
    pallas_call x3, Pallas kernels: 12.4 us -> 16 us  [settle(): pl.pallas_call(functools.partial(settle_kernel, size, bounds, low, high,...]
    ppermute x3, waiting for transfers between devices: 1.48 us -> 3.16 us  [summed(): lax.ppermute(parts[s], axis, hop(axis, s, 1))]
    unnamed x18 -> x20, local copies, waits for them, and re-layouts: 8.03 us -> 9.22 us
  transfers between devices with their start and end apart: 17 -> 17, of which waited for: 4 -> 3; matrix products, arithmetic and copies ran while one was open for 7% -> 7% of each run, Pallas kernels for 18% -> 35%
where the time goes in v4:
time: 124 us; the launch traced here: 125 us
  Pallas kernels  52.3 us (42%)
  starting transfers between devices  40.1 us (32%)
  waiting for transfers between devices  15.7 us (13%)
  local copies, waits for them, and re-layouts  14.4 us (12%)
  between operations  1.85 us (1%)
    pallas_call x3, Pallas kernels, project(): pl.pallas_call(functools.partial(project_kernel, size, width, bounds, sta...  30.4 us
    pallas_call x3, Pallas kernels, settle(): pl.pallas_call(functools.partial(settle_kernel, size, bounds, low, high,...  16 us
    ppermute x5, starting transfers between devices, passed_along(): return lax.ppermute(x, axis, pairs)  13.2 us
    ppermute x5, waiting for transfers between devices, passed_along(): return lax.ppermute(x, axis, pairs)  11.2 us
    unnamed x20, local copies, waits for them, and re-layouts  9.22 us
    ppermute x3, starting transfers between devices, summed(): lax.ppermute(total, axis, hop(axis, s, 1))  9.21 us
    ppermute x3, starting transfers between devices, summed(): lax.ppermute(parts[s], axis, hop(axis, s, 1))  9.21 us
    ppermute x4, starting transfers between devices, summed(): others = [lax.ppermute(piece, axis, outward) for piece in pieces]  5.21 us
  transfers between devices with their start and end apart: 17, of which 3 were waited for; matrix products, arithmetic and copies ran while one was open for 7% of the time, Pallas kernels for 35%

profile of v4, /device:TPU:16, one launch (start us, length us, event | category | flops | bytes accessed | tf_op | source)
XLA Modules:
  0.0 124.6 jit_solution(7306600550160694606)
XLA Ops:
  0.7 1.2 slice-done
  2.8 2.9 %collective-permute-start.2 = (bf16[256,1792]{1,0:T(8,128)(2,1)}, bf16[256,1792]{1,0:T(8,128)(2,1)S(1)}, u32[]{:S(2)}, u32[]{:S(2)}) collective-permute-start(bf16[256,1792]{1,0:T(8,128)(2,1)} %bitcast.18), channel_id=1, source_target_pairs={{1,0},{2,1},{3,2},{4,3},{5,4},{6,5},{7,6},{8,7},{9,8},{10,9},{11,1... | collective-permute-start | bytes 2752520 | tf_op jit(solution)/shard_map/ppermute | solution.py:491
  6.7 2.6 %collective-permute-start.1 = (bf16[256,1280]{1,0:T(8,128)(2,1)}, bf16[256,1280]{1,0:T(8,128)(2,1)}, u32[]{:S(2)}, u32[]{:S(2)}) collective-permute-start(bf16[256,1280]{1,0:T(8,128)(2,1)} %bitcast.16), channel_id=1, source_target_pairs={{1,0},{2,1},{3,2},{4,3},{5,4},{6,5},{7,6},{8,7},{9,8},{10,9},{11,1... | collective-permute-start | bytes 1966088 | tf_op jit(solution)/shard_map/ppermute | solution.py:491
  10.2 1.9 %collective-permute-start = (bf16[256,1024]{1,0:T(8,128)(2,1)}, bf16[256,1024]{1,0:T(8,128)(2,1)S(1)}, u32[]{:S(2)}, u32[]{:S(2)}) collective-permute-start(bf16[256,1024]{1,0:T(8,128)(2,1)} %bitcast.14), channel_id=1, source_target_pairs={{1,0},{2,1},{3,2},{4,3},{5,4},{6,5},{7,6},{8,7},{9,8},{10,9},{11,1... | collective-permute-start | bytes 1572872 | tf_op jit(solution)/shard_map/ppermute | solution.py:491
  12.9 2.5 %copy.11 = bf16[32,8,2,2048]{3,1,2,0:T(8,128)(2,1)S(1)} copy(bf16[32,8,2,2048]{3,2,1,0:T(2,128)(2,1)} %bitcast.25) | data formatting | bytes 4194304
  15.4 3.9 %reshape.33.refs_2_.refs_3_ = f32[4,256,512]{2,1,0:T(8,128)} reshape(f32[4,256,2,256]{3,2,1,0:T(2,128)} %param.9) | data formatting | bytes 4194304 | tf_op jit(solution)/shard_map/reshape | solution.py:650
  19.3 1.6 %copy-done = f32[4,256,512]{2,1,0:T(8,128)S(1)} copy-done((f32[4,256,512]{2,1,0:T(8,128)S(1)}, f32[4,256,512]{2,1,0:T(8,128)}, u32[]{:S(2)}) %copy-start) | copy-done | bytes 2097176
  23.1 9.7 %project_0.1 = (f32[2,6]{1,0:T(2,128)S(1)}, bf16[6,256,512]{2,1,0:T(8,128)(2,1)S(1)}, f32[4,256,512]{2,1,0:T(8,128)S(1)}) custom-call(s32[5,6]{1,0:T(8,128)S(1)} %stack.33.places, bf16[256,4096]{1,0:T(8,128)(2,1)S(1)} %bitcast.20, bf16[256,1792]{1,0:T(8,128)(2,1)S(1)} %collective-permute-done.2.refs_1_.refs_2_, f32[4,256,512]{2,1,0:T(8,128)S(1)} %copy-done, ...), custom_call_target="tpu_custom_call" | custom-call | flops 8000000000 | bytes 16777216 | tf_op jit(solution)/shard_map/project_0/pallas_call | solution.py:343
  32.9 14.0 %project_1.1 = (f32[2,6]{1,0:T(2,128)S(1)}, bf16[6,256,512]{2,1,0:T(8,128)(2,1)S(1)}, f32[4,256,512]{2,1,0:T(8,128)S(1)}) custom-call(s32[5,6]{1,0:T(8,128)S(1)} %stack.33.places, bf16[256,4096]{1,0:T(8,128)(2,1)S(1)} %bitcast.21, bf16[256,1280]{1,0:T(8,128)(2,1)} %collective-permute-done.1.refs_1_.refs_2_, ...), custom_call_target="tpu_custom_call" | custom-call | flops 8000000000 | bytes 16777216 | tf_op jit(solution)/shard_map/project_1/pallas_call | solution.py:343
  46.9 6.7 %project_2.1 = (f32[2,6]{1,0:T(2,128)}, bf16[6,256,512]{2,1,0:T(8,128)(2,1)S(1)}, bf16[4,256,512]{2,1,0:T(8,128)(2,1)S(1)}) custom-call(s32[5,6]{1,0:T(8,128)S(1)} %stack.33.places, bf16[256,4096]{1,0:T(8,128)(2,1)S(1)} %bitcast.22, bf16[256,1024]{1,0:T(8,128)(2,1)S(1)} %collective-permute-done.refs_1_, ...), custom_call_target="tpu_custom_call" | custom-call | flops 8000000000 | bytes 16777216 | tf_op jit(solution)/shard_map/project_2/pallas_call | solution.py:343
  53.6 1.3 %collective-permute-start.3 = (bf16[4,256,512]{2,1,0:T(8,128)(2,1)S(1)}, bf16[4,256,512]{2,1,0:T(8,128)(2,1)S(1)}, u32[]{:S(2)}, u32[]{:S(2)}) collective-permute-start(bf16[4,256,512]{2,1,0:T(8,128)(2,1)S(1)} %get-tuple-element.35), channel_id=1, source_target_pairs={{1,0},{3,2},{5,4},{7,6},{9,8},{11,10},{13,12},{15,14},{17,16},{19,... | collective-permute-start | bytes 3145736 | tf_op jit(solution)/shard_map/ppermute | solution.py:610
  54.9 3.4 %below_0.1 = bf16[256,2048]{1,0:T(8,128)(2,1)S(1)} custom-call(s32[5,6]{1,0:T(8,128)S(1)} %stack.33.places, bf16[6,256,512]{2,1,0:T(8,128)(2,1)S(1)} %get-tuple-element.36.refs_0_, bf16[6,256,512]{2,1,0:T(8,128)(2,1)S(1)} %get-tuple-element.37.refs_1_, bf16[6,256,512]{2,1,0:T(8,128)(2,1)S(1)} %get-tuple-element.38.refs_2_), custom_call_target="tpu_custom_call" | custom-call | flops 1000000000 | bytes 8388608 | tf_op jit(solution)/shard_map/below_0/pallas_call | solution.py:425
  58.4 4.0 %collective-permute-start.7 = (bf16[256,2048]{1,0:T(8,128)(2,1)S(1)}, bf16[256,2048]{1,0:T(8,128)(2,1)S(1)}, u32[]{:S(2)}, u32[]{:S(2)}) collective-permute-start(bf16[256,2048]{1,0:T(8,128)(2,1)S(1)} %below_0.1), channel_id=1, source_target_pairs={{0,1},{1,2},{2,3},{3,4},{4,5},{5,6},{6,7},{7,8},{8,9},{9,10},{10,1... | collective-permute-start | bytes 3145736 | tf_op jit(solution)/shard_map/ppermute | solution.py:491
  63.4 1.9 %collective-permute-start.4 = (bf16[256,512]{1,0:T(8,128)(2,1)S(1)}, bf16[256,512]{1,0:T(8,128)(2,1)S(1)}, u32[]{:S(2)}, u32[]{:S(2)}) collective-permute-start(bf16[256,512]{1,0:T(8,128)(2,1)S(1)} %get-tuple-element.41), channel_id=1, source_target_pairs={{0,2},{2,0},{4,6},{6,4},{8,10},{10,8},{12,14},{14,12},{16,18},{18,... | collective-permute-start | bytes 786440 | tf_op jit(solution)/shard_map/ppermute | solution.py:613
  65.3 1.9 %collective-permute-start.5 = (bf16[256,512]{1,0:T(8,128)(2,1)S(1)}, bf16[256,512]{1,0:T(8,128)(2,1)S(1)}, u32[]{:S(2)}, u32[]{:S(2)}) collective-permute-start(bf16[256,512]{1,0:T(8,128)(2,1)S(1)} %get-tuple-element.42), channel_id=1, source_target_pairs={{0,4},{2,6},{4,0},{6,2},{8,12},{10,14},{12,8},{14,10},{16,20},{18,... | collective-permute-start | bytes 786440 | tf_op jit(solution)/shard_map/ppermute | solution.py:613
  67.3 5.4 %collective-permute-start.6 = (bf16[256,512]{1,0:T(8,128)(2,1)S(1)}, bf16[256,512]{1,0:T(8,128)(2,1)S(1)}, u32[]{:S(2)}, u32[]{:S(2)}) collective-permute-start(bf16[256,512]{1,0:T(8,128)(2,1)S(1)} %get-tuple-element.43), channel_id=1, source_target_pairs={{0,6},{2,4},{4,2},{6,0},{8,14},{10,12},{12,10},{14,8},{16,22},{18,... | collective-permute-start | bytes 786440 | tf_op jit(solution)/shard_map/ppermute | solution.py:613
  72.6 5.2 %below_1024.1 = bf16[256,2048]{1,0:T(8,128)(2,1)S(1)} custom-call(s32[5,6]{1,0:T(8,128)S(1)} %stack.33.places, bf16[6,256,512]{2,1,0:T(8,128)(2,1)S(1)} %get-tuple-element.36.refs_0_, bf16[6,256,512]{2,1,0:T(8,128)(2,1)S(1)} %get-tuple-element.37.refs_1_, bf16[6,256,512]{2,1,0:T(8,128)(2,1)S(1)} %get-tuple-element.38.refs_2_), custom_call_target="tpu_custom_call" | custom-call | flops 1000000000 | bytes 8388608 | tf_op jit(solution)/shard_map/below_1024/pallas_call | solution.py:425
  77.8 3.2 %collective-permute-done.4 = bf16[256,512]{1,0:T(8,128)(2,1)S(1)} collective-permute-done((bf16[256,512]{1,0:T(8,128)(2,1)S(1)}, bf16[256,512]{1,0:T(8,128)(2,1)S(1)}, u32[]{:S(2)}, u32[]{:S(2)}) %collective-permute-start.4) | collective-permute-done | bytes 262176 | tf_op jit(solution)/shard_map/ppermute | solution.py:613
  81.0 1.9 %collective-permute-start.9 = (bf16[256,2048]{1,0:T(8,128)(2,1)S(1)}, bf16[256,2048]{1,0:T(8,128)(2,1)S(1)}, u32[]{:S(2)}, u32[]{:S(2)}) collective-permute-start(bf16[256,2048]{1,0:T(8,128)(2,1)S(1)} %below_1024.1), channel_id=1, source_target_pairs={{0,1},{1,2},{2,3},{3,4},{4,5},{5,6},{6,7},{7,8},{8,9},{9,10},{10,1... | collective-permute-start | bytes 3145736 | tf_op jit(solution)/shard_map/ppermute | solution.py:491
  83.1 1.9 %collective-permute-start.8 = (bf16[256,512]{1,0:T(8,128)(2,1)S(1)}, bf16[256,512]{1,0:T(8,128)(2,1)S(1)}, u32[]{:S(2)}, u32[]{:S(2)}) collective-permute-start(bf16[256,512]{1,0:T(8,128)(2,1)S(1)} %fusion), channel_id=1, source_target_pairs={{0,8},{2,10},{4,12},{6,14},{8,0},{10,2},{12,4},{14,6},{16,24},{18,... | collective-permute-start | bytes 786440 | tf_op jit(solution)/shard_map/ppermute | solution.py:619
  85.0 7.4 %own_rows.1.own = f32[256,4096]{1,0:T(8,128)S(1)} custom-call(s32[5,6]{1,0:T(8,128)S(1)} %stack.33.places, bf16[6,256,512]{2,1,0:T(8,128)(2,1)S(1)} %get-tuple-element.36.refs_0_, bf16[6,256,512]{2,1,0:T(8,128)(2,1)S(1)} %get-tuple-element.37.refs_1_, bf16[6,256,512]{2,1,0:T(8,128)(2,1)S(1)} %get-tuple-element.38.refs_2_), custom_call_target="tpu_custom_call" | custom-call | flops 1000000000 | bytes 8388608 | tf_op jit(solution)/shard_map/own_rows/pallas_call | solution.py:425
  92.4 11.2 %collective-permute-done.9.refs_1_ = bf16[256,2048]{1,0:T(8,128)(2,1)S(1)} collective-permute-done((bf16[256,2048]{1,0:T(8,128)(2,1)S(1)}, bf16[256,2048]{1,0:T(8,128)(2,1)S(1)}, u32[]{:S(2)}, u32[]{:S(2)}) %collective-permute-start.9) | collective-permute-done | bytes 1048608 | tf_op jit(solution)/shard_map/ppermute | solution.py:491
  103.8 1.9 %collective-permute-start.10 = (bf16[256,512]{1,0:T(8,128)(2,1)S(1)}, bf16[256,512]{1,0:T(8,128)(2,1)S(1)}, u32[]{:S(2)}, u32[]{:S(2)}) collective-permute-start(bf16[256,512]{1,0:T(8,128)(2,1)S(1)} %add_convert_fusion.refs_0_), channel_id=1, source_target_pairs={{0,2},{2,0},{4,6},{6,4},{8,10},{10,8},{12,14},{14,12},{16,18},{18,... | collective-permute-start | bytes 786440 | tf_op jit(solution)/shard_map/ppermute | solution.py:625
  105.7 1.9 %collective-permute-start.11 = (bf16[256,512]{1,0:T(8,128)(2,1)S(1)}, bf16[256,512]{1,0:T(8,128)(2,1)S(1)}, u32[]{:S(2)}, u32[]{:S(2)}) collective-permute-start(bf16[256,512]{1,0:T(8,128)(2,1)S(1)} %add_convert_fusion.refs_0_), channel_id=1, source_target_pairs={{0,4},{2,6},{4,0},{6,2},{8,12},{10,14},{12,8},{14,10},{16,20},{18,... | collective-permute-start | bytes 786440 | tf_op jit(solution)/shard_map/ppermute | solution.py:625
  107.6 5.4 %collective-permute-start.12 = (bf16[256,512]{1,0:T(8,128)(2,1)S(1)}, bf16[256,512]{1,0:T(8,128)(2,1)S(1)}, u32[]{:S(2)}, u32[]{:S(2)}) collective-permute-start(bf16[256,512]{1,0:T(8,128)(2,1)S(1)} %add_convert_fusion.refs_0_), channel_id=1, source_target_pairs={{0,6},{2,4},{4,2},{6,0},{8,14},{10,12},{12,10},{14,8},{16,22},{18,... | collective-permute-start | bytes 786440 | tf_op jit(solution)/shard_map/ppermute | solution.py:625
  113.0 1.3 %collective-permute-start.13 = (bf16[256,512]{1,0:T(8,128)(2,1)S(1)}, bf16[256,512]{1,0:T(8,128)(2,1)S(1)}, u32[]{:S(2)}, u32[]{:S(2)}) collective-permute-start(bf16[256,512]{1,0:T(8,128)(2,1)S(1)} %add_convert_fusion.refs_0_), channel_id=1, source_target_pairs={{0,1},{2,3},{4,5},{6,7},{8,9},{10,11},{12,13},{14,15},{16,17},{18,... | collective-permute-start | bytes 786440 | tf_op jit(solution)/shard_map/ppermute | solution.py:626
  114.4 1.3 %collective-permute-start.14 = (bf16[256,512]{1,0:T(8,128)(2,1)S(1)}, bf16[256,512]{1,0:T(8,128)(2,1)S(1)}, u32[]{:S(2)}, u32[]{:S(2)}) collective-permute-start(bf16[256,512]{1,0:T(8,128)(2,1)S(1)} %collective-permute-done.10.refs_1_), channel_id=1, source_target_pairs={{0,1},{2,3},{4,5},{6,7},{8,9},{10,11},{12,13},{14,15},{16,17},{18,... | collective-permute-start | bytes 786440 | tf_op jit(solution)/shard_map/ppermute | solution.py:626
  115.7 1.3 %collective-permute-start.15 = (bf16[256,512]{1,0:T(8,128)(2,1)S(1)}, bf16[256,512]{1,0:T(8,128)(2,1)S(1)}, u32[]{:S(2)}, u32[]{:S(2)}) collective-permute-start(bf16[256,512]{1,0:T(8,128)(2,1)S(1)} %collective-permute-done.11.refs_2_), channel_id=1, source_target_pairs={{0,1},{2,3},{4,5},{6,7},{8,9},{10,11},{12,13},{14,15},{16,17},{18,... | collective-permute-start | bytes 786440 | tf_op jit(solution)/shard_map/ppermute | solution.py:626
  117.0 1.3 %collective-permute-done.12.refs_3_ = bf16[256,512]{1,0:T(8,128)(2,1)S(1)} collective-permute-done((bf16[256,512]{1,0:T(8,128)(2,1)S(1)}, bf16[256,512]{1,0:T(8,128)(2,1)S(1)}, u32[]{:S(2)}, u32[]{:S(2)}) %collective-permute-start.12) | collective-permute-done | bytes 262176 | tf_op jit(solution)/shard_map/ppermute | solution.py:625
  118.2 1.3 %collective-permute-start.16 = (bf16[256,512]{1,0:T(8,128)(2,1)S(1)}, bf16[256,512]{1,0:T(8,128)(2,1)S(1)}, u32[]{:S(2)}, u32[]{:S(2)}) collective-permute-start(bf16[256,512]{1,0:T(8,128)(2,1)S(1)} %collective-permute-done.12.refs_3_), channel_id=1, source_target_pairs={{0,1},{2,3},{4,5},{6,7},{8,9},{10,11},{12,13},{14,15},{16,17},{18,... | collective-permute-start | bytes 786440 | tf_op jit(solution)/shard_map/ppermute | solution.py:626
  119.5 2.8 %finish.1 = f32[256,2,2048]{2,1,0:T(2,128)} custom-call(f32[256,4096]{1,0:T(8,128)S(1)} %own_rows.1.own, bf16[256,2048]{1,0:T(8,128)(2,1)S(1)} %collective-permute-done.7.refs_0_, bf16[256,2048]{1,0:T(8,128)(2,1)S(1)} %collective-permute-done.9.refs_1_), custom_call_target="tpu_custom_call" | custom-call | flops 1000000 | bytes 10485760 | tf_op jit(solution)/shard_map/finish/pallas_call | solution.py:474
  122.4 2.1 %unpack.1 = f32[4,256,2,256]{3,2,1,0:T(2,128)} custom-call(s32[5]{0:T(128)S(1)} %stack.39.order, bf16[256,512]{1,0:T(8,128)(2,1)S(1)} %add_convert_fusion.refs_0_, bf16[256,512]{1,0:T(8,128)(2,1)S(1)} %collective-permute-done.10.refs_1_, bf16[256,512]{1,0:T(8,128)(2,1)S(1)} %collective-permute-done.11.refs_2_, ...), custom_call_target="tpu_custom_call" | custom-call | flops 1000000 | bytes 4194304 | tf_op jit(solution)/shard_map/unpack/pallas_call | solution.py:532
  (44 shorter events, 6.7 us)
Async XLA Ops:
  0.6 1.2 slice-start
  0.6 5.1 %slice-start.1 = ((bf16[256,2,2048]{2,1,0:T(2,128)(2,1)}), bf16[256,2,640]{2,1,0:T(2,128)(2,1)S(1)}, s32[]{:S(2)}) async-start(bf16[256,2,2048]{2,1,0:T(2,128)(2,1)} %param.8), calls=%async_computation.1 | async-start | bytes 1310720 | tf_op jit(solution)/shard_map/slice | solution.py:641
  2.8 6.4 %slice-start.2 = ((bf16[256,2,2048]{2,1,0:T(2,128)(2,1)}), bf16[256,2,512]{2,1,0:T(2,128)(2,1)S(1)}, s32[]{:S(2)}) async-start(bf16[256,2,2048]{2,1,0:T(2,128)(2,1)} %param.8), calls=%async_computation.2 | async-start | bytes 1048576 | tf_op jit(solution)/shard_map/slice | solution.py:641
  2.8 10.0 %copy-start.5 = (s32[6]{0:T(128)S(1)}, s32[6]{0:T(128)}, u32[]{:S(2)}) copy-start(s32[6]{0:T(128)} %param.11) | copy-start | bytes 76
  2.8 10.0 %copy-start.6 = (s32[6]{0:T(128)S(1)}, s32[6]{0:T(128)}, u32[]{:S(2)}) copy-start(s32[6]{0:T(128)} %param.12) | copy-start | bytes 76
  2.8 10.0 %copy-start.7 = (s32[6]{0:T(128)S(1)}, s32[6]{0:T(128)}, u32[]{:S(2)}) copy-start(s32[6]{0:T(128)} %param.13) | copy-start | bytes 76
  2.8 16.4 %collective-permute-start.2 = (bf16[256,1792]{1,0:T(8,128)(2,1)}, bf16[256,1792]{1,0:T(8,128)(2,1)S(1)}, u32[]{:S(2)}, u32[]{:S(2)}) collective-permute-start(bf16[256,1792]{1,0:T(8,128)(2,1)} %bitcast.18), channel_id=1, source_target_pairs={{1,0},{2,1},{3,2},{4,3},{5,4},{6,5},{7,6},{8,7},{9,8},{10,9},{11,1... | collective-permute-start | bytes 2752520 | tf_op jit(solution)/shard_map/ppermute | solution.py:491
  6.7 26.2 %collective-permute-start.1 = (bf16[256,1280]{1,0:T(8,128)(2,1)}, bf16[256,1280]{1,0:T(8,128)(2,1)}, u32[]{:S(2)}, u32[]{:S(2)}) collective-permute-start(bf16[256,1280]{1,0:T(8,128)(2,1)} %bitcast.16), channel_id=1, source_target_pairs={{1,0},{2,1},{3,2},{4,3},{5,4},{6,5},{7,6},{8,7},{9,8},{10,9},{11,1... | collective-permute-start | bytes 1966088 | tf_op jit(solution)/shard_map/ppermute | solution.py:491
  10.2 36.8 %collective-permute-start = (bf16[256,1024]{1,0:T(8,128)(2,1)}, bf16[256,1024]{1,0:T(8,128)(2,1)S(1)}, u32[]{:S(2)}, u32[]{:S(2)}) collective-permute-start(bf16[256,1024]{1,0:T(8,128)(2,1)} %bitcast.14), channel_id=1, source_target_pairs={{1,0},{2,1},{3,2},{4,3},{5,4},{6,5},{7,6},{8,7},{9,8},{10,9},{11,1... | collective-permute-start | bytes 1572872 | tf_op jit(solution)/shard_map/ppermute | solution.py:491
  19.3 1.6 %copy-start = (f32[4,256,512]{2,1,0:T(8,128)S(1)}, f32[4,256,512]{2,1,0:T(8,128)}, u32[]{:S(2)}) copy-start(f32[4,256,512]{2,1,0:T(8,128)} %reshape.33.refs_2_.refs_3_) | copy-start | bytes 6291460
  20.9 1.1 copy-start.1
  22.0 1.1 copy-start.3
  23.1 9.7 %copy-start.2 = (bf16[6,256,256]{2,1,0:T(8,128)(2,1)S(1)}, bf16[6,256,256]{2,1,0:T(8,128)(2,1)}, u32[]{:S(2)}) copy-start(bf16[6,256,256]{2,1,0:T(8,128)(2,1)} %refs_4_.4) | copy-start | bytes 2359300
  23.1 9.7 %copy-start.4 = (bf16[6,256,256]{2,1,0:T(8,128)(2,1)S(1)}, bf16[6,256,256]{2,1,0:T(8,128)(2,1)}, u32[]{:S(2)}) copy-start(bf16[6,256,256]{2,1,0:T(8,128)(2,1)} %constant.44.clone.refs_4_.refs_5_) | copy-start | bytes 2359300
  53.6 8.7 %collective-permute-start.3 = (bf16[4,256,512]{2,1,0:T(8,128)(2,1)S(1)}, bf16[4,256,512]{2,1,0:T(8,128)(2,1)S(1)}, u32[]{:S(2)}, u32[]{:S(2)}) collective-permute-start(bf16[4,256,512]{2,1,0:T(8,128)(2,1)S(1)} %get-tuple-element.35), channel_id=1, source_target_pairs={{1,0},{3,2},{5,4},{7,6},{9,8},{11,10},{13,12},{15,14},{17,16},{19,... | collective-permute-start | bytes 3145736 | tf_op jit(solution)/shard_map/ppermute | solution.py:610
  58.4 19.5 %collective-permute-start.7 = (bf16[256,2048]{1,0:T(8,128)(2,1)S(1)}, bf16[256,2048]{1,0:T(8,128)(2,1)S(1)}, u32[]{:S(2)}, u32[]{:S(2)}) collective-permute-start(bf16[256,2048]{1,0:T(8,128)(2,1)S(1)} %below_0.1), channel_id=1, source_target_pairs={{0,1},{1,2},{2,3},{3,4},{4,5},{5,6},{6,7},{7,8},{8,9},{9,10},{10,1... | collective-permute-start | bytes 3145736 | tf_op jit(solution)/shard_map/ppermute | solution.py:491
  63.4 17.6 %collective-permute-start.4 = (bf16[256,512]{1,0:T(8,128)(2,1)S(1)}, bf16[256,512]{1,0:T(8,128)(2,1)S(1)}, u32[]{:S(2)}, u32[]{:S(2)}) collective-permute-start(bf16[256,512]{1,0:T(8,128)(2,1)S(1)} %get-tuple-element.41), channel_id=1, source_target_pairs={{0,2},{2,0},{4,6},{6,4},{8,10},{10,8},{12,14},{14,12},{16,18},{18,... | collective-permute-start | bytes 786440 | tf_op jit(solution)/shard_map/ppermute | solution.py:613
  65.3 15.7 %collective-permute-start.5 = (bf16[256,512]{1,0:T(8,128)(2,1)S(1)}, bf16[256,512]{1,0:T(8,128)(2,1)S(1)}, u32[]{:S(2)}, u32[]{:S(2)}) collective-permute-start(bf16[256,512]{1,0:T(8,128)(2,1)S(1)} %get-tuple-element.42), channel_id=1, source_target_pairs={{0,4},{2,6},{4,0},{6,2},{8,12},{10,14},{12,8},{14,10},{16,20},{18,... | collective-permute-start | bytes 786440 | tf_op jit(solution)/shard_map/ppermute | solution.py:613
  67.3 13.7 %collective-permute-start.6 = (bf16[256,512]{1,0:T(8,128)(2,1)S(1)}, bf16[256,512]{1,0:T(8,128)(2,1)S(1)}, u32[]{:S(2)}, u32[]{:S(2)}) collective-permute-start(bf16[256,512]{1,0:T(8,128)(2,1)S(1)} %get-tuple-element.43), channel_id=1, source_target_pairs={{0,6},{2,4},{4,2},{6,0},{8,14},{10,12},{12,10},{14,8},{16,22},{18,... | collective-permute-start | bytes 786440 | tf_op jit(solution)/shard_map/ppermute | solution.py:613
  81.0 22.6 %collective-permute-start.9 = (bf16[256,2048]{1,0:T(8,128)(2,1)S(1)}, bf16[256,2048]{1,0:T(8,128)(2,1)S(1)}, u32[]{:S(2)}, u32[]{:S(2)}) collective-permute-start(bf16[256,2048]{1,0:T(8,128)(2,1)S(1)} %below_1024.1), channel_id=1, source_target_pairs={{0,1},{1,2},{2,3},{3,4},{4,5},{5,6},{6,7},{7,8},{8,9},{9,10},{10,1... | collective-permute-start | bytes 3145736 | tf_op jit(solution)/shard_map/ppermute | solution.py:491
  83.1 9.3 %collective-permute-start.8 = (bf16[256,512]{1,0:T(8,128)(2,1)S(1)}, bf16[256,512]{1,0:T(8,128)(2,1)S(1)}, u32[]{:S(2)}, u32[]{:S(2)}) collective-permute-start(bf16[256,512]{1,0:T(8,128)(2,1)S(1)} %fusion), channel_id=1, source_target_pairs={{0,8},{2,10},{4,12},{6,14},{8,0},{10,2},{12,4},{14,6},{16,24},{18,... | collective-permute-start | bytes 786440 | tf_op jit(solution)/shard_map/ppermute | solution.py:619
  103.8 10.6 %collective-permute-start.10 = (bf16[256,512]{1,0:T(8,128)(2,1)S(1)}, bf16[256,512]{1,0:T(8,128)(2,1)S(1)}, u32[]{:S(2)}, u32[]{:S(2)}) collective-permute-start(bf16[256,512]{1,0:T(8,128)(2,1)S(1)} %add_convert_fusion.refs_0_), channel_id=1, source_target_pairs={{0,2},{2,0},{4,6},{6,4},{8,10},{10,8},{12,14},{14,12},{16,18},{18,... | collective-permute-start | bytes 786440 | tf_op jit(solution)/shard_map/ppermute | solution.py:625
  105.7 9.9 %collective-permute-start.11 = (bf16[256,512]{1,0:T(8,128)(2,1)S(1)}, bf16[256,512]{1,0:T(8,128)(2,1)S(1)}, u32[]{:S(2)}, u32[]{:S(2)}) collective-permute-start(bf16[256,512]{1,0:T(8,128)(2,1)S(1)} %add_convert_fusion.refs_0_), channel_id=1, source_target_pairs={{0,4},{2,6},{4,0},{6,2},{8,12},{10,14},{12,8},{14,10},{16,20},{18,... | collective-permute-start | bytes 786440 | tf_op jit(solution)/shard_map/ppermute | solution.py:625
  107.6 10.6 %collective-permute-start.12 = (bf16[256,512]{1,0:T(8,128)(2,1)S(1)}, bf16[256,512]{1,0:T(8,128)(2,1)S(1)}, u32[]{:S(2)}, u32[]{:S(2)}) collective-permute-start(bf16[256,512]{1,0:T(8,128)(2,1)S(1)} %add_convert_fusion.refs_0_), channel_id=1, source_target_pairs={{0,6},{2,4},{4,2},{6,0},{8,14},{10,12},{12,10},{14,8},{16,22},{18,... | collective-permute-start | bytes 786440 | tf_op jit(solution)/shard_map/ppermute | solution.py:625
  113.0 9.3 %collective-permute-start.13 = (bf16[256,512]{1,0:T(8,128)(2,1)S(1)}, bf16[256,512]{1,0:T(8,128)(2,1)S(1)}, u32[]{:S(2)}, u32[]{:S(2)}) collective-permute-start(bf16[256,512]{1,0:T(8,128)(2,1)S(1)} %add_convert_fusion.refs_0_), channel_id=1, source_target_pairs={{0,1},{2,3},{4,5},{6,7},{8,9},{10,11},{12,13},{14,15},{16,17},{18,... | collective-permute-start | bytes 786440 | tf_op jit(solution)/shard_map/ppermute | solution.py:626
  114.4 8.0 %collective-permute-start.14 = (bf16[256,512]{1,0:T(8,128)(2,1)S(1)}, bf16[256,512]{1,0:T(8,128)(2,1)S(1)}, u32[]{:S(2)}, u32[]{:S(2)}) collective-permute-start(bf16[256,512]{1,0:T(8,128)(2,1)S(1)} %collective-permute-done.10.refs_1_), channel_id=1, source_target_pairs={{0,1},{2,3},{4,5},{6,7},{8,9},{10,11},{12,13},{14,15},{16,17},{18,... | collective-permute-start | bytes 786440 | tf_op jit(solution)/shard_map/ppermute | solution.py:626
  115.7 6.7 %collective-permute-start.15 = (bf16[256,512]{1,0:T(8,128)(2,1)S(1)}, bf16[256,512]{1,0:T(8,128)(2,1)S(1)}, u32[]{:S(2)}, u32[]{:S(2)}) collective-permute-start(bf16[256,512]{1,0:T(8,128)(2,1)S(1)} %collective-permute-done.11.refs_2_), channel_id=1, source_target_pairs={{0,1},{2,3},{4,5},{6,7},{8,9},{10,11},{12,13},{14,15},{16,17},{18,... | collective-permute-start | bytes 786440 | tf_op jit(solution)/shard_map/ppermute | solution.py:626
  118.2 4.1 %collective-permute-start.16 = (bf16[256,512]{1,0:T(8,128)(2,1)S(1)}, bf16[256,512]{1,0:T(8,128)(2,1)S(1)}, u32[]{:S(2)}, u32[]{:S(2)}) collective-permute-start(bf16[256,512]{1,0:T(8,128)(2,1)S(1)} %collective-permute-done.12.refs_3_), channel_id=1, source_target_pairs={{0,1},{2,3},{4,5},{6,7},{8,9},{10,11},{12,13},{14,15},{16,17},{18,... | collective-permute-start | bytes 786440 | tf_op jit(solution)/shard_map/ppermute | solution.py:626

commit v5 on v4

--- a/solution.py
+++ b/solution.py
@@ -650,28 +650,29 @@
     flat = probe.reshape(modes, size, 2 * size)
     carried = None
     grads = []
+    edges = (0, min(width // 2 // LANES * LANES, bounds[-2] - size), width)
     for stage in range(stages):
+        if stage == stages - 1:
+            early = settle(places, grads, bounds, edges[0], edges[1], size, BF16, width, "below_early")
+            places, early = lax.optimization_barrier((places, early))
+            aboves = [passed_along(early, "row", 1)]
         moved, grad, *rest = project(stage, bounds, places, own, rims, flat, measured, tables, width, carried)
         grads.append(grad)
         carried = [moved] + rest
-    given = carried[1]
-    edges = (0, width // 2 // LANES * LANES, width)
-    belows = [
-        settle(places, grads, bounds, low, high, size, BF16, width, f"below_{low}")
-        for low, high in zip(edges[:-1], edges[1:])
-    ]
-    aboves = [passed_along(belows[0], "row", 1)]
+    given, aboves = lax.optimization_barrier((carried[1], aboves))
+    aboves = list(aboves)
+    late = settle(places, grads, bounds, edges[1], edges[2], size, BF16, width, "below_late")
     held = {}
 
     def beside(x):
-        return lax.optimization_barrier((x, belows[0]))[0]
+        return x
 
     def during(x):
-        x, aboves[0], held["below"] = lax.optimization_barrier((x, aboves[0], belows[1]))
+        x, held["late"] = lax.optimization_barrier((x, late))
         return x
 
     def between(x):
-        aboves.append(passed_along(held["below"], "row", 1))
+        aboves.append(passed_along(held["late"], "row", 1))
         own_rows = settle(places, grads, bounds, 0, width, 0, F32, width, "own_rows")
         x, aboves[1], held["own"] = lax.optimization_barrier((x, aboves[1], own_rows))
         return x

time: 124 us -> 132 us (1.065)
  the two profiles are of different devices: /device:TPU:16 before, /device:TPU:22 now
where the time goes in v5:
time: 132 us
  starting transfers between devices  52.7 us (40%)
  waiting for transfers between devices  36.2 us (27%)
  Pallas kernels  30.8 us (23%)
  local copies, waits for them, and re-layouts  9.68 us (7%)
  between operations  1.87 us (1%)
    ppermute x3, starting transfers between devices, summed(): lax.ppermute(parts[s], axis, hop(axis, s, 1))  17.8 us
    ppermute x5, waiting for transfers between devices, passed_along(): return lax.ppermute(x, axis, pairs)  17.6 us
    pallas_call x3, Pallas kernels, project(): pl.pallas_call(functools.partial(project_kernel, size, width, bounds, sta...  15.3 us
    ppermute x3, starting transfers between devices, summed(): lax.ppermute(total, axis, hop(axis, s, 1))  15.2 us
    ppermute x5, starting transfers between devices, passed_along(): return lax.ppermute(x, axis, pairs)  11.3 us
    pallas_call x3, Pallas kernels, settle(): pl.pallas_call(functools.partial(settle_kernel, size, bounds, low, high,...  9.55 us
    ppermute x1, waiting for transfers between devices, summed(): sibling = beside(lax.ppermute(given, axis, inward))  6.72 us
    ppermute x1, waiting for transfers between devices, summed(): lax.ppermute(sent, axis, hop(axis, s, near))  6.24 us
  transfers between devices with their start and end apart: 17, of which 9 were waited for; matrix products, arithmetic and copies ran while one was open for 6% of the time, Pallas kernels for 21%

profile of v5, /device:TPU:22, one launch (start us, length us, event | category | flops | bytes accessed | tf_op | source)
XLA Modules:
  0.0 131.5 jit_solution(6406924573773777134)
XLA Ops:
  2.8 2.0 %collective-permute-start = (bf16[256,1792]{1,0:T(8,128)(2,1)}, bf16[256,1792]{1,0:T(8,128)(2,1)S(1)}, u32[]{:S(2)}, u32[]{:S(2)}) collective-permute-start(bf16[256,1792]{1,0:T(8,128)(2,1)} %bitcast.14), channel_id=1, source_target_pairs={{1,0},{2,1},{3,2},{4,3},{5,4},{6,5},{7,6},{8,7},{9,8},{10,9},{11,1... | collective-permute-start | bytes 2752520 | tf_op jit(solution)/shard_map/ppermute | solution.py:491
  5.8 2.5 %collective-permute-start.2 = (bf16[256,1024]{1,0:T(8,128)(2,1)}, bf16[256,1024]{1,0:T(8,128)(2,1)S(1)}, u32[]{:S(2)}, u32[]{:S(2)}) collective-permute-start(bf16[256,1024]{1,0:T(8,128)(2,1)} %bitcast.18), channel_id=1, source_target_pairs={{1,0},{2,1},{3,2},{4,3},{5,4},{6,5},{7,6},{8,7},{9,8},{10,9},{11,1... | collective-permute-start | bytes 1572872 | tf_op jit(solution)/shard_map/ppermute | solution.py:491
  9.3 2.7 %collective-permute-start.1 = (bf16[256,1280]{1,0:T(8,128)(2,1)}, bf16[256,1280]{1,0:T(8,128)(2,1)}, u32[]{:S(2)}, u32[]{:S(2)}) collective-permute-start(bf16[256,1280]{1,0:T(8,128)(2,1)} %bitcast.16), channel_id=1, source_target_pairs={{1,0},{2,1},{3,2},{4,3},{5,4},{6,5},{7,6},{8,7},{9,8},{10,9},{11,1... | collective-permute-start | bytes 1966088 | tf_op jit(solution)/shard_map/ppermute | solution.py:491
  12.8 2.9 %reshape.32.refs_2_.refs_3_ = f32[4,256,512]{2,1,0:T(8,128)S(1)} reshape(f32[4,256,2,256]{3,2,1,0:T(2,128)} %param.9) | data formatting | bytes 4194304 | tf_op jit(solution)/shard_map/reshape | solution.py:650
  15.8 2.6 %copy.11 = bf16[32,8,2,2048]{3,1,2,0:T(8,128)(2,1)S(1)} copy(bf16[32,8,2,2048]{3,2,1,0:T(2,128)(2,1)} %bitcast.25) | data formatting | bytes 4194304
  18.4 6.0 %project_0.1 = (f32[2,6]{1,0:T(2,128)S(1)}, bf16[6,256,512]{2,1,0:T(8,128)(2,1)S(1)}, f32[4,256,512]{2,1,0:T(8,128)S(1)}) custom-call(s32[5,6]{1,0:T(8,128)S(1)} %stack.33.places, bf16[256,4096]{1,0:T(8,128)(2,1)S(1)} %bitcast.20, bf16[256,1792]{1,0:T(8,128)(2,1)S(1)} %collective-permute-done.refs_1_.refs_2_, f32[4,256,512]{2,1,0:T(8,128)S(1)} %reshape.32.refs_2_.refs_3_, ...), custom_call_target="tpu_custom_call" | custom-call | flops 8000000000 | bytes 16777216 | tf_op jit(solution)/shard_map/project_0/pallas_call | solution.py:343
  24.4 4.3 %collective-permute-done.1.refs_1_.refs_2_ = bf16[256,1280]{1,0:T(8,128)(2,1)} collective-permute-done((bf16[256,1280]{1,0:T(8,128)(2,1)}, bf16[256,1280]{1,0:T(8,128)(2,1)}, u32[]{:S(2)}, u32[]{:S(2)}) %collective-permute-start.1) | collective-permute-done | bytes 655392 | tf_op jit(solution)/shard_map/ppermute | solution.py:491
  28.7 6.6 %project_1.1 = (f32[2,6]{1,0:T(2,128)S(1)}, bf16[6,256,512]{2,1,0:T(8,128)(2,1)S(1)}, f32[4,256,512]{2,1,0:T(8,128)S(1)}) custom-call(s32[5,6]{1,0:T(8,128)S(1)} %stack.33.places, bf16[256,4096]{1,0:T(8,128)(2,1)S(1)} %bitcast.21, bf16[256,1280]{1,0:T(8,128)(2,1)} %collective-permute-done.1.refs_1_.refs_2_, ...), custom_call_target="tpu_custom_call" | custom-call | flops 8000000000 | bytes 16777216 | tf_op jit(solution)/shard_map/project_1/pallas_call | solution.py:343
  35.3 3.2 %below_early.1 = bf16[256,2048]{1,0:T(8,128)(2,1)S(1)} custom-call(s32[5,6]{1,0:T(8,128)S(1)} %stack.33.places, bf16[6,256,512]{2,1,0:T(8,128)(2,1)S(1)} %get-tuple-element.33.refs_0_, bf16[6,256,512]{2,1,0:T(8,128)(2,1)S(1)} %get-tuple-element.36.refs_1_), custom_call_target="tpu_custom_call" | custom-call | flops 1000000000 | bytes 8388608 | tf_op jit(solution)/shard_map/below_early/pallas_call | solution.py:425
  38.5 2.1 %collective-permute-start.3 = (bf16[256,2048]{1,0:T(8,128)(2,1)S(1)}, bf16[256,2048]{1,0:T(8,128)(2,1)S(1)}, u32[]{:S(2)}, u32[]{:S(2)}) collective-permute-start(bf16[256,2048]{1,0:T(8,128)(2,1)S(1)} %below_early.1), channel_id=1, source_target_pairs={{0,1},{1,2},{2,3},{3,4},{4,5},{5,6},{6,7},{7,8},{8,9},{9,10},{10,1... | collective-permute-start | bytes 3145736 | tf_op jit(solution)/shard_map/ppermute | solution.py:491
  40.6 2.7 %project_2.1 = (f32[2,6]{1,0:T(2,128)}, bf16[6,256,512]{2,1,0:T(8,128)(2,1)S(1)}, bf16[4,256,512]{2,1,0:T(8,128)(2,1)S(1)}) custom-call(s32[5,6]{1,0:T(8,128)S(1)} %stack.33.places, bf16[256,4096]{1,0:T(8,128)(2,1)S(1)} %bitcast.22, bf16[256,1024]{1,0:T(8,128)(2,1)S(1)} %collective-permute-done.2.refs_1_, ...), custom_call_target="tpu_custom_call" | custom-call | flops 8000000000 | bytes 16777216 | tf_op jit(solution)/shard_map/project_2/pallas_call | solution.py:343
  43.3 11.3 %collective-permute-done.3.refs_0_ = bf16[256,2048]{1,0:T(8,128)(2,1)S(1)} collective-permute-done((bf16[256,2048]{1,0:T(8,128)(2,1)S(1)}, bf16[256,2048]{1,0:T(8,128)(2,1)S(1)}, u32[]{:S(2)}, u32[]{:S(2)}) %collective-permute-start.3) | collective-permute-done | bytes 1048608 | tf_op jit(solution)/shard_map/ppermute | solution.py:491
  55.9 6.7 %collective-permute-done.4 = bf16[4,256,512]{2,1,0:T(8,128)(2,1)S(1)} collective-permute-done((bf16[4,256,512]{2,1,0:T(8,128)(2,1)S(1)}, bf16[4,256,512]{2,1,0:T(8,128)(2,1)S(1)}, u32[]{:S(2)}, u32[]{:S(2)}) %collective-permute-start.4) | collective-permute-done | bytes 1048608 | tf_op jit(solution)/shard_map/ppermute | solution.py:610
  63.6 12.6 %collective-permute-start.5 = (bf16[256,512]{1,0:T(8,128)(2,1)S(1)}, bf16[256,512]{1,0:T(8,128)(2,1)S(1)}, u32[]{:S(2)}, u32[]{:S(2)}) collective-permute-start(bf16[256,512]{1,0:T(8,128)(2,1)S(1)} %get-tuple-element.44), channel_id=1, source_target_pairs={{0,2},{2,0},{4,6},{6,4},{8,10},{10,8},{12,14},{14,12},{16,18},{18,... | collective-permute-start | bytes 786440 | tf_op jit(solution)/shard_map/ppermute | solution.py:613
  76.2 1.9 %collective-permute-start.6 = (bf16[256,512]{1,0:T(8,128)(2,1)S(1)}, bf16[256,512]{1,0:T(8,128)(2,1)S(1)}, u32[]{:S(2)}, u32[]{:S(2)}) collective-permute-start(bf16[256,512]{1,0:T(8,128)(2,1)S(1)} %get-tuple-element.45), channel_id=1, source_target_pairs={{0,4},{2,6},{4,0},{6,2},{8,12},{10,14},{12,8},{14,10},{16,20},{18,... | collective-permute-start | bytes 786440 | tf_op jit(solution)/shard_map/ppermute | solution.py:613
  78.1 3.4 %collective-permute-start.7 = (bf16[256,512]{1,0:T(8,128)(2,1)S(1)}, bf16[256,512]{1,0:T(8,128)(2,1)S(1)}, u32[]{:S(2)}, u32[]{:S(2)}) collective-permute-start(bf16[256,512]{1,0:T(8,128)(2,1)S(1)} %get-tuple-element.46), channel_id=1, source_target_pairs={{0,6},{2,4},{4,2},{6,0},{8,14},{10,12},{12,10},{14,8},{16,22},{18,... | collective-permute-start | bytes 786440 | tf_op jit(solution)/shard_map/ppermute | solution.py:613
  81.5 2.5 %below_late.1 = bf16[256,2048]{1,0:T(8,128)(2,1)S(1)} custom-call(s32[5,6]{1,0:T(8,128)S(1)} %stack.33.places, bf16[6,256,512]{2,1,0:T(8,128)(2,1)S(1)} %get-tuple-element.33.refs_0_, bf16[6,256,512]{2,1,0:T(8,128)(2,1)S(1)} %get-tuple-element.36.refs_1_, bf16[6,256,512]{2,1,0:T(8,128)(2,1)S(1)} %get-tuple-element.47.refs_2_), custom_call_target="tpu_custom_call" | custom-call | flops 1000000000 | bytes 8388608 | tf_op jit(solution)/shard_map/below_late/pallas_call | solution.py:425
  84.5 2.8 %collective-permute-done.7 = bf16[256,512]{1,0:T(8,128)(2,1)S(1)} collective-permute-done((bf16[256,512]{1,0:T(8,128)(2,1)S(1)}, bf16[256,512]{1,0:T(8,128)(2,1)S(1)}, u32[]{:S(2)}, u32[]{:S(2)}) %collective-permute-start.7) | collective-permute-done | bytes 262176 | tf_op jit(solution)/shard_map/ppermute | solution.py:613
  87.3 1.9 %collective-permute-start.9 = (bf16[256,2048]{1,0:T(8,128)(2,1)S(1)}, bf16[256,2048]{1,0:T(8,128)(2,1)S(1)}, u32[]{:S(2)}, u32[]{:S(2)}) collective-permute-start(bf16[256,2048]{1,0:T(8,128)(2,1)S(1)} %below_late.1), channel_id=1, source_target_pairs={{0,1},{1,2},{2,3},{3,4},{4,5},{5,6},{6,7},{7,8},{8,9},{9,10},{10,1... | collective-permute-start | bytes 3145736 | tf_op jit(solution)/shard_map/ppermute | solution.py:491
  89.4 1.9 %collective-permute-start.8 = (bf16[256,512]{1,0:T(8,128)(2,1)S(1)}, bf16[256,512]{1,0:T(8,128)(2,1)S(1)}, u32[]{:S(2)}, u32[]{:S(2)}) collective-permute-start(bf16[256,512]{1,0:T(8,128)(2,1)S(1)} %fusion), channel_id=1, source_target_pairs={{0,8},{2,10},{4,12},{6,14},{8,0},{10,2},{12,4},{14,6},{16,24},{18,... | collective-permute-start | bytes 786440 | tf_op jit(solution)/shard_map/ppermute | solution.py:619
  91.3 3.9 %own_rows.1.own = f32[256,4096]{1,0:T(8,128)S(1)} custom-call(s32[5,6]{1,0:T(8,128)S(1)} %stack.33.places, bf16[6,256,512]{2,1,0:T(8,128)(2,1)S(1)} %get-tuple-element.33.refs_0_, bf16[6,256,512]{2,1,0:T(8,128)(2,1)S(1)} %get-tuple-element.36.refs_1_, bf16[6,256,512]{2,1,0:T(8,128)(2,1)S(1)} %get-tuple-element.47.refs_2_), custom_call_target="tpu_custom_call" | custom-call | flops 1000000000 | bytes 8388608 | tf_op jit(solution)/shard_map/own_rows/pallas_call | solution.py:425
  95.2 6.2 %collective-permute-done.8 = bf16[256,512]{1,0:T(8,128)(2,1)S(1)} collective-permute-done((bf16[256,512]{1,0:T(8,128)(2,1)S(1)}, bf16[256,512]{1,0:T(8,128)(2,1)S(1)}, u32[]{:S(2)}, u32[]{:S(2)}) %collective-permute-start.8) | collective-permute-done | bytes 262176 | tf_op jit(solution)/shard_map/ppermute | solution.py:619
  101.4 2.0 %collective-permute-done.9.refs_1_ = bf16[256,2048]{1,0:T(8,128)(2,1)S(1)} collective-permute-done((bf16[256,2048]{1,0:T(8,128)(2,1)S(1)}, bf16[256,2048]{1,0:T(8,128)(2,1)S(1)}, u32[]{:S(2)}, u32[]{:S(2)}) %collective-permute-start.9) | collective-permute-done | bytes 1048608 | tf_op jit(solution)/shard_map/ppermute | solution.py:491
  103.6 7.1 %collective-permute-start.12 = (bf16[256,512]{1,0:T(8,128)(2,1)S(1)}, bf16[256,512]{1,0:T(8,128)(2,1)S(1)}, u32[]{:S(2)}, u32[]{:S(2)}) collective-permute-start(bf16[256,512]{1,0:T(8,128)(2,1)S(1)} %add_convert_fusion.refs_0_), channel_id=1, source_target_pairs={{0,6},{2,4},{4,2},{6,0},{8,14},{10,12},{12,10},{14,8},{16,22},{18,... | collective-permute-start | bytes 786440 | tf_op jit(solution)/shard_map/ppermute | solution.py:625
  110.7 6.2 %collective-permute-start.11 = (bf16[256,512]{1,0:T(8,128)(2,1)S(1)}, bf16[256,512]{1,0:T(8,128)(2,1)S(1)}, u32[]{:S(2)}, u32[]{:S(2)}) collective-permute-start(bf16[256,512]{1,0:T(8,128)(2,1)S(1)} %add_convert_fusion.refs_0_), channel_id=1, source_target_pairs={{0,4},{2,6},{4,0},{6,2},{8,12},{10,14},{12,8},{14,10},{16,20},{18,... | collective-permute-start | bytes 786440 | tf_op jit(solution)/shard_map/ppermute | solution.py:625
  116.8 1.9 %collective-permute-start.10 = (bf16[256,512]{1,0:T(8,128)(2,1)S(1)}, bf16[256,512]{1,0:T(8,128)(2,1)S(1)}, u32[]{:S(2)}, u32[]{:S(2)}) collective-permute-start(bf16[256,512]{1,0:T(8,128)(2,1)S(1)} %add_convert_fusion.refs_0_), channel_id=1, source_target_pairs={{0,2},{2,0},{4,6},{6,4},{8,10},{10,8},{12,14},{14,12},{16,18},{18,... | collective-permute-start | bytes 786440 | tf_op jit(solution)/shard_map/ppermute | solution.py:625
  118.8 1.3 collective-permute-start.13
  120.1 1.3 collective-permute-start.16
  122.1 1.3 collective-permute-start.15
  123.4 1.7 %collective-permute-done.10.refs_1_ = bf16[256,512]{1,0:T(8,128)(2,1)S(1)} collective-permute-done((bf16[256,512]{1,0:T(8,128)(2,1)S(1)}, bf16[256,512]{1,0:T(8,128)(2,1)S(1)}, u32[]{:S(2)}, u32[]{:S(2)}) %collective-permute-start.10) | collective-permute-done | bytes 262176 | tf_op jit(solution)/shard_map/ppermute | solution.py:625
  126.4 2.8 %finish.1 = f32[256,2,2048]{2,1,0:T(2,128)} custom-call(f32[256,4096]{1,0:T(8,128)S(1)} %own_rows.1.own, bf16[256,2048]{1,0:T(8,128)(2,1)S(1)} %collective-permute-done.3.refs_0_, bf16[256,2048]{1,0:T(8,128)(2,1)S(1)} %collective-permute-done.9.refs_1_), custom_call_target="tpu_custom_call" | custom-call | flops 1000000 | bytes 10485760 | tf_op jit(solution)/shard_map/finish/pallas_call | solution.py:474
  129.2 2.1 %unpack.1 = f32[4,256,2,256]{3,2,1,0:T(2,128)} custom-call(s32[5]{0:T(128)S(1)} %stack.39.order, bf16[256,512]{1,0:T(8,128)(2,1)S(1)} %add_convert_fusion.refs_0_, bf16[256,512]{1,0:T(8,128)(2,1)S(1)} %collective-permute-done.10.refs_1_, bf16[256,512]{1,0:T(8,128)(2,1)S(1)} %collective-permute-done.11.refs_2_, ...), custom_call_target="tpu_custom_call" | custom-call | flops 1000000 | bytes 4194304 | tf_op jit(solution)/shard_map/unpack/pallas_call | solution.py:532
  (38 shorter events, 9.2 us)
Async XLA Ops:
  0.6 1.2 slice-start
  0.6 4.3 %slice-start.1 = ((bf16[256,2,2048]{2,1,0:T(2,128)(2,1)}), bf16[256,2,512]{2,1,0:T(2,128)(2,1)S(1)}, s32[]{:S(2)}) async-start(bf16[256,2,2048]{2,1,0:T(2,128)(2,1)} %param.8), calls=%async_computation.1 | async-start | bytes 1048576 | tf_op jit(solution)/shard_map/slice | solution.py:641
  2.8 5.5 %slice-start.2 = ((bf16[256,2,2048]{2,1,0:T(2,128)(2,1)}), bf16[256,2,640]{2,1,0:T(2,128)(2,1)S(1)}, s32[]{:S(2)}) async-start(bf16[256,2,2048]{2,1,0:T(2,128)(2,1)} %param.8), calls=%async_computation.2 | async-start | bytes 1310720 | tf_op jit(solution)/shard_map/slice | solution.py:641
  2.8 15.6 %collective-permute-start = (bf16[256,1792]{1,0:T(8,128)(2,1)}, bf16[256,1792]{1,0:T(8,128)(2,1)S(1)}, u32[]{:S(2)}, u32[]{:S(2)}) collective-permute-start(bf16[256,1792]{1,0:T(8,128)(2,1)} %bitcast.14), channel_id=1, source_target_pairs={{1,0},{2,1},{3,2},{4,3},{5,4},{6,5},{7,6},{8,7},{9,8},{10,9},{11,1... | collective-permute-start | bytes 2752520 | tf_op jit(solution)/shard_map/ppermute | solution.py:491
  4.9 7.9 %copy-start.2 = (s32[6]{0:T(128)S(1)}, s32[6]{0:T(128)}, u32[]{:S(2)}) copy-start(s32[6]{0:T(128)} %param.11) | copy-start | bytes 76
  4.9 7.9 %copy-start.3 = (s32[6]{0:T(128)S(1)}, s32[6]{0:T(128)}, u32[]{:S(2)}) copy-start(s32[6]{0:T(128)} %param.12) | copy-start | bytes 76
  4.9 7.9 %copy-start.4 = (s32[6]{0:T(128)S(1)}, s32[6]{0:T(128)}, u32[]{:S(2)}) copy-start(s32[6]{0:T(128)} %param.13) | copy-start | bytes 76
  5.8 34.8 %collective-permute-start.2 = (bf16[256,1024]{1,0:T(8,128)(2,1)}, bf16[256,1024]{1,0:T(8,128)(2,1)S(1)}, u32[]{:S(2)}, u32[]{:S(2)}) collective-permute-start(bf16[256,1024]{1,0:T(8,128)(2,1)} %bitcast.18), channel_id=1, source_target_pairs={{1,0},{2,1},{3,2},{4,3},{5,4},{6,5},{7,6},{8,7},{9,8},{10,9},{11,1... | collective-permute-start | bytes 1572872 | tf_op jit(solution)/shard_map/ppermute | solution.py:491
  9.3 19.4 %collective-permute-start.1 = (bf16[256,1280]{1,0:T(8,128)(2,1)}, bf16[256,1280]{1,0:T(8,128)(2,1)}, u32[]{:S(2)}, u32[]{:S(2)}) collective-permute-start(bf16[256,1280]{1,0:T(8,128)(2,1)} %bitcast.16), channel_id=1, source_target_pairs={{1,0},{2,1},{3,2},{4,3},{5,4},{6,5},{7,6},{8,7},{9,8},{10,9},{11,1... | collective-permute-start | bytes 1966088 | tf_op jit(solution)/shard_map/ppermute | solution.py:491
  15.8 2.6 %copy-start = (bf16[6,256,256]{2,1,0:T(8,128)(2,1)S(1)}, bf16[6,256,256]{2,1,0:T(8,128)(2,1)}, u32[]{:S(2)}) copy-start(bf16[6,256,256]{2,1,0:T(8,128)(2,1)} %refs_4_.4) | copy-start | bytes 2359300
  15.8 2.6 %copy-start.1 = (bf16[6,256,256]{2,1,0:T(8,128)(2,1)S(1)}, bf16[6,256,256]{2,1,0:T(8,128)(2,1)}, u32[]{:S(2)}) copy-start(bf16[6,256,256]{2,1,0:T(8,128)(2,1)} %constant.44.clone.refs_4_.refs_5_) | copy-start | bytes 2359300
  38.5 16.1 %collective-permute-start.3 = (bf16[256,2048]{1,0:T(8,128)(2,1)S(1)}, bf16[256,2048]{1,0:T(8,128)(2,1)S(1)}, u32[]{:S(2)}, u32[]{:S(2)}) collective-permute-start(bf16[256,2048]{1,0:T(8,128)(2,1)S(1)} %below_early.1), channel_id=1, source_target_pairs={{0,1},{1,2},{2,3},{3,4},{4,5},{5,6},{6,7},{7,8},{8,9},{9,10},{10,1... | collective-permute-start | bytes 3145736 | tf_op jit(solution)/shard_map/ppermute | solution.py:491
  54.6 8.0 %collective-permute-start.4 = (bf16[4,256,512]{2,1,0:T(8,128)(2,1)S(1)}, bf16[4,256,512]{2,1,0:T(8,128)(2,1)S(1)}, u32[]{:S(2)}, u32[]{:S(2)}) collective-permute-start(bf16[4,256,512]{2,1,0:T(8,128)(2,1)S(1)} %get-tuple-element.42), channel_id=1, source_target_pairs={{1,0},{3,2},{5,4},{7,6},{9,8},{11,10},{13,12},{15,14},{17,16},{19,... | collective-permute-start | bytes 3145736 | tf_op jit(solution)/shard_map/ppermute | solution.py:610
  63.6 20.4 %collective-permute-start.5 = (bf16[256,512]{1,0:T(8,128)(2,1)S(1)}, bf16[256,512]{1,0:T(8,128)(2,1)S(1)}, u32[]{:S(2)}, u32[]{:S(2)}) collective-permute-start(bf16[256,512]{1,0:T(8,128)(2,1)S(1)} %get-tuple-element.44), channel_id=1, source_target_pairs={{0,2},{2,0},{4,6},{6,4},{8,10},{10,8},{12,14},{14,12},{16,18},{18,... | collective-permute-start | bytes 786440 | tf_op jit(solution)/shard_map/ppermute | solution.py:613
  76.2 8.3 %collective-permute-start.6 = (bf16[256,512]{1,0:T(8,128)(2,1)S(1)}, bf16[256,512]{1,0:T(8,128)(2,1)S(1)}, u32[]{:S(2)}, u32[]{:S(2)}) collective-permute-start(bf16[256,512]{1,0:T(8,128)(2,1)S(1)} %get-tuple-element.45), channel_id=1, source_target_pairs={{0,4},{2,6},{4,0},{6,2},{8,12},{10,14},{12,8},{14,10},{16,20},{18,... | collective-permute-start | bytes 786440 | tf_op jit(solution)/shard_map/ppermute | solution.py:613
  78.1 9.2 %collective-permute-start.7 = (bf16[256,512]{1,0:T(8,128)(2,1)S(1)}, bf16[256,512]{1,0:T(8,128)(2,1)S(1)}, u32[]{:S(2)}, u32[]{:S(2)}) collective-permute-start(bf16[256,512]{1,0:T(8,128)(2,1)S(1)} %get-tuple-element.46), channel_id=1, source_target_pairs={{0,6},{2,4},{4,2},{6,0},{8,14},{10,12},{12,10},{14,8},{16,22},{18,... | collective-permute-start | bytes 786440 | tf_op jit(solution)/shard_map/ppermute | solution.py:613
  87.3 16.1 %collective-permute-start.9 = (bf16[256,2048]{1,0:T(8,128)(2,1)S(1)}, bf16[256,2048]{1,0:T(8,128)(2,1)S(1)}, u32[]{:S(2)}, u32[]{:S(2)}) collective-permute-start(bf16[256,2048]{1,0:T(8,128)(2,1)S(1)} %below_late.1), channel_id=1, source_target_pairs={{0,1},{1,2},{2,3},{3,4},{4,5},{5,6},{6,7},{7,8},{8,9},{9,10},{10,1... | collective-permute-start | bytes 3145736 | tf_op jit(solution)/shard_map/ppermute | solution.py:491
  89.4 12.0 %collective-permute-start.8 = (bf16[256,512]{1,0:T(8,128)(2,1)S(1)}, bf16[256,512]{1,0:T(8,128)(2,1)S(1)}, u32[]{:S(2)}, u32[]{:S(2)}) collective-permute-start(bf16[256,512]{1,0:T(8,128)(2,1)S(1)} %fusion), channel_id=1, source_target_pairs={{0,8},{2,10},{4,12},{6,14},{8,0},{10,2},{12,4},{14,6},{16,24},{18,... | collective-permute-start | bytes 786440 | tf_op jit(solution)/shard_map/ppermute | solution.py:619
  103.6 16.5 %collective-permute-start.12 = (bf16[256,512]{1,0:T(8,128)(2,1)S(1)}, bf16[256,512]{1,0:T(8,128)(2,1)S(1)}, u32[]{:S(2)}, u32[]{:S(2)}) collective-permute-start(bf16[256,512]{1,0:T(8,128)(2,1)S(1)} %add_convert_fusion.refs_0_), channel_id=1, source_target_pairs={{0,6},{2,4},{4,2},{6,0},{8,14},{10,12},{12,10},{14,8},{16,22},{18,... | collective-permute-start | bytes 786440 | tf_op jit(solution)/shard_map/ppermute | solution.py:625
  110.7 11.4 %collective-permute-start.11 = (bf16[256,512]{1,0:T(8,128)(2,1)S(1)}, bf16[256,512]{1,0:T(8,128)(2,1)S(1)}, u32[]{:S(2)}, u32[]{:S(2)}) collective-permute-start(bf16[256,512]{1,0:T(8,128)(2,1)S(1)} %add_convert_fusion.refs_0_), channel_id=1, source_target_pairs={{0,4},{2,6},{4,0},{6,2},{8,12},{10,14},{12,8},{14,10},{16,20},{18,... | collective-permute-start | bytes 786440 | tf_op jit(solution)/shard_map/ppermute | solution.py:625
  116.8 8.3 %collective-permute-start.10 = (bf16[256,512]{1,0:T(8,128)(2,1)S(1)}, bf16[256,512]{1,0:T(8,128)(2,1)S(1)}, u32[]{:S(2)}, u32[]{:S(2)}) collective-permute-start(bf16[256,512]{1,0:T(8,128)(2,1)S(1)} %add_convert_fusion.refs_0_), channel_id=1, source_target_pairs={{0,2},{2,0},{4,6},{6,4},{8,10},{10,8},{12,14},{14,12},{16,18},{18,... | collective-permute-start | bytes 786440 | tf_op jit(solution)/shard_map/ppermute | solution.py:625
  118.8 10.4 %collective-permute-start.13 = (bf16[256,512]{1,0:T(8,128)(2,1)S(1)}, bf16[256,512]{1,0:T(8,128)(2,1)S(1)}, u32[]{:S(2)}, u32[]{:S(2)}) collective-permute-start(bf16[256,512]{1,0:T(8,128)(2,1)S(1)} %add_convert_fusion.refs_0_), channel_id=1, source_target_pairs={{0,1},{2,3},{4,5},{6,7},{8,9},{10,11},{12,13},{14,15},{16,17},{18,... | collective-permute-start | bytes 786440 | tf_op jit(solution)/shard_map/ppermute | solution.py:626
  120.1 9.1 %collective-permute-start.16 = (bf16[256,512]{1,0:T(8,128)(2,1)S(1)}, bf16[256,512]{1,0:T(8,128)(2,1)S(1)}, u32[]{:S(2)}, u32[]{:S(2)}) collective-permute-start(bf16[256,512]{1,0:T(8,128)(2,1)S(1)} %collective-permute-done.12.refs_3_), channel_id=1, source_target_pairs={{0,1},{2,3},{4,5},{6,7},{8,9},{10,11},{12,13},{14,15},{16,17},{18,... | collective-permute-start | bytes 786440 | tf_op jit(solution)/shard_map/ppermute | solution.py:626
  122.1 7.2 %collective-permute-start.15 = (bf16[256,512]{1,0:T(8,128)(2,1)S(1)}, bf16[256,512]{1,0:T(8,128)(2,1)S(1)}, u32[]{:S(2)}, u32[]{:S(2)}) collective-permute-start(bf16[256,512]{1,0:T(8,128)(2,1)S(1)} %collective-permute-done.11.refs_2_), channel_id=1, source_target_pairs={{0,1},{2,3},{4,5},{6,7},{8,9},{10,11},{12,13},{14,15},{16,17},{18,... | collective-permute-start | bytes 786440 | tf_op jit(solution)/shard_map/ppermute | solution.py:626
  125.1 4.1 %collective-permute-start.14 = (bf16[256,512]{1,0:T(8,128)(2,1)S(1)}, bf16[256,512]{1,0:T(8,128)(2,1)S(1)}, u32[]{:S(2)}, u32[]{:S(2)}) collective-permute-start(bf16[256,512]{1,0:T(8,128)(2,1)S(1)} %collective-permute-done.10.refs_1_), channel_id=1, source_target_pairs={{0,1},{2,3},{4,5},{6,7},{8,9},{10,11},{12,13},{14,15},{16,17},{18,... | collective-permute-start | bytes 786440 | tf_op jit(solution)/shard_map/ppermute | solution.py:626

commit v6 on v2

--- a/solution.py
+++ b/solution.py
@@ -13,8 +13,8 @@
 F32 = jnp.float32
 BF16 = jnp.bfloat16
 LANES = 128
-VMEM_BYTES = 36 * 2**20
-VMEM_SMALL = 20 * 2**20
+VMEM_BYTES = 26 * 2**20
+VMEM_SMALL = 16 * 2**20
 
 
 def dft_tables(size):
@@ -492,100 +492,91 @@
 
 
 def unpack_kernel(order, *refs):
-    n = (len(refs) - 4) // 2
-    out, wide, narrow, sems = refs[2 * n :]
-    rows = wide.shape[1]
-    size = out.shape[1]
-    span = min(rows, size)
-    for core in range(2):
-
-        @pl.when(order[n] == core)
-        def _():
-            for i in range(n):
-                pltpu.make_async_copy(refs[core * n + i], narrow.at[i], sems.at[0, i]).start()
-
+    pieces, out, wide, sems = refs[:-3], refs[-3], refs[-2], refs[-1]
+    rows = pieces[0].shape[0]
+    modes, size, _, _ = out.shape
     copies = []
-    for i in range(n):
-        pltpu.make_async_copy(refs[i], narrow.at[i], sems.at[0, i]).wait()
-        wide[i] = narrow[i].astype(F32)
-        for j in range(rows // span):
-            line = order[i] * rows + j * span
-            mode = line // size
-            at = pl.multiple_of(line % size, 8)
-            for part in range(2):
-                copies.append(
-                    pltpu.make_async_copy(
-                        wide.at[i, pl.ds(j * span, span), pl.ds(part * size, size)],
-                        out.at[mode, pl.ds(at, span), part, :],
-                        sems.at[1, len(copies)],
-                    )
-                )
-                copies[-1].start()
+    for i, piece in enumerate(pieces):
+        wide[i * rows : (i + 1) * rows] = piece[...].astype(F32)
+        mode = order[i] // (size // rows)
+        at = pl.multiple_of(order[i] % (size // rows) * rows, 8)
+        for part in range(2):
+            copy = pltpu.make_async_copy(
+                wide.at[pl.ds(i * rows, rows), pl.ds(part * size, size)],
+                out.at[mode, pl.ds(at, rows), part, :],
+                sems.at[2 * i + part],
+            )
+            copy.start()
+            copies.append(copy)
     for copy in copies:
         copy.wait()
 
 
-def unpacked(pieces, others, order, shape):
-    n = len(pieces)
-    rows, columns = pieces[0].shape
-    hbm = pl.BlockSpec(memory_space=pl.ANY)
+def unpacked(pieces, order, shape):
+    vmem = pl.BlockSpec(memory_space=pltpu.VMEM)
+    smem = pl.BlockSpec(memory_space=pltpu.SMEM)
     return pl.pallas_call(
         unpack_kernel,
-        in_specs=[pl.BlockSpec(memory_space=pltpu.SMEM)] + [hbm] * (2 * n),
-        out_specs=hbm,
+        in_specs=[smem] + [vmem] * len(pieces),
+        out_specs=pl.BlockSpec(memory_space=pl.ANY),
         out_shape=jax.ShapeDtypeStruct(shape, F32),
         scratch_shapes=[
-            pltpu.VMEM((n, rows, columns), F32),
-            pltpu.VMEM((n, rows, columns), BF16),
-            pltpu.SemaphoreType.DMA((2, 2 * n * max(1, rows // shape[1]))),
+            pltpu.VMEM((len(pieces) * pieces[0].shape[0], pieces[0].shape[1]), F32),
+            pltpu.SemaphoreType.DMA((2 * len(pieces),)),
         ],
-        compiler_params=pltpu.CompilerParams(vmem_limit_bytes=VMEM_SMALL),
-        cost_estimate=pl.CostEstimate(flops=10**6, bytes_accessed=4 * 2**20, transcendentals=0),
+        compiler_params=pltpu.CompilerParams(vmem_limit_bytes=VMEM_BYTES),
         name="unpack",
-    )(order, *pieces, *others)
-
-
-def near_chips(axis):
-    return min(4, lax.axis_size(axis) // 2)
+    )(order, *pieces)
 
 
 def piece_order(axis):
-    near = near_chips(axis)
+    length = lax.axis_size(axis)
+    near = min(4, length // 2)
     me = lax.axis_index(axis)
     core, spot = me % 2, me // 2 % near
-    return jnp.stack([spot ^ s for s in range(near)] + [core])
-
-
-def hop(axis, shift, stride):
-    return [(i, i ^ (2 * stride * shift)) for i in range(0, lax.axis_size(axis), 2)]
-
-
-def summed(given, axis, shape, order, beside, between):
+    return jnp.stack(
+        [core * near + (spot ^ s) for s in range(near)] + [(1 - core) * near + (spot ^ s) for s in range(near)]
+    )
+
+
+def summed(given, axis, shape, order, beside, during, between, last):
     length = lax.axis_size(axis)
-    near = near_chips(axis)
-    far = length // 2 // near
-    inward = [(i + 1, i) for i in range(0, length, 2)]
-    outward = [(i, i + 1) for i in range(0, length, 2)]
-    modes, size, columns = given.shape
-    spot = lax.axis_index(axis) // 2 % near
-    sibling = beside(lax.ppermute(given, axis, inward))
-    parts = (given.astype(F32) + sibling.astype(F32)).astype(BF16).reshape(near, modes * size // near, columns)
+    chips = length // 2
+    near = min(4, chips)
+    far = chips // near
+    me = lax.axis_index(axis)
+    core, chip = me % 2, me // 2
+    across = [(i, i ^ 1) for i in range(length)]
+
+    def hop(shift, stride):
+        return [(i, i ^ (2 * stride * shift)) for i in range(length)]
+
+    size, columns = given.shape[1:]
+    given = given.reshape((2, given.shape[0] // 2) + given.shape[1:])
+    keep = lax.dynamic_index_in_dim(given, core, 0, False)
+    give = lax.dynamic_index_in_dim(given, 1 - core, 0, False)
+    mine = (keep.astype(F32) + beside(lax.ppermute(give, axis, across)).astype(F32)).astype(BF16)
+    rows = mine.shape[0] * size // near
+    mine = mine.reshape(near, rows, columns)
+    parts = mine.astype(BF16)
+    spot = chip % near
     got = [
-        lax.ppermute(lax.dynamic_index_in_dim(parts, spot ^ s, 0, False), axis, hop(axis, s, 1)) for s in range(1, near)
+        lax.ppermute(lax.dynamic_index_in_dim(parts, spot ^ s, 0, False), axis, hop(s, 1)) for s in range(1, near)
     ]
-    total = lax.dynamic_index_in_dim(parts, spot, 0, False).astype(F32)
+    got = during(got)
+    total = lax.dynamic_index_in_dim(mine, spot, 0, False).astype(F32)
     for piece in got:
         total = total + piece.astype(F32)
     sent = total.astype(BF16)
-    others = [lax.ppermute(sent, axis, hop(axis, s, near)) for s in range(1, far)]
+    others = [lax.ppermute(sent, axis, hop(s, near)) for s in range(1, far)]
     if others:
         others[0] = between(others[0])
     for piece in others:
         total = total + piece.astype(F32)
     total = total.astype(BF16)
-    pieces = [total] + [lax.ppermute(total, axis, hop(axis, s, 1)) for s in range(1, near)]
-    others = [lax.ppermute(piece, axis, outward) for piece in pieces]
-    return unpacked(pieces, others, order, shape)
+    pieces = [total] + [lax.ppermute(total, axis, hop(s, 1)) for s in range(1, near)]
+    others = [lax.ppermute(piece, axis, across) for piece in pieces]
+    return unpacked(pieces + others, last(order), shape)
 
 
 def column_bounds(width, shares):
@@ -616,21 +607,34 @@
         grads.append(grad)
         carried = [moved] + rest
     given = carried[1]
-    below = settle(places, grads, bounds, 0, width, size, BF16, width, "below_rows")
+    edges = (0, width // 2 // LANES * LANES, width)
+    belows = [
+        settle(places, grads, bounds, low, high, size, BF16, width, f"below_{low}")
+        for low, high in zip(edges[:-1], edges[1:])
+    ]
+    aboves = [passed_along(belows[0], "row", 1)]
     held = {}
 
     def beside(x):
-        x, held["below"] = lax.optimization_barrier((x, below))
+        return lax.optimization_barrier((x, belows[0]))[0]
+
+    def during(x):
+        x, aboves[0], held["below"] = lax.optimization_barrier((x, aboves[0], belows[1]))
         return x
 
     def between(x):
+        aboves.append(passed_along(held["below"], "row", 1))
         own_rows = settle(places, grads, bounds, 0, width, 0, F32, width, "own_rows")
-        x, held["own"] = lax.optimization_barrier((x, own_rows))
+        x, aboves[1], held["own"] = lax.optimization_barrier((x, aboves[1], own_rows))
         return x
 
-    probe_grad = summed(given, "row", probe.shape, order, beside, between)
-    above = passed_along(held["below"], "row", 1)
-    object_grad = finish(held["own"], [above], (0, width), width)
+    def last(x):
+        object_grad = finish(held["own"], aboves, edges, width)
+        x, held["object_grad"] = lax.optimization_barrier((x, object_grad))
+        return x
+
+    probe_grad = summed(given, "row", probe.shape, order, beside, during, between, last)
+    object_grad = held["object_grad"]
     return object_grad, probe_grad, moved
 
 

time: 129 us -> 120 us (0.930)
  the two profiles are of different devices: /device:TPU:0 before, /device:TPU:16 now
where the time goes in v6:
time: 120 us; the launch traced here: 119 us
  Pallas kernels  34.9 us (29%)
  starting transfers between devices  34.4 us (29%)
  waiting for transfers between devices  25 us (21%)
  local copies, waits for them, and re-layouts  20.1 us (17%)
  other arithmetic  3.32 us (3%)
  between operations  1.78 us (1%)
    ppermute x4, starting transfers between devices, passed_along(): return lax.ppermute(x, axis, pairs)  21.3 us
    pallas_call x2, Pallas kernels, project(): pl.pallas_call(functools.partial(project_kernel, size, width, bounds, sta...  16.5 us
    unnamed x29, local copies, waits for them, and re-layouts  14 us
    ppermute x4, waiting for transfers between devices, passed_along(): return lax.ppermute(x, axis, pairs)  13.7 us
    pallas_call x3, Pallas kernels, settle(): pl.pallas_call(functools.partial(settle_kernel, size, bounds, low, high,...  12.8 us
    ppermute x3, starting transfers between devices, summed(): lax.ppermute(total, axis, hop(s, 1))  6.44 us
    ppermute x3, starting transfers between devices, summed(): lax.ppermute(lax.dynamic_index_in_dim(parts, spot ^ s, 0, False), axis, h...  5.82 us
    ppermute x3, waiting for transfers between devices, summed(): lax.ppermute(total, axis, hop(s, 1))  4.37 us
  transfers between devices with their start and end apart: 16, of which 7 were waited for; matrix products, arithmetic and copies ran while one was open for 10% of the time, Pallas kernels for 18%

profile of v6, /device:TPU:16, one launch (start us, length us, event | category | flops | bytes accessed | tf_op | source)
XLA Modules:
  0.0 119.4 jit_solution(13423468159841938207)
XLA Ops:
  0.6 1.3 %slice-done = bf16[256,2,1152]{2,1,0:T(2,128)(2,1)S(1)} async-done(((bf16[256,2,2048]{2,1,0:T(2,128)(2,1)}), bf16[256,2,1152]{2,1,0:T(2,128)(2,1)S(1)}, s32[]{:S(2)}) %slice-start) | async-done | bytes 1179672 | tf_op jit(solution)/shard_map/slice | solution.py:593
  1.9 1.2 copy.13
  3.1 2.8 %collective-permute-start.1 = (bf16[256,2304]{1,0:T(8,128)(2,1)}, bf16[256,2304]{1,0:T(8,128)(2,1)S(1)}, u32[]{:S(2)}, u32[]{:S(2)}) collective-permute-start(bf16[256,2304]{1,0:T(8,128)(2,1)} %bitcast.27), channel_id=1, source_target_pairs={{1,0},{2,1},{3,2},{4,3},{5,4},{6,5},{7,6},{8,7},{9,8},{10,9},{11,1... | collective-permute-start | bytes 3538952 | tf_op jit(solution)/shard_map/ppermute | solution.py:491
  5.9 1.1 copy.12
  7.0 2.6 %collective-permute-start = (bf16[256,1792]{1,0:T(8,128)(2,1)}, bf16[256,1792]{1,0:T(8,128)(2,1)}, u32[]{:S(2)}, u32[]{:S(2)}) collective-permute-start(bf16[256,1792]{1,0:T(8,128)(2,1)} %bitcast.25), channel_id=1, source_target_pairs={{1,0},{2,1},{3,2},{4,3},{5,4},{6,5},{7,6},{8,7},{9,8},{10,9},{11,1... | collective-permute-start | bytes 2752520 | tf_op jit(solution)/shard_map/ppermute | solution.py:491
  10.4 3.9 %reshape.34.refs_2_.refs_3_ = f32[4,256,512]{2,1,0:T(8,128)} reshape(f32[4,256,2,256]{3,2,1,0:T(2,128)} %param.9) | data formatting | bytes 4194304 | tf_op jit(solution)/shard_map/reshape | solution.py:602
  14.3 3.8 %copy.11 = bf16[32,8,2,2048]{3,1,2,0:T(8,128)(2,1)} copy(bf16[32,8,2,2048]{3,2,1,0:T(2,128)(2,1)} %bitcast.43) | data formatting | bytes 4194304
  18.1 1.8 %collective-permute-done.1.refs_1_.refs_2_ = bf16[256,2304]{1,0:T(8,128)(2,1)S(1)} collective-permute-done((bf16[256,2304]{1,0:T(8,128)(2,1)}, bf16[256,2304]{1,0:T(8,128)(2,1)S(1)}, u32[]{:S(2)}, u32[]{:S(2)}) %collective-permute-start.1) | collective-permute-done | bytes 1179680 | tf_op jit(solution)/shard_map/ppermute | solution.py:491
  19.9 2.0 %copy-done = f32[4,256,512]{2,1,0:T(8,128)S(1)} copy-done((f32[4,256,512]{2,1,0:T(8,128)S(1)}, f32[4,256,512]{2,1,0:T(8,128)}, u32[]{:S(2)}) %copy-start) | copy-done | bytes 2097176
  22.0 1.6 %copy-done.1 = bf16[32,8,2,2048]{3,1,2,0:T(8,128)(2,1)S(1)} copy-done((bf16[32,8,2,2048]{3,1,2,0:T(8,128)(2,1)S(1)}, bf16[32,8,2,2048]{3,1,2,0:T(8,128)(2,1)}, u32[]{:S(2)}) %copy-start.1) | copy-done | bytes 2097176
  23.6 1.1 copy-done.5
  24.7 1.1 copy-done.7
  25.8 9.8 %project_0.1 = (f32[2,6]{1,0:T(2,128)S(1)}, bf16[6,256,512]{2,1,0:T(8,128)(2,1)S(1)}, f32[4,256,512]{2,1,0:T(8,128)S(1)}) custom-call(s32[5,6]{1,0:T(8,128)S(1)} %stack.42.places, bf16[256,4096]{1,0:T(8,128)(2,1)S(1)} %bitcast.39, bf16[256,2304]{1,0:T(8,128)(2,1)S(1)} %collective-permute-done.1.refs_1_.refs_2_, f32[4,256,512]{2,1,0:T(8,128)S(1)} %copy-done, ...), custom_call_target="tpu_custom_call" | custom-call | flops 8000000000 | bytes 16777216 | tf_op jit(solution)/shard_map/project_0/pallas_call | solution.py:343
  35.6 1.3 %copy-done.4 = bf16[256,2304]{1,0:T(8,128)(2,1)S(1)} copy-done((bf16[256,2304]{1,0:T(8,128)(2,1)S(1)}, bf16[256,2304]{1,0:T(8,128)(2,1)}, u32[]{:S(2)}) %copy-start.4) | copy-done | bytes 1179672
  36.9 6.7 %project_1.1 = (f32[2,6]{1,0:T(2,128)}, bf16[6,256,512]{2,1,0:T(8,128)(2,1)S(1)}, bf16[4,256,512]{2,1,0:T(8,128)(2,1)S(1)}) custom-call(s32[5,6]{1,0:T(8,128)S(1)} %stack.42.places, bf16[256,4096]{1,0:T(8,128)(2,1)S(1)} %bitcast.40, bf16[256,1792]{1,0:T(8,128)(2,1)} %collective-permute-done.refs_1_, bf16[256,2304]{1,0:T(8,128)(2,1)S(1)} %copy-done.4, ...), custom_call_target="tpu_custom_call" | custom-call | flops 8000000000 | bytes 16777216 | tf_op jit(solution)/shard_map/project_1/pallas_call | solution.py:343
  43.7 4.1 %below_0.1 = bf16[256,2048]{1,0:T(8,128)(2,1)} custom-call(s32[5,6]{1,0:T(8,128)S(1)} %stack.42.places, bf16[6,256,512]{2,1,0:T(8,128)(2,1)S(1)} %get-tuple-element.27.refs_0_, bf16[6,256,512]{2,1,0:T(8,128)(2,1)S(1)} %get-tuple-element.28.refs_1_), custom_call_target="tpu_custom_call" | custom-call | flops 1000000000 | bytes 8388608 | tf_op jit(solution)/shard_map/below_0/pallas_call | solution.py:425
  47.8 14.0 %collective-permute-start.6 = (bf16[256,2048]{1,0:T(8,128)(2,1)}, bf16[256,2048]{1,0:T(8,128)(2,1)}, u32[]{:S(2)}, u32[]{:S(2)}) collective-permute-start(bf16[256,2048]{1,0:T(8,128)(2,1)} %below_0.1), channel_id=1, source_target_pairs={{0,1},{1,2},{2,3},{3,4},{4,5},{5,6},{6,7},{7,8},{8,9},{9,10},{10,1... | collective-permute-start | bytes 3145736 | tf_op jit(solution)/shard_map/ppermute | solution.py:491
  62.8 2.3 %collective-permute-done.2 = bf16[2,256,512]{2,1,0:T(8,128)(2,1)} collective-permute-done((bf16[2,256,512]{2,1,0:T(8,128)(2,1)}, bf16[2,256,512]{2,1,0:T(8,128)(2,1)}, u32[]{:S(2)}, u32[]{:S(2)}) %collective-permute-start.2) | collective-permute-done | bytes 524320 | tf_op jit(solution)/shard_map/ppermute | solution.py:558
  65.1 1.3 %fusion = bf16[2,256,512]{2,1,0:T(8,128)(2,1)S(1)} fusion(bf16[2,256,512]{2,1,0:T(8,128)(2,1)} %collective-permute-done.2, bf16[2,2,256,512]{3,2,1,0:T(8,128)(2,1)} %bitcast.42, s32[]{:T(128)S(6)} %select_n.45), kind=kLoop, calls=%fused_computation.1 | loop fusion | flops 1048576 | bytes 1572868 | tf_op jit(solution)/shard_map/convert_element_type | solution.py:558
  67.4 5.7 %collective-permute-start.4 = (bf16[128,512]{1,0:T(8,128)(2,1)S(1)}, bf16[128,512]{1,0:T(8,128)(2,1)S(1)}, u32[]{:S(2)}, u32[]{:S(2)}) collective-permute-start(bf16[128,512]{1,0:T(8,128)(2,1)S(1)} %get-tuple-element.42), channel_id=1, source_target_pairs={{0,4},{1,5},{2,6},{3,7},{4,0},{5,1},{6,2},{7,3},{8,12},{9,13},{10,... | collective-permute-start | bytes 393224 | tf_op jit(solution)/shard_map/ppermute | solution.py:564
  73.1 4.1 %below_1024.1 = bf16[256,2048]{1,0:T(8,128)(2,1)} custom-call(s32[5,6]{1,0:T(8,128)S(1)} %stack.42.places, bf16[6,256,512]{2,1,0:T(8,128)(2,1)S(1)} %get-tuple-element.27.refs_0_, bf16[6,256,512]{2,1,0:T(8,128)(2,1)S(1)} %get-tuple-element.28.refs_1_), custom_call_target="tpu_custom_call" | custom-call | flops 1000000000 | bytes 8388608 | tf_op jit(solution)/shard_map/below_1024/pallas_call | solution.py:425
  77.3 2.4 %collective-permute-done.4 = bf16[128,512]{1,0:T(8,128)(2,1)S(1)} collective-permute-done((bf16[128,512]{1,0:T(8,128)(2,1)S(1)}, bf16[128,512]{1,0:T(8,128)(2,1)S(1)}, u32[]{:S(2)}, u32[]{:S(2)}) %collective-permute-start.4) | collective-permute-done | bytes 131104 | tf_op jit(solution)/shard_map/ppermute | solution.py:564
  79.7 2.0 %collective-permute-start.8 = (bf16[256,2048]{1,0:T(8,128)(2,1)}, bf16[256,2048]{1,0:T(8,128)(2,1)}, u32[]{:S(2)}, u32[]{:S(2)}) collective-permute-start(bf16[256,2048]{1,0:T(8,128)(2,1)} %below_1024.1), channel_id=1, source_target_pairs={{0,1},{1,2},{2,3},{3,4},{4,5},{5,6},{6,7},{7,8},{8,9},{9,10},{10,1... | collective-permute-start | bytes 3145736 | tf_op jit(solution)/shard_map/ppermute | solution.py:491
  82.8 4.5 %own_rows.1.own = f32[256,4096]{1,0:T(8,128)S(1)} custom-call(s32[5,6]{1,0:T(8,128)S(1)} %stack.42.places, bf16[6,256,512]{2,1,0:T(8,128)(2,1)S(1)} %get-tuple-element.27.refs_0_, bf16[6,256,512]{2,1,0:T(8,128)(2,1)S(1)} %get-tuple-element.28.refs_1_), custom_call_target="tpu_custom_call" | custom-call | flops 1000000000 | bytes 8388608 | tf_op jit(solution)/shard_map/own_rows/pallas_call | solution.py:425
  87.3 2.1 %collective-permute-done.7 = bf16[128,512]{1,0:T(8,128)(2,1)S(1)} collective-permute-done((bf16[128,512]{1,0:T(8,128)(2,1)S(1)}, bf16[128,512]{1,0:T(8,128)(2,1)S(1)}, u32[]{:S(2)}, u32[]{:S(2)}) %collective-permute-start.7) | collective-permute-done | bytes 131104 | tf_op jit(solution)/shard_map/ppermute | solution.py:571
  89.4 11.9 %collective-permute-done.8.refs_1_ = bf16[256,2048]{1,0:T(8,128)(2,1)} collective-permute-done((bf16[256,2048]{1,0:T(8,128)(2,1)}, bf16[256,2048]{1,0:T(8,128)(2,1)}, u32[]{:S(2)}, u32[]{:S(2)}) %collective-permute-start.8) | collective-permute-done | bytes 1048608 | tf_op jit(solution)/shard_map/ppermute | solution.py:491
  101.3 1.0 add_convert_fusion.refs_0_
  102.9 4.4 %collective-permute-start.10 = (bf16[128,512]{1,0:T(8,128)(2,1)S(1)}, bf16[128,512]{1,0:T(8,128)(2,1)S(1)}, u32[]{:S(2)}, u32[]{:S(2)}) collective-permute-start(bf16[128,512]{1,0:T(8,128)(2,1)S(1)} %add_convert_fusion.refs_0_), channel_id=1, source_target_pairs={{0,4},{1,5},{2,6},{3,7},{4,0},{5,1},{6,2},{7,3},{8,12},{9,13},{10,... | collective-permute-start | bytes 393224 | tf_op jit(solution)/shard_map/ppermute | solution.py:577
  107.3 1.4 %collective-permute-start.9 = (bf16[128,512]{1,0:T(8,128)(2,1)S(1)}, bf16[128,512]{1,0:T(8,128)(2,1)S(1)}, u32[]{:S(2)}, u32[]{:S(2)}) collective-permute-start(bf16[128,512]{1,0:T(8,128)(2,1)S(1)} %add_convert_fusion.refs_0_), channel_id=1, source_target_pairs={{0,2},{1,3},{2,0},{3,1},{4,6},{5,7},{6,4},{7,5},{8,10},{9,11},{10,... | collective-permute-start | bytes 393224 | tf_op jit(solution)/shard_map/ppermute | solution.py:577
  109.6 3.5 %collective-permute-done.10.refs_2_ = bf16[128,512]{1,0:T(8,128)(2,1)S(1)} collective-permute-done((bf16[128,512]{1,0:T(8,128)(2,1)S(1)}, bf16[128,512]{1,0:T(8,128)(2,1)S(1)}, u32[]{:S(2)}, u32[]{:S(2)}) %collective-permute-start.10) | collective-permute-done | bytes 131104 | tf_op jit(solution)/shard_map/ppermute | solution.py:577
  113.6 3.6 %finish.1 = f32[256,2,2048]{2,1,0:T(2,128)} custom-call(f32[256,4096]{1,0:T(8,128)S(1)} %own_rows.1.own, bf16[256,2048]{1,0:T(8,128)(2,1)} %collective-permute-done.6.refs_0_, bf16[256,2048]{1,0:T(8,128)(2,1)} %collective-permute-done.8.refs_1_), custom_call_target="tpu_custom_call" | custom-call | flops 1000000 | bytes 10485760 | tf_op jit(solution)/shard_map/finish/pallas_call | solution.py:474
  117.3 2.0 %unpack.1 = f32[4,256,2,256]{3,2,1,0:T(2,128)} custom-call(s32[8]{0:T(128)S(1)} %stack.51.order, bf16[128,512]{1,0:T(8,128)(2,1)S(1)} %add_convert_fusion.refs_0_, bf16[128,512]{1,0:T(8,128)(2,1)S(1)} %collective-permute-done.9.refs_1_, bf16[128,512]{1,0:T(8,128)(2,1)S(1)} %collective-permute-done.10.refs_2_, ...), custom_call_target="tpu_custom_call" | custom-call | tf_op jit(solution)/shard_map/unpack/pallas_call | solution.py:518
  (50 shorter events, 5.2 us)
Async XLA Ops:
  0.6 1.3 %slice-start = ((bf16[256,2,2048]{2,1,0:T(2,128)(2,1)}), bf16[256,2,1152]{2,1,0:T(2,128)(2,1)S(1)}, s32[]{:S(2)}) async-start(bf16[256,2,2048]{2,1,0:T(2,128)(2,1)} %param.8), calls=%async_computation | async-start | bytes 2359296 | tf_op jit(solution)/shard_map/slice | solution.py:593
  1.9 4.0 %slice-start.1 = ((bf16[256,2,2048]{2,1,0:T(2,128)(2,1)}), bf16[256,2,896]{2,1,0:T(2,128)(2,1)S(1)}, s32[]{:S(2)}) async-start(bf16[256,2,2048]{2,1,0:T(2,128)(2,1)} %param.8), calls=%async_computation.1 | async-start | bytes 1835008 | tf_op jit(solution)/shard_map/slice | solution.py:593
  3.1 7.2 %copy-start.10 = (s32[6]{0:T(128)S(1)}, s32[6]{0:T(128)}, u32[]{:S(2)}) copy-start(s32[6]{0:T(128)} %param.11) | copy-start | bytes 76
  3.1 7.2 %copy-start.11 = (s32[6]{0:T(128)S(1)}, s32[6]{0:T(128)}, u32[]{:S(2)}) copy-start(s32[6]{0:T(128)} %param.12) | copy-start | bytes 76
  3.1 7.2 %copy-start.12 = (s32[6]{0:T(128)S(1)}, s32[6]{0:T(128)}, u32[]{:S(2)}) copy-start(s32[6]{0:T(128)} %param.13) | copy-start | bytes 76
  3.1 16.9 %collective-permute-start.1 = (bf16[256,2304]{1,0:T(8,128)(2,1)}, bf16[256,2304]{1,0:T(8,128)(2,1)S(1)}, u32[]{:S(2)}, u32[]{:S(2)}) collective-permute-start(bf16[256,2304]{1,0:T(8,128)(2,1)} %bitcast.27), channel_id=1, source_target_pairs={{1,0},{2,1},{3,2},{4,3},{5,4},{6,5},{7,6},{8,7},{9,8},{10,9},{11,1... | collective-permute-start | bytes 3538952 | tf_op jit(solution)/shard_map/ppermute | solution.py:491
  7.0 28.6 %collective-permute-start = (bf16[256,1792]{1,0:T(8,128)(2,1)}, bf16[256,1792]{1,0:T(8,128)(2,1)}, u32[]{:S(2)}, u32[]{:S(2)}) collective-permute-start(bf16[256,1792]{1,0:T(8,128)(2,1)} %bitcast.25), channel_id=1, source_target_pairs={{1,0},{2,1},{3,2},{4,3},{5,4},{6,5},{7,6},{8,7},{9,8},{10,9},{11,1... | collective-permute-start | bytes 2752520 | tf_op jit(solution)/shard_map/ppermute | solution.py:491
  19.9 15.6 %copy-start.3 = (bf16[256,2304]{1,0:T(8,128)(2,1)}, bf16[256,2304]{1,0:T(8,128)(2,1)S(1)}, u32[]{:S(2)}) copy-start(bf16[256,2304]{1,0:T(8,128)(2,1)S(1)} %collective-permute-done.1.refs_1_.refs_2_) | copy-start | bytes 3538948
  19.9 2.0 %copy-start = (f32[4,256,512]{2,1,0:T(8,128)S(1)}, f32[4,256,512]{2,1,0:T(8,128)}, u32[]{:S(2)}) copy-start(f32[4,256,512]{2,1,0:T(8,128)} %reshape.34.refs_2_.refs_3_) | copy-start | bytes 6291460
  22.0 1.6 %copy-start.1 = (bf16[32,8,2,2048]{3,1,2,0:T(8,128)(2,1)S(1)}, bf16[32,8,2,2048]{3,1,2,0:T(8,128)(2,1)}, u32[]{:S(2)}) copy-start(bf16[32,8,2,2048]{3,1,2,0:T(8,128)(2,1)} %copy.11) | copy-start | bytes 6291460
  23.6 1.1 copy-start.5
  24.7 1.1 copy-start.7
  25.8 9.8 %copy-start.6 = (bf16[6,256,256]{2,1,0:T(8,128)(2,1)S(1)}, bf16[6,256,256]{2,1,0:T(8,128)(2,1)}, u32[]{:S(2)}) copy-start(bf16[6,256,256]{2,1,0:T(8,128)(2,1)} %refs_4_.2) | copy-start | bytes 2359300
  25.8 9.8 %copy-start.8 = (bf16[6,256,256]{2,1,0:T(8,128)(2,1)S(1)}, bf16[6,256,256]{2,1,0:T(8,128)(2,1)}, u32[]{:S(2)}) copy-start(bf16[6,256,256]{2,1,0:T(8,128)(2,1)} %constant.67.clone.refs_4_.refs_5_) | copy-start | bytes 2359300
  35.6 1.3 %copy-start.4 = (bf16[256,2304]{1,0:T(8,128)(2,1)S(1)}, bf16[256,2304]{1,0:T(8,128)(2,1)}, u32[]{:S(2)}) copy-start(bf16[256,2304]{1,0:T(8,128)(2,1)} %copy-done.3) | copy-start | bytes 3538948
  43.6 18.1 %copy-start.2 = (bf16[4,256,512]{2,1,0:T(8,128)(2,1)}, bf16[4,256,512]{2,1,0:T(8,128)(2,1)S(1)}, u32[]{:S(2)}) copy-start(bf16[4,256,512]{2,1,0:T(8,128)(2,1)S(1)} %get-tuple-element.26) | copy-start | bytes 3145732
  47.8 31.9 %collective-permute-start.6 = (bf16[256,2048]{1,0:T(8,128)(2,1)}, bf16[256,2048]{1,0:T(8,128)(2,1)}, u32[]{:S(2)}, u32[]{:S(2)}) collective-permute-start(bf16[256,2048]{1,0:T(8,128)(2,1)} %below_0.1), channel_id=1, source_target_pairs={{0,1},{1,2},{2,3},{3,4},{4,5},{5,6},{6,7},{7,8},{8,9},{9,10},{10,1... | collective-permute-start | bytes 3145736 | tf_op jit(solution)/shard_map/ppermute | solution.py:491
  62.6 2.5 %collective-permute-start.2 = (bf16[2,256,512]{2,1,0:T(8,128)(2,1)}, bf16[2,256,512]{2,1,0:T(8,128)(2,1)}, u32[]{:S(2)}, u32[]{:S(2)}) collective-permute-start(bf16[2,256,512]{2,1,0:T(8,128)(2,1)} %dynamic-slice_bitcast_fusion), channel_id=1, source_target_pairs={{0,1},{1,0},{2,3},{3,2},{4,5},{5,4},{6,7},{7,6},{8,9},{9,8},{10,11... | collective-permute-start | bytes 1572872 | tf_op jit(solution)/shard_map/ppermute | solution.py:558
  66.5 0.8 copy-start.9
  67.3 10.0 %collective-permute-start.5 = (bf16[128,512]{1,0:T(8,128)(2,1)S(1)}, bf16[128,512]{1,0:T(8,128)(2,1)S(1)}, u32[]{:S(2)}, u32[]{:S(2)}) collective-permute-start(bf16[128,512]{1,0:T(8,128)(2,1)S(1)} %get-tuple-element.41), channel_id=1, source_target_pairs={{0,6},{1,7},{2,4},{3,5},{4,2},{5,3},{6,0},{7,1},{8,14},{9,15},{10,... | collective-permute-start | bytes 393224 | tf_op jit(solution)/shard_map/ppermute | solution.py:564
  67.4 12.3 %collective-permute-start.4 = (bf16[128,512]{1,0:T(8,128)(2,1)S(1)}, bf16[128,512]{1,0:T(8,128)(2,1)S(1)}, u32[]{:S(2)}, u32[]{:S(2)}) collective-permute-start(bf16[128,512]{1,0:T(8,128)(2,1)S(1)} %get-tuple-element.42), channel_id=1, source_target_pairs={{0,4},{1,5},{2,6},{3,7},{4,0},{5,1},{6,2},{7,3},{8,12},{9,13},{10,... | collective-permute-start | bytes 393224 | tf_op jit(solution)/shard_map/ppermute | solution.py:564
  73.1 6.6 %collective-permute-start.3 = (bf16[128,512]{1,0:T(8,128)(2,1)S(1)}, bf16[128,512]{1,0:T(8,128)(2,1)S(1)}, u32[]{:S(2)}, u32[]{:S(2)}) collective-permute-start(bf16[128,512]{1,0:T(8,128)(2,1)S(1)} %get-tuple-element.43), channel_id=1, source_target_pairs={{0,2},{1,3},{2,0},{3,1},{4,6},{5,7},{6,4},{7,5},{8,10},{9,11},{10,... | collective-permute-start | bytes 393224 | tf_op jit(solution)/shard_map/ppermute | solution.py:564
  79.7 21.5 %collective-permute-start.8 = (bf16[256,2048]{1,0:T(8,128)(2,1)}, bf16[256,2048]{1,0:T(8,128)(2,1)}, u32[]{:S(2)}, u32[]{:S(2)}) collective-permute-start(bf16[256,2048]{1,0:T(8,128)(2,1)} %below_1024.1), channel_id=1, source_target_pairs={{0,1},{1,2},{2,3},{3,4},{4,5},{5,6},{6,7},{7,8},{8,9},{9,10},{10,1... | collective-permute-start | bytes 3145736 | tf_op jit(solution)/shard_map/ppermute | solution.py:491
  82.7 6.7 %collective-permute-start.7 = (bf16[128,512]{1,0:T(8,128)(2,1)S(1)}, bf16[128,512]{1,0:T(8,128)(2,1)S(1)}, u32[]{:S(2)}, u32[]{:S(2)}) collective-permute-start(bf16[128,512]{1,0:T(8,128)(2,1)S(1)} %fusion.3), channel_id=1, source_target_pairs={{0,8},{1,9},{2,10},{3,11},{4,12},{5,13},{6,14},{7,15},{8,0},{9,1},... | collective-permute-start | bytes 393224 | tf_op jit(solution)/shard_map/ppermute | solution.py:571
  102.3 7.3 %collective-permute-start.11 = (bf16[128,512]{1,0:T(8,128)(2,1)S(1)}, bf16[128,512]{1,0:T(8,128)(2,1)S(1)}, u32[]{:S(2)}, u32[]{:S(2)}) collective-permute-start(bf16[128,512]{1,0:T(8,128)(2,1)S(1)} %add_convert_fusion.refs_0_), channel_id=1, source_target_pairs={{0,6},{1,7},{2,4},{3,5},{4,2},{5,3},{6,0},{7,1},{8,14},{9,15},{10,... | collective-permute-start | bytes 393224 | tf_op jit(solution)/shard_map/ppermute | solution.py:577
  102.9 10.2 %collective-permute-start.10 = (bf16[128,512]{1,0:T(8,128)(2,1)S(1)}, bf16[128,512]{1,0:T(8,128)(2,1)S(1)}, u32[]{:S(2)}, u32[]{:S(2)}) collective-permute-start(bf16[128,512]{1,0:T(8,128)(2,1)S(1)} %add_convert_fusion.refs_0_), channel_id=1, source_target_pairs={{0,4},{1,5},{2,6},{3,7},{4,0},{5,1},{6,2},{7,3},{8,12},{9,13},{10,... | collective-permute-start | bytes 393224 | tf_op jit(solution)/shard_map/ppermute | solution.py:577
  107.3 5.8 %collective-permute-start.9 = (bf16[128,512]{1,0:T(8,128)(2,1)S(1)}, bf16[128,512]{1,0:T(8,128)(2,1)S(1)}, u32[]{:S(2)}, u32[]{:S(2)}) collective-permute-start(bf16[128,512]{1,0:T(8,128)(2,1)S(1)} %add_convert_fusion.refs_0_), channel_id=1, source_target_pairs={{0,2},{1,3},{2,0},{3,1},{4,6},{5,7},{6,4},{7,5},{8,10},{9,11},{10,... | collective-permute-start | bytes 393224 | tf_op jit(solution)/shard_map/ppermute | solution.py:577
  108.7 8.5 %collective-permute-start.12 = (bf16[128,512]{1,0:T(8,128)(2,1)S(1)}, bf16[128,512]{1,0:T(8,128)(2,1)S(1)}, u32[]{:S(2)}, u32[]{:S(2)}) collective-permute-start(bf16[128,512]{1,0:T(8,128)(2,1)S(1)} %add_convert_fusion.refs_0_), channel_id=1, source_target_pairs={{0,1},{1,0},{2,3},{3,2},{4,5},{5,4},{6,7},{7,6},{8,9},{9,8},{10,11... | collective-permute-start | bytes 393224 | tf_op jit(solution)/shard_map/ppermute | solution.py:578
  109.6 7.7 %collective-permute-start.15 = (bf16[128,512]{1,0:T(8,128)(2,1)S(1)}, bf16[128,512]{1,0:T(8,128)(2,1)S(1)}, u32[]{:S(2)}, u32[]{:S(2)}) collective-permute-start(bf16[128,512]{1,0:T(8,128)(2,1)S(1)} %collective-permute-done.11.refs_3_), channel_id=1, source_target_pairs={{0,1},{1,0},{2,3},{3,2},{4,5},{5,4},{6,7},{7,6},{8,9},{9,8},{10,11... | collective-permute-start | bytes 393224 | tf_op jit(solution)/shard_map/ppermute | solution.py:578
  113.1 4.2 %collective-permute-start.14 = (bf16[128,512]{1,0:T(8,128)(2,1)S(1)}, bf16[128,512]{1,0:T(8,128)(2,1)S(1)}, u32[]{:S(2)}, u32[]{:S(2)}) collective-permute-start(bf16[128,512]{1,0:T(8,128)(2,1)S(1)} %collective-permute-done.10.refs_2_), channel_id=1, source_target_pairs={{0,1},{1,0},{2,3},{3,2},{4,5},{5,4},{6,7},{7,6},{8,9},{9,8},{10,11... | collective-permute-start | bytes 393224 | tf_op jit(solution)/shard_map/ppermute | solution.py:578
  113.1 4.2 %collective-permute-start.13 = (bf16[128,512]{1,0:T(8,128)(2,1)S(1)}, bf16[128,512]{1,0:T(8,128)(2,1)S(1)}, u32[]{:S(2)}, u32[]{:S(2)}) collective-permute-start(bf16[128,512]{1,0:T(8,128)(2,1)S(1)} %collective-permute-done.9.refs_1_), channel_id=1, source_target_pairs={{0,1},{1,0},{2,3},{3,2},{4,5},{5,4},{6,7},{7,6},{8,9},{9,8},{10,11... | collective-permute-start | bytes 393224 | tf_op jit(solution)/shard_map/ppermute | solution.py:578
